TPU v7x, 32 devices: a whole 2x2x4 slice. The times are simulated.
32 devices in a mesh: dp: 8 (over z, x), tensor: 4 (over y, core).
Axes of the slice: x: 2, y: 2, z: 4, core: 2. Of those that a mesh axis runs over, the one named last changes fastest.
Arguments:
- tokens: bfloat16 [32768, 768], P(('dp', 'tensor')), may hold values from -6 to 6
- cotangent: bfloat16 [32768, 768], P(('dp', 'tensor')), may hold values from -6 to 6
- segment_ids: int32 [32768], P('dp'), may hold values from 0 to 255, never falling along the last dimension, each value on 1 to 1024 neighbouring positions
- buckets: int32 [2047], replicated, may hold values from 0 to 31
- owners: int32 [2304], replicated, may hold values from 0 to 7, as said below
- master: float32 [4, 4608, 768], P('tensor', 'dp'), may hold values from -2 to 2
- first_moment: float32 [4, 4608, 768], P('tensor', 'dp'), may hold values from -262144 to 262144
- second_moment: float32 [4, 4608, 768], P('tensor', 'dp'), may hold values from 0 to 2097152
- small_params: float32 [3616], replicated, may hold values from -5 to 5
- small_first: float32 [3616], replicated, may hold values from -524288 to 524288
- small_second: float32 [3616], replicated, may hold values from 0 to 2097152
- adapter_ema: float32 [1696], replicated, may hold values from -5 to 5
- step_count: int32 [1], replicated, may hold values from 2 to 20
Outputs:
- layer_out: bfloat16 [32768, 768], P(('dp', 'tensor'))
- input_grad: bfloat16 [32768, 768], P(('dp', 'tensor'))
- weight_grads: float32 [4, 4608, 768], P('tensor', 'dp')
- new_first: float32 [4, 4608, 768], P('tensor', 'dp')
- new_second: float32 [4, 4608, 768], P('tensor', 'dp')
- new_master: float32 [4, 4608, 768], P('tensor', 'dp')
- new_copies: bfloat16 [4, 4608, 768], P('tensor', 'dp')
- small_grads: float32 [3616], replicated
- small_first_new: float32 [3616], replicated
- small_second_new: float32 [3616], replicated
- small_new: float32 [3616], replicated
- ema_new: float32 [1696], replicated
Inputs may be any that keep to these rules, and one draw needn't show every extreme that they name: `owners`: no owner holds more than 576 rows, and some owner holds exactly 576.
All inputs are finite; a program needn't handle non-finite values.
Results may differ from a plain program's by a relative error of at most 0.02.
Values may be sent and summed in bfloat16 or wider, within the bound.
A program may use at most 192 MiB of HBM per device.

v0:
```python
from functools import partial
import math

import jax
import jax.numpy as jnp
from jax import lax
from jax.sharding import PartitionSpec as P

D = 768
H = 12
HS = 64
FF = 3072
NB = 32
R = 48
PHM = 4
SEQ = 1024
NADAPT = 1696


highest = lax.Precision.HIGHEST
norm_epsilon = 1e-06
beta_first = 0.5
beta_second = 0.5
adam_epsilon = 1e-08
rate_per_step = 0.01
weight_decay = 0.1
average_keep = 0.75
masked_score = -1000000000.0


def owner_slots(owners, devices, capacity):
    onehot = (owners[:, None] == jnp.arange(devices, dtype=jnp.int32)[None, :]).astype(jnp.int32)
    within = jnp.sum(jnp.cumsum(onehot, axis=0) * onehot, axis=1) - 1
    return owners * capacity + within


def unpack(packed):
    widths = (D, D, PHM**3, D, R, R, D, NB * H)
    pieces = []
    offset = 0
    for width in widths:
        pieces.append(packed[offset : offset + width])
        offset = offset + width
    gain_one, gain_two, mix_flat, down_left, down_right, up_left, up_right, table_flat = pieces
    adapter = (
        mix_flat.reshape(PHM, PHM, PHM),
        down_left.reshape(PHM, D // PHM),
        down_right.reshape(PHM, R // PHM),
        up_left.reshape(PHM, R // PHM),
        up_right.reshape(PHM, D // PHM),
    )
    return (gain_one, gain_two, adapter, table_flat.reshape(NB, H))


def adapter_apply(features, adapter):
    mix, down_left, down_right, up_left, up_right = adapter
    down_matrix = jnp.einsum(
        "iab,ip,iq->apbq", mix, down_left, down_right, precision=highest
    ).reshape(D, R)
    up_matrix = jnp.einsum("iab,iq,ip->aqbp", mix, up_left, up_right, precision=highest).reshape(
        R, D
    )
    hidden = jnp.dot(features, down_matrix, precision=highest)
    return features + jnp.dot(jax.nn.gelu(hidden, approximate=False), up_matrix, precision=highest)


def gelu_slope(values):
    normal_cdf = 0.5 * (1.0 + lax.erf(values * (1.0 / math.sqrt(2.0))))
    normal_pdf = jnp.exp(-0.5 * values * values) * (1.0 / math.sqrt(2.0 * math.pi))
    return normal_cdf + values * normal_pdf


def rms_norm(values, gain):
    return (
        values * lax.rsqrt(jnp.mean(values * values, axis=-1, keepdims=True) + norm_epsilon) * gain
    )


def contract_rows(left, right):
    return lax.dot_general(
        left, right, (((0,), (0,)), ((), ())), preferred_element_type=jnp.float32
    )


def contract_cols(left, right):
    return lax.dot_general(
        left, right, (((1,), (1,)), ((), ())), preferred_element_type=jnp.float32
    )


def toeplitz_rows(per_offset, start, row_count, key_count):
    heads_here = per_offset.shape[0]
    base_index = key_count - 1 - start
    upper_part = per_offset[:, base_index : base_index + key_count]
    lower_part = per_offset[:, base_index - (row_count - 1) : base_index]
    period = key_count + row_count
    pattern = jnp.concatenate(
        [upper_part, jnp.zeros((heads_here, 1), jnp.float32), lower_part], axis=1
    )
    tiled = jnp.tile(pattern, (1, row_count))[:, : row_count * (period - 1)]
    return tiled.reshape(heads_here, row_count, period - 1)[:, :, :key_count]


def toeplitz_back(offset_grad, block_grad, start):
    heads_here, row_count, key_count = block_grad.shape
    period = key_count + row_count
    widened = jnp.pad(block_grad, ((0, 0), (0, 0), (0, row_count - 1))).reshape(
        heads_here, row_count * (period - 1)
    )
    widened = jnp.pad(widened, ((0, 0), (0, row_count))).reshape(heads_here, row_count, period)
    pattern_grad = jnp.sum(widened, axis=1)
    base_index = key_count - 1 - start
    offset_grad = offset_grad.at[:, base_index : base_index + key_count].add(
        pattern_grad[:, :key_count]
    )
    offset_grad = offset_grad.at[:, base_index - (row_count - 1) : base_index].add(
        pattern_grad[:, key_count + 1 :]
    )
    return offset_grad


def block_scores(query_block, key_rows, segment_query, segment_keys, per_offset, start):
    raw_scores = jnp.einsum(
        "ihd,lhd->hil", query_block, key_rows, preferred_element_type=jnp.float32
    )
    bias = toeplitz_rows(per_offset, start, query_block.shape[0], key_rows.shape[0])
    same_doc = segment_query[:, None] == segment_keys[None, :]
    return jnp.where(same_doc[None], raw_scores + bias, masked_score)


def attend_sequence(inputs, per_offset, block_rows):
    queries, key_rows, value_rows, segments = inputs
    outputs = []
    log_parts = []
    for start in range(0, queries.shape[0], block_rows):
        scores = block_scores(
            queries[start : start + block_rows],
            key_rows,
            segments[start : start + block_rows],
            segments,
            per_offset,
            start,
        )
        peak_score = jnp.max(scores, axis=-1, keepdims=True)
        exp_scores = jnp.exp(scores - peak_score)
        row_total = jnp.sum(exp_scores, axis=-1, keepdims=True)
        soft_probs = (exp_scores / row_total).astype(jnp.bfloat16)
        outputs.append(
            jnp.einsum("hil,lhd->ihd", soft_probs, value_rows, preferred_element_type=jnp.float32)
        )
        log_parts.append((peak_score + jnp.log(row_total))[..., 0])
    return (jnp.concatenate(outputs, axis=0), jnp.concatenate(log_parts, axis=1))


def attend_back(inputs, per_offset, block_rows):
    queries, key_rows, value_rows, segments, log_sums, out_grad = inputs
    key_grad = jnp.zeros(key_rows.shape, jnp.float32)
    value_grad = jnp.zeros(value_rows.shape, jnp.float32)
    offset_grad = jnp.zeros(per_offset.shape, jnp.float32)
    query_parts = []
    for start in range(0, queries.shape[0], block_rows):
        query_block = queries[start : start + block_rows]
        grad_block = out_grad[start : start + block_rows]
        scores = block_scores(
            query_block, key_rows, segments[start : start + block_rows], segments, per_offset, start
        )
        soft_probs = jnp.exp(scores - log_sums[:, start : start + block_rows, None])
        value_grad = value_grad + jnp.einsum(
            "hil,ihd->lhd",
            soft_probs.astype(jnp.bfloat16),
            grad_block,
            preferred_element_type=jnp.float32,
        )
        prob_grad = jnp.einsum(
            "ihd,lhd->hil", grad_block, value_rows, preferred_element_type=jnp.float32
        )
        score_grad = (
            soft_probs * (prob_grad - jnp.sum(soft_probs * prob_grad, axis=-1, keepdims=True))
        ).astype(jnp.bfloat16)
        query_parts.append(
            jnp.einsum("hil,lhd->ihd", score_grad, key_rows, preferred_element_type=jnp.float32)
        )
        key_grad = key_grad + jnp.einsum(
            "hil,ihd->lhd", score_grad, query_block, preferred_element_type=jnp.float32
        )
        offset_grad = toeplitz_back(offset_grad, score_grad.astype(jnp.float32), start)
    return (jnp.concatenate(query_parts, axis=0), key_grad, value_grad, offset_grad)


def adamw(weights, grads, first, second, step):
    first_new = beta_first * first + (1.0 - beta_first) * grads
    second_new = beta_second * second + (1.0 - beta_second) * grads * grads
    first_hat = first_new / (1.0 - beta_first**step)
    second_hat = second_new / (1.0 - beta_second**step)
    weights_new = weights - rate_per_step * step * (
        first_hat / (jnp.sqrt(second_hat) + adam_epsilon) + weight_decay * weights
    )
    return (weights_new, first_new, second_new)


def per_device(
    tokens,
    cotangent,
    segment_ids,
    buckets,
    owners,
    master,
    first_moment,
    second_moment,
    small_params,
    small_first,
    small_second,
    adapter_ema,
    step_count,
):
    dp_count = lax.axis_size("dp")
    tensor_count = lax.axis_size("tensor")
    capacity = master.shape[1]
    head_count = H // tensor_count
    head_rows = head_count * HS
    hidden_rows = FF // tensor_count
    slots = owner_slots(owners, dp_count, capacity)
    gathered = lax.all_gather(master[0].astype(jnp.bfloat16), "dp", axis=0, tiled=True)
    bank = jnp.take(gathered, slots, axis=0)
    w_qkv = bank[: 3 * head_rows]
    w_out = bank[3 * head_rows : 4 * head_rows]
    w_in = bank[4 * head_rows : 4 * head_rows + hidden_rows]
    w_down = bank[4 * head_rows + hidden_rows :]
    gain_one, gain_two, adapter, table = unpack(small_params)
    tensor_pos = lax.axis_index("tensor")
    table_heads = lax.dynamic_slice_in_dim(table, tensor_pos * head_count, head_count, 1)
    bucket_onehot = (buckets[:, None] == jnp.arange(NB, dtype=jnp.int32)[None, :]).astype(
        jnp.float32
    )
    per_offset = jnp.dot(bucket_onehot, table_heads, precision=highest).T
    inputs_f = tokens.astype(jnp.float32)
    own_rows = tokens.shape[0]
    normed_one = rms_norm(inputs_f, gain_one).astype(jnp.bfloat16)
    rows_one = lax.all_gather(normed_one, "tensor", axis=0, tiled=True)
    group_rows = rows_one.shape[0]
    seq_count = group_rows // SEQ
    block_rows = min(512, SEQ)
    projected = contract_cols(rows_one, w_qkv).astype(jnp.bfloat16)
    seq_shape = (seq_count, SEQ, head_count, HS)
    queries = projected[:, :head_rows].reshape(seq_shape)
    key_rows = projected[:, head_rows : 2 * head_rows].reshape(seq_shape)
    value_rows = projected[:, 2 * head_rows :].reshape(seq_shape)
    segments = segment_ids.reshape(seq_count, SEQ)
    forward_fn = partial(attend_sequence, per_offset=per_offset, block_rows=block_rows)
    attended, log_sums = lax.map(forward_fn, (queries, key_rows, value_rows, segments))
    attended_b = attended.reshape(group_rows, head_rows).astype(jnp.bfloat16)
    attn = lax.psum_scatter(
        jnp.dot(
            lax.slice_in_dim(attended_b, 0, own_rows * lax.axis_size("tensor"), axis=0),
            w_out,
            preferred_element_type=jnp.float32,
        ).astype(jnp.bfloat16),
        "tensor",
        scatter_dimension=0,
        tiled=True,
    ).astype(jnp.float32)
    mid = inputs_f + attn
    normed_two = rms_norm(mid, gain_two).astype(jnp.bfloat16)
    rows_two = lax.all_gather(normed_two, "tensor", axis=0, tiled=True)
    pre_act = contract_cols(rows_two, w_in)
    activ = jax.nn.gelu(pre_act, approximate=False).astype(jnp.bfloat16)
    ffn_out = lax.psum_scatter(
        jnp.dot(
            lax.slice_in_dim(activ, 0, own_rows * lax.axis_size("tensor"), axis=0),
            w_down,
            preferred_element_type=jnp.float32,
        ).astype(jnp.bfloat16),
        "tensor",
        scatter_dimension=0,
        tiled=True,
    ).astype(jnp.float32)
    final, adapter_pull = jax.vjp(adapter_apply, ffn_out, adapter)
    layer_out = (mid + final).astype(jnp.bfloat16)
    out_grad = cotangent.astype(jnp.float32)
    ffn_grad, adapter_grad = adapter_pull(out_grad)
    ffn_rows_grad = lax.all_gather(ffn_grad.astype(jnp.bfloat16), "tensor", axis=0, tiled=True)
    down_grad = contract_rows(activ, ffn_rows_grad)
    act_grad = contract_cols(ffn_rows_grad, w_down)
    pre_grad = (act_grad * gelu_slope(pre_act)).astype(jnp.bfloat16)
    in_grad = contract_rows(pre_grad, rows_two)
    normed_two_grad = lax.psum_scatter(
        jnp.dot(
            lax.slice_in_dim(pre_grad, 0, own_rows * lax.axis_size("tensor"), axis=0),
            w_in,
            preferred_element_type=jnp.float32,
        ).astype(jnp.bfloat16),
        "tensor",
        scatter_dimension=0,
        tiled=True,
    ).astype(jnp.float32)
    _, norm_two_pull = jax.vjp(rms_norm, mid, gain_two)
    mid_extra, gain_two_grad = norm_two_pull(normed_two_grad)
    mid_grad = out_grad + mid_extra
    attn_rows_grad = lax.all_gather(mid_grad.astype(jnp.bfloat16), "tensor", axis=0, tiled=True)
    out_weight_grad = contract_rows(attended_b, attn_rows_grad)
    attended_grad = contract_cols(attn_rows_grad, w_out).astype(jnp.bfloat16)
    back_fn = partial(attend_back, per_offset=per_offset, block_rows=block_rows)
    query_grad, key_grad, value_grad, offset_parts = lax.map(
        back_fn,
        (queries, key_rows, value_rows, segments, log_sums, attended_grad.reshape(seq_shape)),
    )
    proj_grad = jnp.concatenate(
        [
            query_grad.reshape(group_rows, head_rows),
            key_grad.reshape(group_rows, head_rows),
            value_grad.reshape(group_rows, head_rows),
        ],
        axis=1,
    ).astype(jnp.bfloat16)
    qkv_grad = contract_rows(proj_grad, rows_one)
    normed_one_grad = lax.psum_scatter(
        jnp.dot(
            lax.slice_in_dim(proj_grad, 0, own_rows * lax.axis_size("tensor"), axis=0),
            w_qkv,
            preferred_element_type=jnp.float32,
        ).astype(jnp.bfloat16),
        "tensor",
        scatter_dimension=0,
        tiled=True,
    ).astype(jnp.float32)
    _, norm_one_pull = jax.vjp(rms_norm, inputs_f, gain_one)
    input_extra, gain_one_grad = norm_one_pull(normed_one_grad)
    input_grad = (mid_grad + input_extra).astype(jnp.bfloat16)
    offset_total = jnp.sum(offset_parts, axis=0)
    table_grad = jnp.dot(bucket_onehot.T, offset_total.T, precision=highest)
    table_full = lax.dynamic_update_slice(
        jnp.zeros((NB, H), jnp.float32), table_grad, (0, tensor_pos * head_count)
    )
    small_local = jnp.concatenate(
        [gain_one_grad, gain_two_grad]
        + [piece.reshape(-1) for piece in adapter_grad]
        + [table_full.reshape(-1)]
    )
    small_total = lax.psum(small_local, ("dp", "tensor"))
    bank_grad = jnp.concatenate([qkv_grad, out_weight_grad, in_grad, down_grad], axis=0)
    packed = jnp.zeros((dp_count * capacity, D), jnp.float32).at[slots].set(bank_grad)
    received = lax.all_to_all(
        packed.reshape(dp_count, capacity, D).astype(jnp.bfloat16),
        "dp",
        split_axis=0,
        concat_axis=0,
        tiled=True,
    ).astype(jnp.float32)
    owned_grad = jnp.sum(received, axis=0)
    filled = jnp.zeros((dp_count * capacity,), jnp.float32).at[slots].set(1.0)
    own_filled = lax.dynamic_slice_in_dim(filled, lax.axis_index("dp") * capacity, capacity, 0)[
        :, None
    ]
    step = step_count[0].astype(jnp.float32)
    new_master, new_first, new_second = adamw(
        master[0], owned_grad, first_moment[0], second_moment[0], step
    )
    new_master = new_master * own_filled
    new_first = new_first * own_filled
    new_second = new_second * own_filled
    small_new, small_first_new, small_second_new = adamw(
        small_params, small_total, small_first, small_second, step
    )
    ema_new = average_keep * adapter_ema + (1.0 - average_keep) * small_new[2 * D : 2 * D + NADAPT]
    return (
        layer_out,
        input_grad,
        owned_grad[None],
        new_first[None],
        new_second[None],
        new_master[None],
        new_master.astype(jnp.bfloat16)[None],
        small_total,
        small_first_new,
        small_second_new,
        small_new,
        ema_new,
    )


def solution(mesh):
    return jax.shard_map(
        per_device,
        mesh=mesh,
        in_specs=(
            P(("dp", "tensor"), None),
            P(("dp", "tensor"), None),
            P("dp"),
            P(),
            P(),
            P("tensor", "dp", None),
            P("tensor", "dp", None),
            P("tensor", "dp", None),
            P(),
            P(),
            P(),
            P(),
            P(),
        ),
        out_specs=(
            P(("dp", "tensor"), None),
            P(("dp", "tensor"), None),
            P("tensor", "dp", None),
            P("tensor", "dp", None),
            P("tensor", "dp", None),
            P("tensor", "dp", None),
            P("tensor", "dp", None),
            P(),
            P(),
            P(),
            P(),
            P(),
        ),
        check_vma=False,
    )
```

profile of v0, /device:TPU:0, one launch (start us, length us, event | category | flops | bytes accessed | tf_op | source)
XLA Modules:
  0.0 2342.3 jit_solution(620989935647254342)
XLA Ops:
  19.6 102.7 %all-gather.15.cloned.1.call-done = bf16[1,4608,768]{2,1,0:T(8,128)(2,1)} async-done(((bf16[1,576,768]{2,1,0:T(8,128)(2,1)}), bf16[1,4608,768]{2,1,0:T(8,128)(2,1)}) %all-gather.15.cloned.1.call-update) | async-done | bytes 7077904 | tf_op jit(solution)/shard_map/all_gather | solution.py:223
  122.3 12.9 gather_fusion
  138.3 30.8 %all-gather.7.cloned.1.call-done = bf16[4096,768]{1,0:T(8,128)(2,1)} async-done(((bf16[1024,768]{1,0:T(8,128)(2,1)}), bf16[4096,768]{1,0:T(8,128)(2,1)}) %all-gather.7.cloned.1.call-update) | async-done | bytes 6291472 | tf_op jit(solution)/shard_map/all_gather | solution.py:239
  195.2 550.5 %while.36 = (s32[]{:T(128)}, bf16[4,1024,3,64]{1,3,2,0:T(8,128)(2,1)}, f32[4,3,1024]{2,1,0:T(4,128)}, bf16[4,1024,3,64]{1,3,2,0:T(8,128)(2,1)}, s32[4,1024]{1,0:...) while((s32[]{:T(128)}, ...), condition=%wide.region_9.10_spmd, body=%wide.region_4.9_spmd.sunk | while | flops 832307200 | bytes 225708672 | solution.py:250
  219.0 19.9 copy.128
  244.8 13.2 reshape.701
  258.0 15.6 reshape.702
  283.3 19.9 copy.127
  309.1 13.2 reshape.699
  322.3 15.6 reshape.700
  350.2 19.9 copy.128
  375.9 13.2 reshape.701
  389.1 15.6 reshape.702
  414.6 19.9 copy.127
  440.4 13.2 reshape.699
  453.6 15.6 reshape.700
  481.4 19.9 copy.128
  507.2 13.2 reshape.701
  520.3 15.6 reshape.702
  545.8 19.9 copy.127
  571.5 13.2 reshape.699
  584.7 15.6 reshape.700
  612.6 19.9 copy.128
  638.3 13.2 reshape.701
  651.5 15.6 reshape.702
  676.9 19.9 copy.127
  702.7 13.2 reshape.699
  715.9 15.6 reshape.700
  756.3 58.5 %reduce-scatter.5.cloned.1.call-done = bf16[1024,768]{1,0:T(8,128)(2,1)} async-done(((bf16[4096,768]{1,0:T(8,128)(2,1)}), bf16[1024,768]{1,0:T(8,128)(2,1)}) %reduce-scatter.5.cloned.1.call-update) | async-done | bytes 1572880 | tf_op jit(solution)/shard_map/reduce_scatter | solution.py:252
  818.7 46.5 %all-gather.9.cloned.1.call-done = bf16[4096,768]{1,0:T(8,128)(2,1)} async-done(((bf16[1024,768]{1,0:T(8,128)(2,1)}), bf16[4096,768]{1,0:T(8,128)(2,1)}) %all-gather.9.cloned.1.call-update) | async-done | bytes 6291472 | tf_op jit(solution)/shard_map/all_gather | solution.py:264
  865.2 33.3 %fusion.72 = (bf16[4096,768]{1,0:T(8,128)(2,1)S(1)}, f32[4096,768]{1,0:T(8,128)}) fusion(bf16[4096,768]{1,0:T(8,128)(2,1)} %all-gather.9.cloned.1.call-done, bf16[2304,768]{1,0:T(8,128)(2,1)} %broadcast_select_fusion), kind=kOutput, calls=%fused_computation.121 | convolution fusion | flops 5036310528 | bytes 26345472 | tf_op jit(solution)/shard_map/dot_general | solution.py:86
  914.9 53.0 %reduce-scatter.7.cloned.1.call-done = bf16[1024,768]{1,0:T(8,128)(2,1)} async-done(((bf16[4096,768]{1,0:T(8,128)(2,1)}), bf16[1024,768]{1,0:T(8,128)(2,1)}) %reduce-scatter.7.cloned.1.call-update) | async-done | bytes 1572880 | tf_op jit(solution)/shard_map/reduce_scatter | solution.py:267
  979.4 46.5 %all-gather.11.cloned.1.call-done = bf16[4096,768]{1,0:T(8,128)(2,1)} async-done(((bf16[1024,768]{1,0:T(8,128)(2,1)}), bf16[4096,768]{1,0:T(8,128)(2,1)}) %all-gather.11.cloned.1.call-update) | async-done | bytes 6291472 | tf_op jit(solution)/shard_map/all_gather | solution.py:281
  1025.9 11.5 fusion.78
  1048.6 58.3 %reduce-scatter.9.cloned.1.call-done = bf16[1024,768]{1,0:T(8,128)(2,1)} async-done(((bf16[4096,768]{1,0:T(8,128)(2,1)}), bf16[1024,768]{1,0:T(8,128)(2,1)}) %reduce-scatter.9.cloned.1.call-update) | async-done | bytes 1572880 | tf_op jit(solution)/shard_map/reduce_scatter | solution.py:286
  1134.5 24.9 %all-gather.13.cloned.1.call-done = bf16[4096,768]{1,0:T(8,128)(2,1)} async-done(((bf16[1024,768]{1,0:T(8,128)(2,1)}), bf16[4096,768]{1,0:T(8,128)(2,1)}) %all-gather.13.cloned.1.call-update) | async-done | bytes 6291472 | tf_op jit(solution)/shard_map/all_gather | solution.py:299
  1170.2 898.8 %while.37 = (s32[]{:T(128)}, bf16[4,1024,3,64]{1,3,2,0:T(8,128)(2,1)}, bf16[4,1024,3,64]{1,3,2,0:T(8,128)(2,1)}, bf16[4,1024,3,64]{1,3,2,0:T(8,128)(2,1)}, f32[4...) while((s32[]{:T(128)}, ...), condition=%wide.region_24.25_spmd, body=%wide.region_18.24_spmd.sunk | while | flops 2053244416 | bytes 491329472 | solution.py:303
  1183.4 19.9 copy.132
  1209.1 13.2 reshape.707
  1222.3 16.2 reshape.708
  1285.0 19.9 copy.131
  1310.7 13.2 reshape.705
  1323.9 16.2 reshape.706
  1405.9 19.9 copy.132
  1431.7 13.2 reshape.707
  1444.9 16.3 reshape.708
  1507.7 19.9 copy.131
  1533.5 13.2 reshape.705
  1546.6 16.2 reshape.706
  1628.7 19.9 copy.132
  1654.4 13.2 reshape.707
  1667.6 16.3 reshape.708
  1730.3 19.9 copy.131
  1756.1 13.2 reshape.705
  1769.3 16.2 reshape.706
  1851.3 19.9 copy.132
  1877.1 13.2 reshape.707
  1890.2 16.3 reshape.708
  1952.9 19.9 copy.131
  1978.7 13.2 reshape.705
  1991.8 16.2 reshape.706
  2086.8 22.5 scatter_custom_fusion
  2174.8 104.0 %all-to-all-done = bf16[8,576,768]{2,1,0:T(8,128)(2,1)} async-done(((bf16[8,576,768]{2,1,0:T(8,128)(2,1)}), bf16[8,576,768]{2,1,0:T(8,128)(2,1)}, u32[]{:S(2)}, u32[]{:S(2)}) %all-to-all-start) | async-done | bytes 7077920 | tf_op jit(solution)/shard_map/all_to_all | solution.py:342
  2291.8 37.7 %psum.7 = f32[3616]{0:T(1024)S(1)} all-reduce(f32[3616]{0:T(1024)S(1)} %concatenate.64), channel_id=1, replica_groups=mesh['dp'=8,'tensor'=4] {'dp','tensor'}, use_global_device_ids=true, to_apply=%region_33.34 | all-reduce | flops 3616 | bytes 28928 | tf_op jit(solution)/shard_map/psum | solution.py:339
  (678 shorter events, 857.9 us)
Async XLA Ops:
  7.2 115.1 %all-gather.15.cloned.1.call-start = ((), (), s32[]{:S(2)}) async-start(), calls=%async_computation.13 | async-start | bytes 7962624 | tf_op jit(solution)/shard_map/all_gather | solution.py:223
  9.9 8.3 copy-start.78
  9.9 159.2 %all-gather.7.cloned.1.call-start = ((), (), s32[]{:S(2)}) async-start(), calls=%async_computation.5 | async-start | bytes 7864320 | tf_op jit(solution)/shard_map/all_gather | solution.py:239
  13.8 801.0 %reduce-scatter.5.cloned.1.call-start = ((), (), s32[]{:S(2)}) async-start(), calls=%async_computation.6 | async-start | bytes 7864320 | tf_op jit(solution)/shard_map/reduce_scatter | solution.py:252
  17.6 104.8 %copy-start.51 = (s32[2304]{0:T(1024)}, s32[2304]{0:T(1024)S(1)}, u32[]{:S(2)}) copy-start(s32[2304]{0:T(1024)S(1)} %get-tuple-element.500) | copy-start | bytes 27652
  187.0 8.2 copy-start.15
  745.7 10.5 copy-start.1
  745.7 10.5 copy-start.30
  756.2 58.5 %copy-start.3 = (bf16[1024,768]{1,0:T(8,128)(2,1)S(1)}, bf16[1024,768]{1,0:T(8,128)(2,1)}, u32[]{:S(2)}) copy-start(bf16[1024,768]{1,0:T(8,128)(2,1)} %param.25) | copy-start | bytes 4718596
  756.2 60.7 %copy-start.42 = (f32[768]{0:T(1024)S(1)}, f32[768]{0:T(1024)}, u32[]{:S(2)}) copy-start(f32[768]{0:T(1024)} %get-tuple-element.535) | copy-start | bytes 9220
  756.3 108.9 %all-gather.9.cloned.1.call-start = ((), (), s32[]{:S(2)}) async-start(), calls=%async_computation.7 | async-start | bytes 7864320 | tf_op jit(solution)/shard_map/all_gather | solution.py:264
  816.9 293.7 %copy-start.40 = (f32[1024]{0:T(1024)}, f32[1024]{0:T(1024)S(1)}, u32[]{:S(2)}) copy-start(f32[1024]{0:T(1024)S(1)} %fusion.172) | copy-start | bytes 12292
  818.7 149.3 %reduce-scatter.7.cloned.1.call-start = ((), (), s32[]{:S(2)}) async-start(), calls=%async_computation.8 | async-start | bytes 7864320 | tf_op jit(solution)/shard_map/reduce_scatter | solution.py:267
  909.4 116.5 %all-gather.11.cloned.1.call-start = ((), (), s32[]{:S(2)}) async-start(), calls=%async_computation.9 | async-start | bytes 7864320 | tf_op jit(solution)/shard_map/all_gather | solution.py:281
  967.9 7.5 copy-start.10
  979.3 127.6 %reduce-scatter.9.cloned.1.call-start = ((), (), s32[]{:S(2)}) async-start(), calls=%async_computation.10 | async-start | bytes 7864320 | tf_op jit(solution)/shard_map/reduce_scatter | solution.py:286
  1048.4 111.1 %all-gather.13.cloned.1.call-start = ((), (), s32[]{:S(2)}) async-start(), calls=%async_computation.11 | async-start | bytes 7864320 | tf_op jit(solution)/shard_map/all_gather | solution.py:299
  1112.9 12.3 slice-start.8
  1115.0 10.2 slice-start.9
  1170.4 7.2 copy-start.8
  1222.3 23.8 %slice-start.2 = ((s8[6291456]{0:T(1024)(128)(4,1)}), s8[2097152]{0:T(1024)(128)(4,1)S(1)}, s32[]{:S(2)}) async-start(s8[6291456]{0:T(1024)(128)(4,1)} %bitcast.377), calls=%async_computation.16 | async-start | bytes 4194304 | tf_op jit(solution)/shard_map/while
  1238.5 7.6 slice-start.3
  1323.9 23.7 %slice-start = ((s8[6291456]{0:T(1024)(128)(4,1)}), s8[2097152]{0:T(1024)(128)(4,1)S(1)}, s32[]{:S(2)}) async-start(s8[6291456]{0:T(1024)(128)(4,1)} %bitcast.375), calls=%async_computation.14 | async-start | bytes 4194304 | tf_op jit(solution)/shard_map/while
  1340.1 7.5 slice-start.1
  1392.9 7.2 copy-start.8
  1444.9 23.9 %slice-start.2 = ((s8[6291456]{0:T(1024)(128)(4,1)}), s8[2097152]{0:T(1024)(128)(4,1)S(1)}, s32[]{:S(2)}) async-start(s8[6291456]{0:T(1024)(128)(4,1)} %bitcast.377), calls=%async_computation.16 | async-start | bytes 4194304 | tf_op jit(solution)/shard_map/while
  1461.1 7.7 slice-start.3
  1546.6 23.7 %slice-start = ((s8[6291456]{0:T(1024)(128)(4,1)}), s8[2097152]{0:T(1024)(128)(4,1)S(1)}, s32[]{:S(2)}) async-start(s8[6291456]{0:T(1024)(128)(4,1)} %bitcast.375), calls=%async_computation.14 | async-start | bytes 4194304 | tf_op jit(solution)/shard_map/while
  1562.9 7.5 slice-start.1
  1615.7 7.2 copy-start.8
  1667.6 23.8 %slice-start.2 = ((s8[6291456]{0:T(1024)(128)(4,1)}), s8[2097152]{0:T(1024)(128)(4,1)S(1)}, s32[]{:S(2)}) async-start(s8[6291456]{0:T(1024)(128)(4,1)} %bitcast.377), calls=%async_computation.16 | async-start | bytes 4194304 | tf_op jit(solution)/shard_map/while
  1683.9 7.6 slice-start.3
  1769.3 23.7 %slice-start = ((s8[6291456]{0:T(1024)(128)(4,1)}), s8[2097152]{0:T(1024)(128)(4,1)S(1)}, s32[]{:S(2)}) async-start(s8[6291456]{0:T(1024)(128)(4,1)} %bitcast.375), calls=%async_computation.14 | async-start | bytes 4194304 | tf_op jit(solution)/shard_map/while
  1785.5 7.5 slice-start.1
  1838.3 7.2 copy-start.8
  1890.2 23.8 %slice-start.2 = ((s8[6291456]{0:T(1024)(128)(4,1)}), s8[2097152]{0:T(1024)(128)(4,1)S(1)}, s32[]{:S(2)}) async-start(s8[6291456]{0:T(1024)(128)(4,1)} %bitcast.377), calls=%async_computation.16 | async-start | bytes 4194304 | tf_op jit(solution)/shard_map/while
  1906.5 7.5 slice-start.3
  1991.8 23.7 %slice-start = ((s8[6291456]{0:T(1024)(128)(4,1)}), s8[2097152]{0:T(1024)(128)(4,1)S(1)}, s32[]{:S(2)}) async-start(s8[6291456]{0:T(1024)(128)(4,1)} %bitcast.375), calls=%async_computation.14 | async-start | bytes 4194304 | tf_op jit(solution)/shard_map/while
  2008.0 7.5 slice-start.1
  2117.9 161.0 %all-to-all-start = ((bf16[8,576,768]{2,1,0:T(8,128)(2,1)}), bf16[8,576,768]{2,1,0:T(8,128)(2,1)}, u32[]{:S(2)}, u32[]{:S(2)}) async-start(bf16[8,576,768]{2,1,0:T(8,128)(2,1)} %bitcast.386), calls=%async_computation.4 | async-start | bytes 14155776 | tf_op jit(solution)/shard_map/all_to_all | solution.py:342
  2123.4 165.4 %reduce-scatter.11.cloned.1.call-start = ((), (), s32[]{:S(2)}) async-start(), calls=%async_computation.12 | async-start | bytes 7864320 | tf_op jit(solution)/shard_map/reduce_scatter | solution.py:316
  2132.4 13.4 copy-start.36
  2133.0 17.5 copy-start.34
  2133.0 20.5 copy-start.57
  2133.0 23.2 copy-start.29
  2145.8 16.1 copy-start.55
  2145.8 21.1 copy-start.4
  2145.8 21.1 copy-start.6
  2167.0 6.2 copy-start.37
  2167.0 6.2 copy-start.79
  2174.8 109.6 %copy-start.63 = (f32[576]{0:T(1024)S(1)}, f32[576]{0:T(1024)}, u32[]{:S(2)}) copy-start(f32[576]{0:T(1024)} %dynamic_slice.74) | copy-start | bytes 6916
  2278.9 5.6 copy-start.26
  2278.9 5.6 copy-start.27
  2284.5 7.2 copy-start.64
  2284.5 7.2 copy-start.67
  2284.5 45.0 %copy-start.59 = (f32[1024]{0:T(1024)S(1)}, f32[1024]{0:T(1024)}, u32[]{:S(2)}) copy-start(f32[1024]{0:T(1024)} %copy-done.58) | copy-start | bytes 12292
  2284.5 45.0 %copy-start.45 = (f32[3616]{0:T(1024)S(1)}, f32[3616]{0:T(1024)}, u32[]{:S(2)}) copy-start(f32[3616]{0:T(1024)} %param.33) | copy-start | bytes 43396
  2284.5 45.0 %copy-start.65 = (f32[3616]{0:T(1024)S(1)}, f32[3616]{0:T(1024)}, u32[]{:S(2)}) copy-start(f32[3616]{0:T(1024)} %param.35) | copy-start | bytes 43396
  2284.5 45.0 %copy-start.66 = (f32[3616]{0:T(1024)S(1)}, f32[3616]{0:T(1024)}, u32[]{:S(2)}) copy-start(f32[3616]{0:T(1024)} %param.34) | copy-start | bytes 43396
  2284.5 45.6 %copy-start.71 = (f32[1696]{0:T(1024)S(1)}, f32[1696]{0:T(1024)}, u32[]{:S(2)}) copy-start(f32[1696]{0:T(1024)} %param.36) | copy-start | bytes 20356
  2284.6 46.2 %copy-start.41 = (f32[1024]{0:T(1024)S(1)}, f32[1024]{0:T(1024)}, u32[]{:S(2)}) copy-start(f32[1024]{0:T(1024)} %copy-done.40) | copy-start | bytes 12292
  2284.6 46.2 %copy-start.43 = (f32[768]{0:T(1024)S(1)}, f32[768]{0:T(1024)}, u32[]{:S(2)}) copy-start(f32[768]{0:T(1024)} %get-tuple-element.535) | copy-start | bytes 9220
  2284.6 46.2 %copy-start.53 = (f32[1024]{0:T(1024)S(1)}, f32[1024]{0:T(1024)}, u32[]{:S(2)}) copy-start(f32[1024]{0:T(1024)} %copy-done.52) | copy-start | bytes 12292
  2329.5 6.0 copy-start.50
  (74 other events, 192.9 us)
Sparse Core Ops, SparseCore 0:
  10.8 111.4 all-gather.14
  124.5 44.5 all-gather.6
  756.4 58.3 reduce-scatter.4
  818.8 46.3 all-gather.8
  909.5 58.3 reduce-scatter.6
  979.5 46.3 all-gather.10
  1048.5 58.3 reduce-scatter.8
  1113.1 46.3 all-gather.12
  2132.6 58.8 reduce-scatter.10
where the time goes:
time: 2360 us; the launch traced here: 2340 us
  local copies, waits for them, and re-layouts  1170 us (50%)
  waiting for transfers between devices  525 us (22%)
  matrix products  359 us (15%)
  other arithmetic  188 us (8%)
  loops' own time  42.1 us (2%)
  blocking collectives  37.7 us (2%)
    while x152, local copies, waits for them, and re-layouts  640 us
    reshape x16, local copies, waits for them, and re-layouts, toeplitz_rows(): return tiled.reshape(heads_here, row_count, period - 1)[:, :, :key_count]  255 us
    all_to_all x1, waiting for transfers between devices, per_device(): lax.all_to_all(packed.reshape(dp_count, capacity, D).astype(jnp.bfloat16)...  104 us
    all_gather x1, waiting for transfers between devices, per_device(): lax.all_gather(master[0].astype(jnp.bfloat16), 'dp', axis=0, tiled=True)  103 us
    dot_general x16, matrix products, block_scores(): jnp.einsum('ihd,lhd->hil', query_block, key_rows, preferred_element_type=...  95.3 us
    slice x16, local copies, waits for them, and re-layouts, toeplitz_rows(): tiled = jnp.tile(pattern, (1, row_count))[:, :row_count * (period - 1)]  94.2 us
    reshape x8, local copies, waits for them, and re-layouts, toeplitz_back(): jnp.pad(block_grad, ((0, 0), (0, 0), (0, row_count - 1)))  60.4 us
    reduce_scatter x1, waiting for transfers between devices, per_device(): lax.psum_scatter(jnp.dot(lax.slice_in_dim(attended_b, 0, own_rows * lax.a...  58.5 us
  transfers between devices with their start and end apart: 10, of which 9 were waited for; matrix products, arithmetic and copies ran while one was open for 5% of the time, Pallas kernels for 0%

commit v1 on v0

v1 whole, which is shorter than its diff:
```python
import functools
import math

import jax
import jax.numpy as jnp
from jax import lax
from jax.experimental import pallas as pl
from jax.experimental.pallas import tpu as pltpu
from jax.sharding import PartitionSpec as P

D = 768
H = 12
HS = 64
FF = 3072
NB = 32
R = 48
PHM = 4
SEQ = 1024
NADAPT = 1696

highest = lax.Precision.HIGHEST
norm_epsilon = 1e-06
beta_first = 0.5
beta_second = 0.5
adam_epsilon = 1e-08
rate_per_step = 0.01
weight_decay = 0.1
average_keep = 0.75
masked_score = -1000000000.0

TILE = 128
WINDOW = 2 * SEQ - TILE
QUERY_TILE = 256
KEY_TILE = 256
VMEM_LIMIT = 48 * 1024 * 1024


def owner_slots(owners, devices, capacity):
    onehot = (owners[:, None] == jnp.arange(devices, dtype=jnp.int32)[None, :]).astype(jnp.int32)
    within = jnp.sum(jnp.cumsum(onehot, axis=0) * onehot, axis=1) - 1
    return owners * capacity + within


def unpack(packed):
    widths = (D, D, PHM**3, D, R, R, D, NB * H)
    pieces = []
    offset = 0
    for width in widths:
        pieces.append(packed[offset : offset + width])
        offset = offset + width
    gain_one, gain_two, mix_flat, down_left, down_right, up_left, up_right, table_flat = pieces
    adapter = (
        mix_flat.reshape(PHM, PHM, PHM),
        down_left.reshape(PHM, D // PHM),
        down_right.reshape(PHM, R // PHM),
        up_left.reshape(PHM, R // PHM),
        up_right.reshape(PHM, D // PHM),
    )
    return (gain_one, gain_two, adapter, table_flat.reshape(NB, H))


def adapter_apply(features, adapter):
    mix, down_left, down_right, up_left, up_right = adapter
    down_matrix = jnp.einsum(
        "iab,ip,iq->apbq", mix, down_left, down_right, precision=highest
    ).reshape(D, R)
    up_matrix = jnp.einsum("iab,iq,ip->aqbp", mix, up_left, up_right, precision=highest).reshape(
        R, D
    )
    hidden = jnp.dot(features, down_matrix, precision=highest)
    return features + jnp.dot(jax.nn.gelu(hidden, approximate=False), up_matrix, precision=highest)


def rms_norm(values, gain):
    return (
        values * lax.rsqrt(jnp.mean(values * values, axis=-1, keepdims=True) + norm_epsilon) * gain
    )


def contract(left, right, left_dim, right_dim):
    return lax.dot_general(
        left,
        right,
        (((left_dim,), (right_dim,)), ((), ())),
        preferred_element_type=jnp.float32,
    )


def attend_kernel(
    query_ref,
    key_ref,
    value_ref,
    bias_ref,
    segment_keys_ref,
    segment_queries_ref,
    exp_ref,
    out_ref,
    scale_ref,
    window,
    scores,
):
    for tile in range(WINDOW // TILE):
        base = WINDOW - TILE * tile
        row = jnp.broadcast_to(bias_ref[0, :, base - TILE : base + TILE], (TILE, 2 * TILE))
        rolled = pltpu.roll(row, TILE, 1, stride=1, stride_axis=0)
        window[TILE * tile : TILE * (tile + 1), :] = rolled[:, :TILE]
    keys = key_ref[...].T
    values = jnp.concatenate([value_ref[...], jnp.ones((16, SEQ), jnp.bfloat16)], axis=0)
    for q0 in range(0, SEQ, QUERY_TILE):
        queries = query_ref[:, q0 : q0 + QUERY_TILE]
        peak = jnp.full((8, QUERY_TILE), -jnp.inf, jnp.float32)
        for k0 in range(0, SEQ, KEY_TILE):
            raw = jnp.dot(keys[k0 : k0 + KEY_TILE], queries, preferred_element_type=jnp.float32)
            parts = []
            for l0 in range(0, QUERY_TILE, TILE):
                start = SEQ - TILE - (q0 + l0) + k0
                same_doc = (
                    segment_keys_ref[k0 : k0 + KEY_TILE, :]
                    == segment_queries_ref[:, q0 + l0 : q0 + l0 + TILE]
                )
                part = jnp.where(
                    same_doc,
                    raw[:, l0 : l0 + TILE] + window[start : start + KEY_TILE, :],
                    masked_score,
                )
                scores[k0 : k0 + KEY_TILE, l0 : l0 + TILE] = part
                parts.append(part)
            whole = jnp.concatenate(parts, axis=1)
            peak = jnp.maximum(peak, jnp.max(whole.reshape(KEY_TILE // 8, 8, QUERY_TILE), axis=0))
        peak = jnp.max(peak, axis=0, keepdims=True)
        total = jnp.zeros((HS + 16, QUERY_TILE), jnp.float32)
        for k0 in range(0, SEQ, KEY_TILE):
            exp_scores = jnp.exp(scores[k0 : k0 + KEY_TILE, :] - peak).astype(jnp.bfloat16)
            exp_ref[0, k0 : k0 + KEY_TILE, q0 : q0 + QUERY_TILE] = exp_scores
            total = total + jnp.dot(
                values[:, k0 : k0 + KEY_TILE], exp_scores, preferred_element_type=jnp.float32
            )
        scale = 1.0 / total[HS : HS + 1]
        scale_ref[0, :, q0 : q0 + QUERY_TILE] = scale
        out_ref[:, q0 : q0 + QUERY_TILE] = (total[:HS] * scale).astype(jnp.bfloat16)


def attend_back_kernel(
    query_ref,
    key_ref,
    value_ref,
    exp_ref,
    out_ref,
    scale_ref,
    out_grad_ref,
    query_grad_ref,
    key_grad_ref,
    value_grad_ref,
    offset_grad_ref,
    window,
    score_grads,
):
    scaled = out_grad_ref[...].astype(jnp.float32) * scale_ref[0]
    delta = jnp.sum(scaled * out_ref[...].astype(jnp.float32), axis=0, keepdims=True)
    scaled_low = scaled.astype(jnp.bfloat16)
    delta_high = delta.astype(jnp.bfloat16).astype(jnp.float32)
    delta_rest = delta - delta_high
    place = lax.broadcasted_iota(jnp.int32, (16, SEQ), 0)
    extra = jnp.where(
        place == 0,
        jnp.broadcast_to(-delta_high, (16, SEQ)),
        jnp.where(place == 1, jnp.broadcast_to(-delta_rest, (16, SEQ)), 0.0),
    ).astype(jnp.bfloat16)
    grads = jnp.concatenate([scaled_low, extra], axis=0)
    values = jnp.concatenate([value_ref[...], jnp.ones((16, SEQ), jnp.bfloat16)], axis=0).T
    window[...] = jnp.zeros_like(window)
    keys = key_ref[...]
    for q0 in range(0, SEQ, QUERY_TILE):
        total = jnp.zeros((HS, QUERY_TILE), jnp.float32)
        for k0 in range(0, SEQ, KEY_TILE):
            centered = jnp.dot(
                values[k0 : k0 + KEY_TILE],
                grads[:, q0 : q0 + QUERY_TILE],
                preferred_element_type=jnp.float32,
            )
            score_grad = centered * exp_ref[
                0, k0 : k0 + KEY_TILE, q0 : q0 + QUERY_TILE
            ].astype(jnp.float32)
            for l0 in range(0, QUERY_TILE, TILE):
                start = SEQ - TILE - (q0 + l0) + k0
                window[start : start + KEY_TILE, :] += score_grad[:, l0 : l0 + TILE]
            score_low = score_grad.astype(jnp.bfloat16)
            score_grads[k0 : k0 + KEY_TILE, q0 : q0 + QUERY_TILE] = score_low
            total = total + jnp.dot(
                keys[:, k0 : k0 + KEY_TILE], score_low, preferred_element_type=jnp.float32
            )
        query_grad_ref[:, q0 : q0 + QUERY_TILE] = total.astype(jnp.bfloat16)
    queries = query_ref[...].T
    scaled_rows = scaled_low.T
    for k0 in range(0, SEQ, KEY_TILE):
        key_grad = jnp.dot(
            score_grads[k0 : k0 + KEY_TILE, :], queries, preferred_element_type=jnp.float32
        )
        value_grad = jnp.dot(
            exp_ref[0, k0 : k0 + KEY_TILE, :], scaled_rows, preferred_element_type=jnp.float32
        )
        key_grad_ref[:, k0 : k0 + KEY_TILE] = key_grad.T.astype(jnp.bfloat16)
        value_grad_ref[:, k0 : k0 + KEY_TILE] = value_grad.T.astype(jnp.bfloat16)
    offset_grad_ref[...] = jnp.zeros_like(offset_grad_ref)
    for tile in range(WINDOW // TILE):
        base = WINDOW - TILE * tile
        block = window[TILE * tile : TILE * (tile + 1), :]
        folded = jnp.concatenate([jnp.zeros((TILE, TILE), jnp.float32), block], axis=1)
        rows = TILE // 2
        while rows >= 1:
            folded = folded[:rows] + pltpu.roll(folded[rows:], 2 * TILE - rows, 1)
            rows //= 2
        offset_grad_ref[0, :, base - TILE : base + TILE] += folded


def head_specs(group_heads):
    def rows(part):
        return pl.BlockSpec(
            (HS, SEQ),
            lambda h: ((h // group_heads) * 3 * group_heads + part * group_heads + h % group_heads, 0),
        )

    return [rows(0), rows(1), rows(2)]


def head_block():
    return pl.BlockSpec((HS, SEQ), lambda h: (h, 0))


def attend(projected, bias_rows, segment_keys, segment_queries, group_heads):
    return pl.pallas_call(
        attend_kernel,
        grid=(H,),
        in_specs=head_specs(group_heads)
        + [
            pl.BlockSpec((1, 1, 2 * SEQ), lambda h: (h, 0, 0)),
            pl.BlockSpec((SEQ, TILE), lambda h: (0, 0)),
            pl.BlockSpec((1, SEQ), lambda h: (0, 0)),
        ],
        out_specs=[
            pl.BlockSpec((1, SEQ, SEQ), lambda h: (h, 0, 0)),
            head_block(),
            pl.BlockSpec((1, 1, SEQ), lambda h: (h, 0, 0)),
        ],
        out_shape=[
            jax.ShapeDtypeStruct((H, SEQ, SEQ), jnp.bfloat16),
            jax.ShapeDtypeStruct((D, SEQ), jnp.bfloat16),
            jax.ShapeDtypeStruct((H, 1, SEQ), jnp.float32),
        ],
        scratch_shapes=[
            pltpu.VMEM((WINDOW, TILE), jnp.float32),
            pltpu.VMEM((SEQ, QUERY_TILE), jnp.float32),
        ],
        compiler_params=pltpu.CompilerParams(vmem_limit_bytes=VMEM_LIMIT),
        cost_estimate=pl.CostEstimate(
            flops=4 * H * SEQ * SEQ * 256, bytes_accessed=32 * 1024 * 1024, transcendentals=H * SEQ * SEQ
        ),
        name="attend",
    )(projected, projected, projected, bias_rows, segment_keys, segment_queries)


def attend_back(projected, exp_scores, attended, scale, attended_grad, group_heads):
    return pl.pallas_call(
        attend_back_kernel,
        grid=(H,),
        in_specs=head_specs(group_heads)
        + [
            pl.BlockSpec((1, SEQ, SEQ), lambda h: (h, 0, 0)),
            head_block(),
            pl.BlockSpec((1, 1, SEQ), lambda h: (h, 0, 0)),
            head_block(),
        ],
        out_specs=[
            head_block(),
            head_block(),
            head_block(),
            pl.BlockSpec((1, 1, 2 * SEQ), lambda h: (h, 0, 0)),
        ],
        out_shape=[jax.ShapeDtypeStruct((D, SEQ), jnp.bfloat16)] * 3
        + [jax.ShapeDtypeStruct((H, 1, 2 * SEQ), jnp.float32)],
        scratch_shapes=[
            pltpu.VMEM((WINDOW, TILE), jnp.float32),
            pltpu.VMEM((SEQ, SEQ), jnp.bfloat16),
        ],
        compiler_params=pltpu.CompilerParams(vmem_limit_bytes=VMEM_LIMIT),
        cost_estimate=pl.CostEstimate(
            flops=8 * H * SEQ * SEQ * 256, bytes_accessed=32 * 1024 * 1024, transcendentals=0
        ),
        name="attend_back",
    )(projected, projected, projected, exp_scores, attended, scale, attended_grad)


def feed_kernel(rows_ref, w_in_ref, w_down_ref, activ_ref, slope_ref, out_ref):
    step = pl.program_id(0)
    row_tile = 256

    @pl.when(step == 0)
    def _():
        out_ref[...] = jnp.zeros_like(out_ref)

    for r0 in range(0, SEQ, row_tile):
        pre = contract(rows_ref[r0 : r0 + row_tile, :], w_in_ref[...], 1, 1)
        cdf = 0.5 * (1.0 + lax.erf(pre * (1.0 / math.sqrt(2.0))))
        pdf = jnp.exp(-0.5 * pre * pre) * (1.0 / math.sqrt(2.0 * math.pi))
        activ = (pre * cdf).astype(jnp.bfloat16)
        activ_ref[r0 : r0 + row_tile, :] = activ
        slope_ref[r0 : r0 + row_tile, :] = (cdf + pre * pdf).astype(jnp.bfloat16)
        out_ref[r0 : r0 + row_tile, :] += jnp.dot(
            activ, w_down_ref[...], preferred_element_type=jnp.float32
        )


def feed(rows, w_in, w_down):
    width = 384
    tokens = rows.shape[0]
    return pl.pallas_call(
        feed_kernel,
        grid=(FF // width,),
        in_specs=[
            pl.BlockSpec((tokens, D), lambda j: (0, 0)),
            pl.BlockSpec((width, D), lambda j: (j, 0)),
            pl.BlockSpec((width, D), lambda j: (j, 0)),
        ],
        out_specs=[
            pl.BlockSpec((tokens, width), lambda j: (0, j)),
            pl.BlockSpec((tokens, width), lambda j: (0, j)),
            pl.BlockSpec((tokens, D), lambda j: (0, 0)),
        ],
        out_shape=[
            jax.ShapeDtypeStruct((tokens, FF), jnp.bfloat16),
            jax.ShapeDtypeStruct((tokens, FF), jnp.bfloat16),
            jax.ShapeDtypeStruct((tokens, D), jnp.float32),
        ],
        compiler_params=pltpu.CompilerParams(vmem_limit_bytes=VMEM_LIMIT),
        cost_estimate=pl.CostEstimate(
            flops=4 * tokens * FF * D,
            bytes_accessed=24 * 1024 * 1024,
            transcendentals=2 * tokens * FF,
        ),
        name="feed",
    )(rows, w_in, w_down)


def adamw(weights, grads, first, second, step):
    first_new = beta_first * first + (1.0 - beta_first) * grads
    second_new = beta_second * second + (1.0 - beta_second) * grads * grads
    first_hat = first_new / (1.0 - beta_first**step)
    second_hat = second_new / (1.0 - beta_second**step)
    weights_new = weights - rate_per_step * step * (
        first_hat / (jnp.sqrt(second_hat) + adam_epsilon) + weight_decay * weights
    )
    return (weights_new, first_new, second_new)


def per_device(
    tokens,
    cotangent,
    segment_ids,
    buckets,
    owners,
    master,
    first_moment,
    second_moment,
    small_params,
    small_first,
    small_second,
    adapter_ema,
    step_count,
):
    dp_count = lax.axis_size("dp")
    tensor_count = lax.axis_size("tensor")
    capacity = master.shape[1]
    group_heads = H // tensor_count
    head_rows = group_heads * HS
    hidden_rows = FF // tensor_count
    dp_pos = lax.axis_index("dp")
    tensor_pos = lax.axis_index("tensor")

    slots = owner_slots(owners, dp_count, capacity)
    gathered = lax.all_gather(master[0].astype(jnp.bfloat16), "dp", axis=0, tiled=True)
    ends = (0, 3 * head_rows, 4 * head_rows, 4 * head_rows + hidden_rows, owners.shape[0])
    w_qkv, w_out, w_in, w_down = [
        lax.all_gather(jnp.take(gathered, slots[low:high], axis=0), "tensor", axis=0, tiled=True)
        for low, high in zip(ends[:-1], ends[1:])
    ]

    gain_one, gain_two, adapter, table = unpack(small_params)
    bucket_onehot = (buckets[:, None] == jnp.arange(NB, dtype=jnp.int32)[None, :]).astype(
        jnp.float32
    )
    per_offset = contract(table, bucket_onehot, 0, 1)
    bias_rows = jnp.concatenate([jnp.zeros((H, 1), jnp.float32), per_offset[:, ::-1]], axis=1)
    segments = lax.dynamic_slice_in_dim(segment_ids, tensor_pos * SEQ, SEQ, 0)
    segment_keys = jnp.broadcast_to(segments[:, None], (SEQ, TILE))

    inputs_f = tokens.astype(jnp.float32)
    normed_one = rms_norm(inputs_f, gain_one).astype(jnp.bfloat16)
    projected = contract(w_qkv, normed_one, 1, 1).astype(jnp.bfloat16)
    exp_scores, attended, scale = attend(
        projected, bias_rows[:, None, :], segment_keys, segments[None, :], group_heads
    )
    mid = inputs_f + contract(attended, w_out, 0, 0)
    normed_two = rms_norm(mid, gain_two).astype(jnp.bfloat16)
    activ, slope, ffn_out = feed(normed_two, w_in, w_down)
    final, adapter_pull = jax.vjp(adapter_apply, ffn_out, adapter)
    layer_out = (mid + final).astype(jnp.bfloat16)

    out_grad = cotangent.astype(jnp.float32)
    ffn_grad, adapter_grad = adapter_pull(out_grad)
    ffn_grad = ffn_grad.astype(jnp.bfloat16)

    def reduce_rows(part):
        part = lax.psum_scatter(
            part.astype(jnp.bfloat16), "tensor", scatter_dimension=0, tiled=True
        )
        return lax.psum(part, "dp")

    pre_grad = (contract(ffn_grad, w_down, 1, 1) * slope.astype(jnp.float32)).astype(jnp.bfloat16)
    down_grad = reduce_rows(contract(activ, ffn_grad, 0, 0))
    in_grad = reduce_rows(contract(pre_grad, normed_two, 0, 0))
    normed_two_grad = jnp.dot(pre_grad, w_in, preferred_element_type=jnp.float32)
    _, norm_two_pull = jax.vjp(rms_norm, mid, gain_two)
    mid_extra, gain_two_grad = norm_two_pull(normed_two_grad)
    mid_grad = out_grad + mid_extra
    mid_grad_low = mid_grad.astype(jnp.bfloat16)
    attended_grad = contract(w_out, mid_grad_low, 1, 1).astype(jnp.bfloat16)
    out_weight_grad = reduce_rows(jnp.dot(attended, mid_grad_low, preferred_element_type=jnp.float32))
    query_grad, key_grad, value_grad, offset_grad = attend_back(
        projected, exp_scores, attended, scale, attended_grad, group_heads
    )
    proj_grad = jnp.stack(
        [
            part.reshape(tensor_count, head_rows, SEQ)
            for part in (query_grad, key_grad, value_grad)
        ],
        axis=1,
    ).reshape(3 * D, SEQ)
    qkv_grad = reduce_rows(jnp.dot(proj_grad, normed_one, preferred_element_type=jnp.float32))
    normed_one_grad = contract(proj_grad, w_qkv, 0, 0)
    _, norm_one_pull = jax.vjp(rms_norm, inputs_f, gain_one)
    input_extra, gain_one_grad = norm_one_pull(normed_one_grad)
    input_grad = (mid_grad + input_extra).astype(jnp.bfloat16)
    table_grad = jnp.dot(
        bucket_onehot.T, offset_grad[:, 0, 1:][:, ::-1].T, precision=highest
    )
    small_local = jnp.concatenate(
        [gain_one_grad, gain_two_grad]
        + [piece.reshape(-1) for piece in adapter_grad]
        + [table_grad.reshape(-1)]
    )
    small_total = lax.psum(small_local, ("dp", "tensor"))

    bank_grad = jnp.concatenate([qkv_grad, out_weight_grad, in_grad, down_grad], axis=0)
    own_slots = dp_pos * capacity + jnp.arange(capacity, dtype=jnp.int32)
    match = slots[None, :] == own_slots[:, None]
    own_filled = jnp.any(match, axis=1)
    own_rows = jnp.sum(
        jnp.where(match, jnp.arange(owners.shape[0], dtype=jnp.int32)[None, :], 0), axis=1
    )
    own_filled = own_filled.astype(jnp.float32)[:, None]
    owned_grad = jnp.take(bank_grad, own_rows, axis=0).astype(jnp.float32) * own_filled
    step = step_count[0].astype(jnp.float32)
    new_master, new_first, new_second = adamw(
        master[0], owned_grad, first_moment[0], second_moment[0], step
    )
    new_master = new_master * own_filled
    new_first = new_first * own_filled
    new_second = new_second * own_filled
    small_new, small_first_new, small_second_new = adamw(
        small_params, small_total, small_first, small_second, step
    )
    ema_new = average_keep * adapter_ema + (1.0 - average_keep) * small_new[2 * D : 2 * D + NADAPT]
    return (
        layer_out,
        input_grad,
        owned_grad[None],
        new_first[None],
        new_second[None],
        new_master[None],
        new_master.astype(jnp.bfloat16)[None],
        small_total,
        small_first_new,
        small_second_new,
        small_new,
        ema_new,
    )


def solution(mesh):
    token_spec = P(("dp", "tensor"), None)
    owner_spec = P("tensor", "dp", None)
    return jax.shard_map(
        per_device,
        mesh=mesh,
        in_specs=(token_spec, token_spec, P("dp"), P(), P())
        + (owner_spec,) * 3
        + (P(),) * 5,
        out_specs=(token_spec,) * 2 + (owner_spec,) * 5 + (P(),) * 5,
        check_vma=False,
    )
```

time: 2360 us -> 674 us (0.29)
  local copies, waits for them, and re-layouts: 1170 us -> 51.9 us
  matrix products: 359 us -> 98.7 us
  waiting for transfers between devices: 525 us -> 335 us
  other arithmetic: 188 us -> 31.7 us
  Pallas kernels: 0 us -> 90.7 us
  loops' own time: 42.1 us -> 0 us
    while x156 -> x0, local copies, waits for them, and re-layouts: 649 us -> none
    reshape x30 -> x1, local copies, waits for them, and re-layouts: 325 us -> 0.11 us  [per_device(): table_grad.reshape(-1)]
    dot_general x70 -> x12, matrix products: 325 us -> 71.4 us  [the longest x8 55.8 us: contract(): lax.dot_general(left, right, (((left_dim,), (right_dim,)), ((), ())), pre...]
    all_to_all x1 -> x0, waiting for transfers between devices: 104 us -> none  [per_device(): lax.all_to_all(packed.reshape(dp_count, capacity, D).astype(jnp.bfloat16)...]
    all_gather x4, waiting for transfers between devices: 149 us -> 49.2 us  [per_device(): lax.all_gather(jnp.take(gathered, slots[low:high], axis=0), 'tensor', axi...]
    slice x45 -> x2, local copies, waits for them, and re-layouts: 97 us -> 0.58 us  [the longest x16 94.2 us: toeplitz_rows(): tiled = jnp.tile(pattern, (1, row_count))[:, :row_count * (period - 1)]]
    pallas_call x0 -> x3, Pallas kernels: none -> 90.7 us  [the longest x1 38.2 us: attend_back(): pl.pallas_call(attend_back_kernel, grid=(H,), in_specs=head_specs(group_h...]
    psum x0 -> x1, waiting for transfers between devices: none -> 71.8 us  [reduce_rows(): return lax.psum(part, 'dp')]
  transfers between devices with their start and end apart: 10 -> 10, of which waited for: 9 -> 7; matrix products, arithmetic and copies ran while one was open for 5% -> 19% of each run, Pallas kernels for 0% -> 11%
where the time goes in v1:
time: 674 us; the launch traced here: 667 us
  waiting for transfers between devices  335 us (50%)
  matrix products  98.7 us (15%)
  Pallas kernels  90.7 us (13%)
  local copies, waits for them, and re-layouts  51.9 us (8%)
  blocking collectives  42.1 us (6%)
  other arithmetic  31.7 us (5%)
  between operations  15.9 us (2%)
    all_gather x1, waiting for transfers between devices, per_device(): lax.all_gather(master[0].astype(jnp.bfloat16), 'dp', axis=0, tiled=True)  110 us
    reduce_scatter x4, waiting for transfers between devices, reduce_rows(): lax.psum_scatter(part.astype(jnp.bfloat16), 'tensor', scatter_dimension=0...  104 us
    psum x1, waiting for transfers between devices, reduce_rows(): return lax.psum(part, 'dp')  71.8 us
    dot_general x8, matrix products, contract(): lax.dot_general(left, right, (((left_dim,), (right_dim,)), ((), ())), pre...  55.8 us
    all_gather x4, waiting for transfers between devices, per_device(): lax.all_gather(jnp.take(gathered, slots[low:high], axis=0), 'tensor', axi...  49.2 us
    psum x1, blocking collectives, per_device(): small_total = lax.psum(small_local, ('dp', 'tensor'))  42.1 us
    pallas_call x1, Pallas kernels, attend_back(): pl.pallas_call(attend_back_kernel, grid=(H,), in_specs=head_specs(group_h...  38.2 us
    pallas_call x1, Pallas kernels, attend(): pl.pallas_call(attend_kernel, grid=(H,), in_specs=head_specs(group_heads)...  32.2 us
  transfers between devices with their start and end apart: 10, of which 7 were waited for; matrix products, arithmetic and copies ran while one was open for 19% of the time, Pallas kernels for 11%

profile of v1, /device:TPU:0, one launch (start us, length us, event | category | flops | bytes accessed | tf_op | source)
XLA Modules:
  0.0 666.8 jit_solution(8558002549009879045)
XLA Ops:
  7.2 2.5 convert_element_type.97
  9.8 2.3 reduce-window.6
  12.8 109.5 %all-gather.15.cloned.1.call-done = bf16[1,4608,768]{2,1,0:T(8,128)(2,1)} async-done(((bf16[1,576,768]{2,1,0:T(8,128)(2,1)}), bf16[1,4608,768]{2,1,0:T(8,128)(2,1)}) %all-gather.15.cloned.1.call-update) | async-done | bytes 7077904 | tf_op jit(solution)/shard_map/all_gather | solution.py:380
  122.3 7.4 %gather_fusion = bf16[576,768]{1,0:T(8,128)(2,1)S(1)} fusion(bf16[4608,768]{1,0:T(8,128)(2,1)} %bitcast.134, s32[1024]{0:T(1024)S(1)} %pad_clamp_fusion.4), kind=kCustom, calls=%fused_computation.2 | custom fusion | bytes 1771776 | tf_op jit(solution)/shard_map/jit(_take)/gather | solution.py:383
  129.7 1.1 broadcast_select_fusion.2
  131.0 5.1 gather_fusion.1
  136.1 0.8 broadcast_select_fusion.3
  137.0 7.7 %gather_fusion.4 = bf16[768,768]{1,0:T(8,128)(2,1)S(1)} fusion(bf16[4608,768]{1,0:T(8,128)(2,1)} %bitcast.136, s32[1024]{0:T(1024)S(1)} %get-tuple-element.63), kind=kCustom, calls=%fused_computation.1.clone | custom fusion | bytes 2362368 | tf_op jit(solution)/shard_map/jit(_take)/gather | solution.py:383
  144.8 1.2 broadcast_select_fusion
  146.1 7.3 %gather_fusion.3 = bf16[768,768]{1,0:T(8,128)(2,1)S(1)} fusion(bf16[4608,768]{1,0:T(8,128)(2,1)} %bitcast.137, s32[1024]{0:T(1024)S(1)} %get-tuple-element.64), kind=kCustom, calls=%fused_computation.clone | custom fusion | bytes 2362368 | tf_op jit(solution)/shard_map/jit(_take)/gather | solution.py:383
  153.4 1.2 broadcast_select_fusion.1
  156.7 1.1 reverse
  158.9 0.8 reshape.382
  161.8 8.0 %convolution_convert_fusion.query_ref.key_ref.value_ref = bf16[2304,1024]{1,0:T(8,128)(2,1)} fusion(bf16[2304,768]{1,0:T(8,128)(2,1)} %all-gather.7.cloned.1.call-done, bf16[1024,768]{1,0:T(8,128)(2,1)S(1)} %copy-done.10, f32[768]{0:T(1024)S(1)} %get-tuple-element.51, f32[1024]{0:T(1024)S(1)} %fusion.64), kind=kOutput, calls=%fused_computation.13 | convolution fusion | flops 3629383680 | bytes 9837568 | tf_op jit(solution)/shard_map/dot_general | solution.py:81
  170.0 32.2 %attend.1 = (bf16[12,1024,1024]{2,1,0:T(8,128)(2,1)}, bf16[768,1024]{1,0:T(8,128)(2,1)S(1)}, f32[12,1,1024]{2,1,0:T(1,128)S(1)}) custom-call(bf16[2304,1024]{1,0:T(8,128)(2,1)} %convolution_convert_fusion.query_ref.key_ref.value_ref, bf16[2304,1024]{1,0:T(8,128)(2,1)} %convolution_convert_fusion.query_ref.key_ref.value_ref, ...), custom_call_target="tpu_custom_call" | custom-call | flops 12884901888 | bytes 33554432 | tf_op jit(solution)/shard_map/attend/pallas_call | solution.py:231
  202.2 4.0 multiply_reduce_fusion.2
  206.2 1.7 copy-done.3
  207.9 1.5 multiply_convert_fusion.1.rows_ref
  209.4 9.7 %all-gather.13.cloned.1.call-done.w_down_ref = bf16[3072,768]{1,0:T(8,128)(2,1)} async-done(((bf16[768,768]{1,0:T(8,128)(2,1)}), bf16[3072,768]{1,0:T(8,128)(2,1)}) %all-gather.13.cloned.1.call-update) | async-done | bytes 4718608 | tf_op jit(solution)/shard_map/all_gather | solution.py:383
  219.0 39.5 %all-gather.11.cloned.1.call-done.w_in_ref = bf16[3072,768]{1,0:T(8,128)(2,1)} async-done(((bf16[768,768]{1,0:T(8,128)(2,1)}), bf16[3072,768]{1,0:T(8,128)(2,1)}) %all-gather.11.cloned.1.call-update) | async-done | bytes 4718608 | tf_op jit(solution)/shard_map/all_gather | solution.py:383
  258.5 1.4 copy-done
  259.9 20.3 %feed.1 = (bf16[1024,3072]{1,0:T(8,128)(2,1)}, bf16[1024,3072]{1,0:T(8,128)(2,1)}, f32[1024,768]{1,0:T(8,128)S(1)}) custom-call(bf16[1024,768]{1,0:T(8,128)(2,1)S(1)} %copy-done, bf16[3072,768]{1,0:T(8,128)(2,1)} %all-gather.11.cloned.1.call-done.w_in_ref, bf16[3072,768]{1,0:T(8,128)(2,1)} %all-gather.13.cloned.1.call-done.w_down_ref), custom_call_target="tpu_custom_call" | custom-call | flops 9663676416 | bytes 25165824 | tf_op jit(solution)/shard_map/feed/pallas_call | solution.py:316
  280.2 3.1 fusion.76
  284.0 1.7 multiply_add_fusion.1
  285.7 2.7 fusion.5
  288.5 8.0 %multiply_convert_fusion = bf16[1024,3072]{1,0:T(8,128)(2,1)S(1)} fusion(bf16[1024,3072]{1,0:T(8,128)(2,1)} %get-tuple-element.25, bf16[1024,768]{1,0:T(8,128)(2,1)S(1)} %fusion.5, bf16[3072,768]{1,0:T(8,128)(2,1)S(1)} %bitcast.153), kind=kOutput, calls=%fused_computation.5 | convolution fusion | flops 4841275392 | bytes 18874368 | tf_op jit(solution)/shard_map/dot_general | solution.py:81
  296.6 5.9 multiply_reduce_fusion
  302.5 0.8 convert_add_fusion.1
  303.4 1.6 copy-done.5
  305.0 2.4 convolution_convert_fusion.5
  307.4 4.8 convolution_convert_fusion.4.out_grad_ref
  312.3 38.2 %attend_back.1 = (bf16[768,1024]{1,0:T(8,128)(2,1)S(1)}, bf16[768,1024]{1,0:T(8,128)(2,1)S(1)}, bf16[768,1024]{1,0:T(8,128)(2,1)S(1)}, f32[12,1,2048]{2,1,0:T(1,128)S(1)}) custom-call(bf16[2304,1024]{1,0:T(8,128)(2,1)} %convolution_convert_fusion.query_ref.key_ref.value_ref, bf16[2304,1024]{1,0:T(8,128)(2,1)} %convolution_convert_fusion.query_ref.key_ref.value_ref, ...), custom_call_target="tpu_custom_call" | custom-call | flops 25769803776 | bytes 33554432 | tf_op jit(solution)/shard_map/attend_back/pallas_call | solution.py:263
  351.1 2.1 copy-done.14
  353.2 5.5 convolution_convert_fusion.3
  358.8 9.7 %convolution_convert_fusion.2 = bf16[3072,768]{1,0:T(8,128)(2,1)} fusion(bf16[1024,3072]{1,0:T(8,128)(2,1)} %copy-done.42, bf16[1024,768]{1,0:T(8,128)(2,1)} %multiply_convert_fusion.1.rows_ref), kind=kOutput, calls=%fused_computation.16 | convolution fusion | flops 4834197504 | bytes 12582912 | tf_op jit(solution)/shard_map/dot_general | solution.py:81
  368.5 9.3 %convolution_convert_fusion.1 = bf16[3072,768]{1,0:T(8,128)(2,1)} fusion(bf16[1024,3072]{1,0:T(8,128)(2,1)} %get-tuple-element.31, bf16[1024,768]{1,0:T(8,128)(2,1)} %copy-done.16), kind=kOutput, calls=%fused_computation.15 | convolution fusion | flops 4834197504 | bytes 12582912 | tf_op jit(solution)/shard_map/dot_general | solution.py:81
  380.1 0.8 compare_reduce_fusion
  380.9 0.8 fusion
  382.9 3.4 fusion.35
  386.3 1.1 reshape.384
  388.4 1.0 convolution_bitcast_fusion.5
  390.3 3.7 fusion.77
  394.0 1.1 reshape.385
  395.1 1.0 convolution_bitcast_fusion.4
  396.1 3.4 reduce-scatter.5.cloned.1.call-done
  399.5 50.4 %reduce-scatter.9.cloned.1.call-done = bf16[768,768]{1,0:T(8,128)(2,1)} async-done(((bf16[3072,768]{1,0:T(8,128)(2,1)}), bf16[768,768]{1,0:T(8,128)(2,1)}) %reduce-scatter.9.cloned.1.call-update) | async-done | bytes 1179664 | tf_op jit(solution)/shard_map/reduce_scatter | solution.py:413
  449.9 50.6 %reduce-scatter.11.cloned.1.call-done = bf16[768,768]{1,0:T(8,128)(2,1)} async-done(((bf16[3072,768]{1,0:T(8,128)(2,1)}), bf16[768,768]{1,0:T(8,128)(2,1)}) %reduce-scatter.11.cloned.1.call-update) | async-done | bytes 1179664 | tf_op jit(solution)/shard_map/reduce_scatter | solution.py:413
  500.5 1.0 fusion.48
  501.4 1.0 fusion.44
  503.1 1.0 fusion.42
  505.4 1.3 reverse.1
  506.7 1.8 fusion.14
  508.7 11.3 %fusion.4 = (f32[768]{0:T(1024)S(1)}, f32[1024]{0:T(1024)}, f32[1024,768]{1,0:T(8,128)}) fusion(bf16[1024,768]{1,0:T(8,128)(2,1)} %param.15, f32[1024]{0:T(1024)} %copy-done.29, f32[768]{0:T(1024)} %copy-done.32, bf16[2304,1024]{1,0:T(8,128)(2,1)} %bitcast.139, bf16[2304,768]{1,0:T(8,128)(2,1)} %all-gather.7.cloned.1.call-done), kind=kOutput, calls=%fused_computation.27 | convolution fusion | flops 3629381888 | bytes 12990464 | tf_op jit(solution)/shard_map/dot_general | solution.py:81
  520.0 0.7 concatenate.11
  520.7 42.1 %psum.39 = f32[3616]{0:T(1024)S(1)} all-reduce(f32[3616]{0:T(1024)S(1)} %concatenate.11), channel_id=1, replica_groups=mesh['dp'=8,'tensor'=4] {'dp','tensor'}, use_global_device_ids=true, to_apply=%region_19.21 | all-reduce | flops 3616 | bytes 28928 | tf_op jit(solution)/shard_map/psum | solution.py:451
  563.5 1.4 multiply_subtract_fusion
  564.9 1.3 fusion.59
  566.2 5.7 add_convert_fusion
  572.0 2.0 fusion.7
  573.9 71.8 %all-reduce.4.cloned.1.call-done = (bf16[768,768]{1,0:T(8,128)(2,1)}, bf16[768,768]{1,0:T(8,128)(2,1)}, bf16[192,768]{1,0:T(8,128)(2,1)}, bf16[576,768]{1,0:T(8,128)(2,1)}) async-done(((bf16[768,768]{1,0:T(8,128)(2,1)}, bf16[768,768]{1,0:T(8,128)(2,1)}, bf16[192,768]{1,0:T(8,128)(2,1)}, bf16[576,768]{1,0:T(8,128)(2,1)}), (bf16[768,768]{1,0:T(8,128)(2,1)}, bf16[768,768]{1,0:T(8,128)(2,1)}, ...) | async-done | bytes 3538960 | tf_op jit(solution)/shard_map/psum | solution.py:416
  645.8 2.1 pad_maximum_fusion.1
  648.0 3.3 gather_fusion.2
  651.3 6.1 fusion.72
  657.4 2.4 broadcast_multiply_fusion
  (178 shorter events, 15.4 us)
Async XLA Ops:
  7.2 2.6 copy-start.23
  7.2 115.1 %all-gather.15.cloned.1.call-start = ((), (), s32[]{:S(2)}) async-start(), calls=%async_computation.12 | async-start | bytes 7962624 | tf_op jit(solution)/shard_map/all_gather | solution.py:380
  9.7 152.0 %all-gather.7.cloned.1.call-start = ((), (), s32[]{:S(2)}) async-start(), calls=%async_computation.4 | async-start | bytes 4423680 | tf_op jit(solution)/shard_map/all_gather | solution.py:383
  130.8 71.4 %all-gather.9.cloned.1.call-start = ((), (), s32[]{:S(2)}) async-start(), calls=%async_computation.5 | async-start | bytes 1474560 | tf_op jit(solution)/shard_map/all_gather | solution.py:383
  137.0 82.1 %all-gather.13.cloned.1.call-start = ((), (), s32[]{:S(2)}) async-start(), calls=%async_computation.7 | async-start | bytes 5898240 | tf_op jit(solution)/shard_map/all_gather | solution.py:383
  146.0 112.5 %all-gather.11.cloned.1.call-start = ((), (), s32[]{:S(2)}) async-start(), calls=%async_computation.6 | async-start | bytes 5898240 | tf_op jit(solution)/shard_map/all_gather | solution.py:383
  153.3 1.8 copy-start.24
  153.4 2.7 copy-start.41
  153.4 8.0 %copy-start.10 = (bf16[1024,768]{1,0:T(8,128)(2,1)S(1)}, bf16[1024,768]{1,0:T(8,128)(2,1)}, u32[]{:S(2)}) copy-start(bf16[1024,768]{1,0:T(8,128)(2,1)} %param.15) | copy-start | bytes 4718596
  154.6 241.5 %reduce-scatter.7.cloned.1.call-start = ((), (), s32[]{:S(2)}) async-start(), calls=%async_computation.9 | async-start | bytes 1474560 | tf_op jit(solution)/shard_map/reduce_scatter | solution.py:413
  155.4 5.3 copy-start.27
  155.9 195.2 %copy-start.32 = (f32[768]{0:T(1024)}, f32[768]{0:T(1024)S(1)}, u32[]{:S(2)}) copy-start(f32[768]{0:T(1024)S(1)} %get-tuple-element.51) | copy-start | bytes 9220
  161.7 189.4 %copy-start.29 = (f32[1024]{0:T(1024)}, f32[1024]{0:T(1024)S(1)}, u32[]{:S(2)}) copy-start(f32[1024]{0:T(1024)S(1)} %fusion.64) | copy-start | bytes 12292
  202.2 4.0 copy-start.1
  206.2 1.7 copy-start.3
  258.5 1.4 copy-start
  280.2 3.8 copy-start.13
  280.2 3.8 copy-start.21
  280.2 8.2 %slice-start = ((s8[4718592]{0:T(1024)(128)(4,1)}), s8[4194304]{0:T(1024)(128)(4,1)S(1)}, s32[]{:S(2)}) async-start(s8[4718592]{0:T(1024)(128)(4,1)} %bitcast.152), calls=%async_computation.14 | async-start | bytes 8388608
  283.3 0.7 copy-start.17
  284.0 4.4 slice-start.1
  285.7 10.8 %copy-start.20 = (f32[1024,48]{0,1:T(8,128)}, f32[1024,48]{0,1:T(8,128)S(1)}, u32[]{:S(2)}) copy-start(f32[1024,48]{0,1:T(8,128)S(1)} %multiply_add_fusion.1) | copy-start | bytes 589828
  285.7 10.8 %slice-start.2 = ((s8[4718592]{0:T(1024)(128)(4,1)}), s8[4194304]{0:T(1024)(128)(4,1)S(1)}, s32[]{:S(2)}) async-start(s8[4718592]{0:T(1024)(128)(4,1)} %bitcast.154), calls=%async_computation.16 | async-start | bytes 8388608
  288.4 8.1 %copy-start.16 = (bf16[1024,768]{1,0:T(8,128)(2,1)}, bf16[1024,768]{1,0:T(8,128)(2,1)S(1)}, u32[]{:S(2)}) copy-start(bf16[1024,768]{1,0:T(8,128)(2,1)S(1)} %fusion.5) | copy-start | bytes 4718596
  288.5 8.1 %copy-start.4 = (f32[1024,768]{1,0:T(8,128)S(1)}, f32[1024,768]{1,0:T(8,128)}, u32[]{:S(2)}) copy-start(f32[1024,768]{1,0:T(8,128)} %copy-done.3) | copy-start | bytes 9437188
  288.5 8.1 %slice-start.3 = ((s8[4718592]{0:T(1024)(128)(4,1)}), s8[524288]{0:T(1024)(128)(4,1)S(1)}, s32[]{:S(2)}) async-start(s8[4718592]{0:T(1024)(128)(4,1)} %bitcast.154), calls=%async_computation.17 | async-start | bytes 1048576
  296.6 5.9 copy-start.42
  302.5 2.5 copy-start.2
  303.3 1.6 copy-start.5
  307.4 92.1 %reduce-scatter.5.cloned.1.call-start = ((), (), s32[]{:S(2)}) async-start(), calls=%async_computation.8 | async-start | bytes 4423680 | tf_op jit(solution)/shard_map/reduce_scatter | solution.py:413
  350.5 2.7 copy-start.11
  351.1 2.1 copy-start.14
  358.7 91.1 %reduce-scatter.9.cloned.1.call-start = ((), (), s32[]{:S(2)}) async-start(), calls=%async_computation.10 | async-start | bytes 5898240 | tf_op jit(solution)/shard_map/reduce_scatter | solution.py:413
  368.5 132.0 %reduce-scatter.11.cloned.1.call-start = ((), (), s32[]{:S(2)}) async-start(), calls=%async_computation.11 | async-start | bytes 5898240 | tf_op jit(solution)/shard_map/reduce_scatter | solution.py:413
  377.9 5.1 copy-start.18
  377.9 267.9 %all-reduce.4.cloned.1.call-start = ((), (), s32[]{:S(2)}) async-start(), calls=%async_computation.13 | async-start | bytes 7077888 | tf_op jit(solution)/shard_map/psum | solution.py:416
  379.4 10.1 %copy-start.35 = (f32[4,4,4,1]{2,1,0,3:T(4,128)}, f32[4,4,4,1]{2,1,0,3:T(4,128)S(1)}, u32[]{:S(2)}) copy-start(f32[4,4,4,1]{2,1,0,3:T(4,128)S(1)} %reshape.448) | copy-start | bytes 772
  390.3 110.2 %copy-start.37 = (f32[4,12,1,1]{1,0,2,3:T(4,128)S(1)}, f32[4,12,1,1]{1,0,2,3:T(4,128)}, u32[]{:S(2)}) copy-start(f32[4,12,1,1]{1,0,2,3:T(4,128)} %reshape.443) | copy-start | bytes 580
  390.3 111.1 %copy-start.36 = (f32[4,12,1,1]{1,0,2,3:T(4,128)S(1)}, f32[4,12,1,1]{1,0,2,3:T(4,128)}, u32[]{:S(2)}) copy-start(f32[4,12,1,1]{1,0,2,3:T(4,128)} %reshape.445) | copy-start | bytes 580
  390.3 114.3 %copy-start.28 = (f32[4,12]{1,0:T(4,128)S(1)}, f32[4,12]{1,0:T(4,128)}, u32[]{:S(2)}) copy-start(f32[4,12]{1,0:T(4,128)} %copy-done.27) | copy-start | bytes 580
  508.6 11.4 %copy-start.34 = (f32[768]{0:T(1024)S(1)}, f32[768]{0:T(1024)}, u32[]{:S(2)}) copy-start(f32[768]{0:T(1024)} %reshape.390) | copy-start | bytes 9220
  508.6 11.4 %copy-start.38 = (f32[768]{0:T(1024)S(1)}, f32[768]{0:T(1024)}, u32[]{:S(2)}) copy-start(f32[768]{0:T(1024)} %get-tuple-element.33) | copy-start | bytes 9220
  508.6 11.4 %copy-start.40 = (f32[48]{0:T(128)S(1)}, f32[48]{0:T(128)}, u32[]{:S(2)}) copy-start(f32[48]{0:T(128)} %reshape.389) | copy-start | bytes 580
  508.6 57.5 %copy-start.19 = (f32[1024,48]{0,1:T(8,128)S(1)}, f32[1024,48]{0,1:T(8,128)}, u32[]{:S(2)}) copy-start(f32[1024,48]{0,1:T(8,128)} %copy-done.17) | copy-start | bytes 589828
  508.6 57.5 %copy-start.22 = (f32[48,768]{1,0:T(8,128)S(1)}, f32[48,768]{1,0:T(8,128)}, u32[]{:S(2)}) copy-start(f32[48,768]{1,0:T(8,128)} %reshape.382) | copy-start | bytes 442372
  562.8 9.1 %copy-start.25 = (f32[3616]{0:T(1024)}, f32[3616]{0:T(1024)S(1)}, u32[]{:S(2)}) copy-start(f32[3616]{0:T(1024)S(1)} %psum.39) | copy-start | bytes 43396
  564.9 7.1 %copy-start.26 = (f32[3616]{0:T(1024)}, f32[3616]{0:T(1024)S(1)}, u32[]{:S(2)}) copy-start(f32[3616]{0:T(1024)S(1)} %get-tuple-element.41) | copy-start | bytes 43396
  566.2 5.8 copy-start.6
  566.2 5.8 copy-start.12
  566.2 5.8 copy-start.15
  566.2 5.8 copy-start.30
  566.2 5.8 copy-start.33
  645.8 2.2 copy-start.31
  647.9 3.4 copy-start.39
  651.3 6.1 copy-start.7
  651.3 6.1 copy-start.8
  657.4 2.4 copy-start.9
Sparse Core Ops, SparseCore 0:
  10.8 111.4 all-gather.14
  130.9 29.2 all-gather.6
  162.3 17.2 all-gather.8
  181.5 37.4 all-gather.12
  221.0 37.4 all-gather.10
  307.5 25.7 reduce-scatter.6
  358.9 40.5 reduce-scatter.4
  402.0 47.8 reduce-scatter.8
  452.6 47.8 reduce-scatter.10
  504.2 141.5 all-reduce.3

commit v2 on v1

v2 whole, which is shorter than its diff:
```python
import functools
import math

import jax
import jax.numpy as jnp
from jax import lax
from jax.experimental import pallas as pl
from jax.experimental.pallas import tpu as pltpu
from jax.sharding import PartitionSpec as P

D = 768
H = 12
HS = 64
FF = 3072
NB = 32
R = 48
PHM = 4
SEQ = 1024
NADAPT = 1696

highest = lax.Precision.HIGHEST
norm_epsilon = 1e-06
beta_first = 0.5
beta_second = 0.5
adam_epsilon = 1e-08
rate_per_step = 0.01
weight_decay = 0.1
average_keep = 0.75
masked_score = -1000000000.0

TILE = 128
WINDOW = 2 * SEQ - TILE
QUERY_TILE = 256
KEY_TILE = 256
VMEM_LIMIT = 48 * 1024 * 1024
MESH = pl.DeviceIdType.MESH


def unpack(packed):
    widths = (D, D, PHM**3, D, R, R, D, NB * H)
    pieces = []
    offset = 0
    for width in widths:
        pieces.append(packed[offset : offset + width])
        offset = offset + width
    gain_one, gain_two, mix_flat, down_left, down_right, up_left, up_right, table_flat = pieces
    adapter = (
        mix_flat.reshape(PHM, PHM, PHM),
        down_left.reshape(PHM, D // PHM),
        down_right.reshape(PHM, R // PHM),
        up_left.reshape(PHM, R // PHM),
        up_right.reshape(PHM, D // PHM),
    )
    return (gain_one, gain_two, adapter, table_flat.reshape(NB, H))


def adapter_apply(features, adapter):
    mix, down_left, down_right, up_left, up_right = adapter
    down_matrix = jnp.einsum(
        "iab,ip,iq->apbq", mix, down_left, down_right, precision=highest
    ).reshape(D, R)
    up_matrix = jnp.einsum("iab,iq,ip->aqbp", mix, up_left, up_right, precision=highest).reshape(
        R, D
    )
    hidden = jnp.dot(features, down_matrix, precision=highest)
    return features + jnp.dot(jax.nn.gelu(hidden, approximate=False), up_matrix, precision=highest)


def rms_norm(values, gain):
    return (
        values * lax.rsqrt(jnp.mean(values * values, axis=-1, keepdims=True) + norm_epsilon) * gain
    )


def contract(left, right, left_dim, right_dim):
    return lax.dot_general(
        left,
        right,
        (((left_dim,), (right_dim,)), ((), ())),
        preferred_element_type=jnp.float32,
    )


def bias_window(bias, window):
    for tile in range(WINDOW // TILE):
        base = WINDOW - TILE * tile
        row = jnp.broadcast_to(bias[:, base - TILE : base + TILE], (TILE, 2 * TILE))
        rolled = pltpu.roll(row, TILE, 1, stride=1, stride_axis=0)
        window[TILE * tile : TILE * (tile + 1), :] = rolled[:, :TILE]


def attend_head(
    query_rows, key_rows, value_rows, segment_keys_ref, segment_queries_ref, window, scores, exp_ref
):
    keys = key_rows.T
    values = jnp.concatenate([value_rows, jnp.ones((16, SEQ), jnp.bfloat16)], axis=0)
    outs, scales = [], []
    for q0 in range(0, SEQ, QUERY_TILE):
        queries = query_rows[:, q0 : q0 + QUERY_TILE]
        peak = jnp.full((8, QUERY_TILE), -jnp.inf, jnp.float32)
        for k0 in range(0, SEQ, KEY_TILE):
            raw = jnp.dot(keys[k0 : k0 + KEY_TILE], queries, preferred_element_type=jnp.float32)
            parts = []
            for l0 in range(0, QUERY_TILE, TILE):
                start = SEQ - TILE - (q0 + l0) + k0
                same_doc = (
                    segment_keys_ref[k0 : k0 + KEY_TILE, :]
                    == segment_queries_ref[:, q0 + l0 : q0 + l0 + TILE]
                )
                part = jnp.where(
                    same_doc,
                    raw[:, l0 : l0 + TILE] + window[start : start + KEY_TILE, :],
                    masked_score,
                )
                scores[k0 : k0 + KEY_TILE, l0 : l0 + TILE] = part
                parts.append(part)
            whole = jnp.concatenate(parts, axis=1)
            peak = jnp.maximum(peak, jnp.max(whole.reshape(KEY_TILE // 8, 8, QUERY_TILE), axis=0))
        peak = jnp.max(peak, axis=0, keepdims=True)
        total = jnp.zeros((HS + 16, QUERY_TILE), jnp.float32)
        for k0 in range(0, SEQ, KEY_TILE):
            exp_scores = jnp.exp(scores[k0 : k0 + KEY_TILE, :] - peak).astype(jnp.bfloat16)
            exp_ref[k0 : k0 + KEY_TILE, q0 : q0 + QUERY_TILE] = exp_scores
            total = total + jnp.dot(
                values[:, k0 : k0 + KEY_TILE], exp_scores, preferred_element_type=jnp.float32
            )
        scale = 1.0 / total[HS : HS + 1]
        scales.append(scale)
        outs.append((total[:HS] * scale).astype(jnp.bfloat16))
    return jnp.concatenate(outs, axis=1), jnp.concatenate(scales, axis=1)


def one_hot(place, shape, dim):
    hit = lax.broadcasted_iota(jnp.int32, shape, dim) == place
    return jnp.where(hit, 1.0, 0.0).astype(jnp.bfloat16)


def front_kernel(
    sizes,
    mine_ref,
    slot_place_ref,
    spread_place_ref,
    order_qkv_ref,
    order_out_ref,
    order_in_ref,
    order_down_ref,
    normed_ref,
    bias_ref,
    segment_keys_ref,
    segment_queries_ref,
    w_qkv_ref,
    w_out_ref,
    w_in_ref,
    w_down_ref,
    projected_ref,
    attended_ref,
    scale_ref,
    exp_ref,
    sent,
    received,
    spread,
    buf_qkv,
    buf_out,
    buf_in,
    buf_down,
    stage_out,
    stage_in,
    stage_down,
    window,
    scores,
    exp_stage,
    deal_send,
    deal_recv,
    gather_send,
    gather_recv,
    group_send,
    group_recv,
    local_sem,
    exp_sem,
):
    dp_count, pair_rows = sent.shape[0], sent.shape[1]
    tensor_count = w_qkv_ref.shape[0]
    heads = bias_ref.shape[0]
    group_heads = heads // tensor_count
    head_rows = group_heads * HS
    dp_pos, tensor_pos = lax.axis_index("dp"), lax.axis_index("tensor")
    core_peer = (dp_pos, tensor_pos + 1 - 2 * lax.rem(tensor_pos, 2))
    far_peer = (dp_pos, lax.rem(tensor_pos + 2, tensor_count))

    def dp_peer(m):
        return (lax.rem(dp_pos + m, dp_count), tensor_pos)

    def each_peer(run):
        def step(m, carry):
            run(m)
            return carry

        lax.fori_loop(1, dp_count, step, 0)

    barrier = pltpu.get_barrier_semaphore()

    def greet(m):
        pl.semaphore_signal(barrier, inc=1, device_id=dp_peer(m), device_id_type=MESH)

    each_peer(greet)
    for peer in (core_peer, far_peer):
        pl.semaphore_signal(barrier, inc=1, device_id=peer, device_id_type=MESH)

    place = slot_place_ref[...]
    mine = mine_ref[...]
    for m in range(dp_count):
        hot = one_hot(place - m * pair_rows, (pair_rows, mine.shape[0]), 0)
        sent[m] = jnp.dot(hot, mine, preferred_element_type=jnp.float32).astype(jnp.bfloat16)
    pl.semaphore_wait(barrier, dp_count + 1)

    def deal(m):
        return pltpu.make_async_remote_copy(
            sent.at[m],
            received.at[m],
            deal_send.at[m],
            deal_recv.at[m],
            device_id=dp_peer(m),
            device_id_type=MESH,
        )

    each_peer(lambda m: deal(m).start())
    received[0] = sent[0]
    each_peer(lambda m: deal(m).wait())
    rows = spread.shape[0]
    hot = one_hot(spread_place_ref[...], (rows, dp_count * pair_rows), 0)
    spread[...] = jnp.dot(
        hot, received[...].reshape(dp_count * pair_rows, D), preferred_element_type=jnp.float32
    ).astype(jnp.bfloat16)

    bufs = (buf_qkv, buf_out, buf_in, buf_down)
    orders = (order_qkv_ref, order_out_ref, order_in_ref, order_down_ref)
    stages = (w_qkv_ref.at[0], stage_out, stage_in, stage_down)
    finals = (w_qkv_ref, w_out_ref, w_in_ref, w_down_ref)
    offsets = [sum(buf.shape[1] for buf in bufs[:role]) for role in range(len(bufs))]

    def gather(role, m):
        count = bufs[role].shape[1]
        return pltpu.make_async_remote_copy(
            spread.at[pl.ds(offsets[role], count)],
            bufs[role].at[m],
            gather_send.at[role, m],
            gather_recv.at[role, m],
            device_id=dp_peer(m),
            device_id_type=MESH,
        )

    def start_gather(role):
        each_peer(lambda m: gather(role, m).start())
        bufs[role][0] = spread[offsets[role] : offsets[role] + bufs[role].shape[1], :]

    def order(role):
        each_peer(lambda m: gather(role, m).wait())
        count = bufs[role].shape[1]
        source = bufs[role][...].reshape(dp_count * count, D)
        step = 192
        for r0 in range(0, sizes[role], step):
            hot = one_hot(orders[role][r0 : r0 + step, :], (step, dp_count * count), 1)
            stages[role][r0 : r0 + step, :] = jnp.dot(
                hot, source, preferred_element_type=jnp.float32
            ).astype(jnp.bfloat16)

    def share(role, part):
        src, slot, peer = (
            (stages[role], 1, core_peer),
            (stages[role], 2, far_peer),
            (finals[role].at[2], 3, core_peer),
        )[part]
        return pltpu.make_async_remote_copy(
            src,
            finals[role].at[slot],
            group_send.at[role, part],
            group_recv.at[role, part],
            device_id=peer,
            device_id_type=MESH,
        )

    def keep(role):
        return pltpu.make_async_copy(stages[role], finals[role].at[0], local_sem.at[role])

    def start_share(role):
        order(role)
        share(role, 0).start()
        share(role, 1).start()
        if role > 0:
            keep(role).start()

    def forward(role):
        share(role, 1).wait_recv()
        share(role, 2).start()

    start_gather(0)
    start_share(0)
    start_gather(1)
    start_gather(2)

    def head_step(i, carry):
        group, head = lax.div(i, group_heads), lax.rem(i, group_heads)

        @pl.when(i == 1)
        def _():
            start_share(1)

        @pl.when(i == group_heads)
        def _():
            share(0, 0).wait_recv()

        @pl.when(i == 2 * group_heads)
        def _():
            forward(0)

        @pl.when(i == 3 * group_heads)
        def _():
            share(0, 2).wait_recv()
            forward(1)
            start_gather(3)

        @pl.when(head == 0)
        def _():
            projected_ref[group] = contract(w_qkv_ref[group], normed_ref[...], 1, 1).astype(
                jnp.bfloat16
            )

        def head_part(part):
            start = pl.multiple_of(part * head_rows + head * HS, HS)
            return projected_ref[group, pl.ds(start, HS), :]

        slot = lax.rem(i, 2)

        def save(head_index, slot):
            return pltpu.make_async_copy(
                exp_stage.at[slot], exp_ref.at[head_index], exp_sem.at[slot]
            )

        @pl.when(i >= 2)
        def _():
            save(i - 2, slot).wait()

        bias_window(bias_ref[i], window)
        attended, scale = attend_head(
            head_part(0),
            head_part(1),
            head_part(2),
            segment_keys_ref,
            segment_queries_ref,
            window,
            scores,
            exp_stage.at[slot],
        )
        attended_ref[pl.ds(pl.multiple_of(i * HS, HS), HS), :] = attended
        scale_ref[i] = scale
        save(i, slot).start()
        return carry

    lax.fori_loop(0, heads, head_step, 0)
    for i in (heads - 2, heads - 1):
        pltpu.make_async_copy(exp_stage.at[i % 2], exp_ref.at[i], exp_sem.at[i % 2]).wait()
    start_share(2)
    start_share(3)
    forward(2)
    forward(3)
    for role in range(len(bufs)):
        share(role, 0).wait_send()
        share(role, 1).wait_send()
        share(role, 2).wait_send()
        if role > 0:
            share(role, 0).wait_recv()
            share(role, 2).wait_recv()
            keep(role).wait()


def front(mine, slot_place, spread_place, orders, local_sizes, pair_rows, normed, bias, segments):
    dp_count, tensor_count = lax.axis_size("dp"), lax.axis_size("tensor")
    sizes = [order.shape[0] for order in orders]
    heads = bias.shape[0]
    low = jnp.bfloat16
    dma = pltpu.SemaphoreType.DMA
    roles = len(sizes)
    whole = pl.BlockSpec(memory_space=pltpu.VMEM)
    away = pl.BlockSpec(memory_space=pl.ANY)
    return pl.pallas_call(
        functools.partial(front_kernel, sizes),
        in_specs=[whole] * 11,
        out_specs=[whole, away, away, away, whole, whole, whole, away],
        out_shape=[jax.ShapeDtypeStruct((tensor_count, size, D), low) for size in sizes]
        + [
            jax.ShapeDtypeStruct((tensor_count, sizes[0], SEQ), low),
            jax.ShapeDtypeStruct((heads * HS, SEQ), low),
            jax.ShapeDtypeStruct((heads, 1, SEQ), jnp.float32),
            jax.ShapeDtypeStruct((heads, SEQ, SEQ), low),
        ],
        scratch_shapes=[
            pltpu.VMEM((dp_count, pair_rows, D), low),
            pltpu.VMEM((dp_count, pair_rows, D), low),
            pltpu.VMEM((sum(local_sizes), D), low),
        ]
        + [pltpu.VMEM((dp_count, size, D), low) for size in local_sizes]
        + [pltpu.VMEM((size, D), low) for size in sizes[1:]]
        + [
            pltpu.VMEM((WINDOW, TILE), jnp.float32),
            pltpu.VMEM((SEQ, QUERY_TILE), jnp.float32),
            pltpu.VMEM((2, SEQ, SEQ), low),
            dma((dp_count,)),
            dma((dp_count,)),
            dma((roles, dp_count)),
            dma((roles, dp_count)),
            dma((roles, 3)),
            dma((roles, 3)),
            dma((roles,)),
            dma((2,)),
        ],
        compiler_params=pltpu.CompilerParams(
            collective_id=1, has_side_effects=True, vmem_limit_bytes=56 * 1024 * 1024
        ),
        cost_estimate=pl.CostEstimate(
            flops=10 * heads * SEQ * SEQ * 256,
            bytes_accessed=64 * 1024 * 1024,
            transcendentals=heads * SEQ * SEQ,
        ),
        name="front",
    )(
        mine,
        slot_place[None, :],
        spread_place[None, :],
        *[order[:, None] for order in orders],
        normed,
        bias,
        jnp.broadcast_to(segments[:, None], (SEQ, TILE)),
        segments[None, :],
    )


def attend_back_kernel(
    query_ref,
    key_ref,
    value_ref,
    exp_ref,
    out_ref,
    scale_ref,
    out_grad_ref,
    proj_grad_ref,
    offset_grad_ref,
    window,
    score_grads,
):
    scaled = out_grad_ref[...].astype(jnp.float32) * scale_ref[0]
    delta = jnp.sum(scaled * out_ref[0].astype(jnp.float32), axis=0, keepdims=True)
    scaled_low = scaled.astype(jnp.bfloat16)
    delta_high = delta.astype(jnp.bfloat16).astype(jnp.float32)
    delta_rest = delta - delta_high
    place = lax.broadcasted_iota(jnp.int32, (16, SEQ), 0)
    extra = jnp.where(
        place == 0,
        jnp.broadcast_to(-delta_high, (16, SEQ)),
        jnp.where(place == 1, jnp.broadcast_to(-delta_rest, (16, SEQ)), 0.0),
    ).astype(jnp.bfloat16)
    grads = jnp.concatenate([scaled_low, extra], axis=0)
    values = jnp.concatenate([value_ref[0], jnp.ones((16, SEQ), jnp.bfloat16)], axis=0).T
    window[...] = jnp.zeros_like(window)
    keys = key_ref[0]
    for q0 in range(0, SEQ, QUERY_TILE):
        total = jnp.zeros((HS, QUERY_TILE), jnp.float32)
        for k0 in range(0, SEQ, KEY_TILE):
            centered = jnp.dot(
                values[k0 : k0 + KEY_TILE],
                grads[:, q0 : q0 + QUERY_TILE],
                preferred_element_type=jnp.float32,
            )
            score_grad = centered * exp_ref[
                0, k0 : k0 + KEY_TILE, q0 : q0 + QUERY_TILE
            ].astype(jnp.float32)
            for l0 in range(0, QUERY_TILE, TILE):
                start = SEQ - TILE - (q0 + l0) + k0
                window[start : start + KEY_TILE, :] += score_grad[:, l0 : l0 + TILE]
            score_low = score_grad.astype(jnp.bfloat16)
            score_grads[k0 : k0 + KEY_TILE, q0 : q0 + QUERY_TILE] = score_low
            total = total + jnp.dot(
                keys[:, k0 : k0 + KEY_TILE], score_low, preferred_element_type=jnp.float32
            )
        proj_grad_ref[0, 0, :, q0 : q0 + QUERY_TILE] = total.astype(jnp.bfloat16)
    queries = query_ref[0].T
    scaled_rows = scaled_low.T
    for k0 in range(0, SEQ, KEY_TILE):
        key_grad = jnp.dot(
            score_grads[k0 : k0 + KEY_TILE, :], queries, preferred_element_type=jnp.float32
        )
        value_grad = jnp.dot(
            exp_ref[0, k0 : k0 + KEY_TILE, :], scaled_rows, preferred_element_type=jnp.float32
        )
        proj_grad_ref[1, 0, :, k0 : k0 + KEY_TILE] = key_grad.T.astype(jnp.bfloat16)
        proj_grad_ref[2, 0, :, k0 : k0 + KEY_TILE] = value_grad.T.astype(jnp.bfloat16)
    offset_grad_ref[...] = jnp.zeros_like(offset_grad_ref)
    for tile in range(WINDOW // TILE):
        base = WINDOW - TILE * tile
        block = window[TILE * tile : TILE * (tile + 1), :]
        folded = jnp.concatenate([jnp.zeros((TILE, TILE), jnp.float32), block], axis=1)
        rows = TILE // 2
        while rows >= 1:
            folded = folded[:rows] + pltpu.roll(folded[rows:], 2 * TILE - rows, 1)
            rows //= 2
        offset_grad_ref[0, :, base - TILE : base + TILE] += folded


def attend_back(group, projected, exp_scores, attended, scale, attended_grad):
    heads = H // projected.shape[0]
    first = group * heads
    return pl.pallas_call(
        attend_back_kernel,
        grid=(heads,),
        in_specs=[
            pl.BlockSpec((1, HS, SEQ), lambda h, part=part: (group, part * heads + h, 0))
            for part in range(3)
        ]
        + [
            pl.BlockSpec((1, SEQ, SEQ), lambda h: (first + h, 0, 0)),
            pl.BlockSpec((1, HS, SEQ), lambda h: (group, h, 0)),
            pl.BlockSpec((1, 1, SEQ), lambda h: (first + h, 0, 0)),
            pl.BlockSpec((HS, SEQ), lambda h: (h, 0)),
        ],
        out_specs=[
            pl.BlockSpec((3, 1, HS, SEQ), lambda h: (0, h, 0, 0)),
            pl.BlockSpec((1, 1, 2 * SEQ), lambda h: (h, 0, 0)),
        ],
        out_shape=[
            jax.ShapeDtypeStruct((3, heads, HS, SEQ), jnp.bfloat16),
            jax.ShapeDtypeStruct((heads, 1, 2 * SEQ), jnp.float32),
        ],
        scratch_shapes=[
            pltpu.VMEM((WINDOW, TILE), jnp.float32),
            pltpu.VMEM((SEQ, SEQ), jnp.bfloat16),
        ],
        compiler_params=pltpu.CompilerParams(vmem_limit_bytes=VMEM_LIMIT),
        cost_estimate=pl.CostEstimate(
            flops=12 * heads * SEQ * SEQ * 256, bytes_accessed=3 * heads * SEQ * SEQ, transcendentals=0
        ),
        name="attend_back",
    )(projected, projected, projected, exp_scores, attended, scale, attended_grad)


def feed_kernel(rows_ref, w_in_ref, w_down_ref, before_ref, activ_ref, slope_ref, out_ref):
    row_tile = 256

    @pl.when(pl.program_id(0) == 0)
    def _():
        out_ref[...] = before_ref[...]

    for r0 in range(0, SEQ, row_tile):
        pre = contract(rows_ref[r0 : r0 + row_tile, :], w_in_ref[...], 1, 1)
        cdf = 0.5 * (1.0 + lax.erf(pre * (1.0 / math.sqrt(2.0))))
        pdf = jnp.exp(-0.5 * pre * pre) * (1.0 / math.sqrt(2.0 * math.pi))
        activ = (pre * cdf).astype(jnp.bfloat16)
        activ_ref[r0 : r0 + row_tile, :] = activ
        slope_ref[r0 : r0 + row_tile, :] = (cdf + pre * pdf).astype(jnp.bfloat16)
        out_ref[r0 : r0 + row_tile, :] += jnp.dot(
            activ, w_down_ref[...], preferred_element_type=jnp.float32
        )


def feed(rows, w_in, w_down, before):
    width = 384
    tokens = rows.shape[0]
    hidden = w_in.shape[0]
    return pl.pallas_call(
        feed_kernel,
        grid=(hidden // width,),
        in_specs=[
            pl.BlockSpec((tokens, D), lambda j: (0, 0)),
            pl.BlockSpec((width, D), lambda j: (j, 0)),
            pl.BlockSpec((width, D), lambda j: (j, 0)),
            pl.BlockSpec((tokens, D), lambda j: (0, 0)),
        ],
        out_specs=[
            pl.BlockSpec((tokens, width), lambda j: (0, j)),
            pl.BlockSpec((tokens, width), lambda j: (0, j)),
            pl.BlockSpec((tokens, D), lambda j: (0, 0)),
        ],
        out_shape=[
            jax.ShapeDtypeStruct((tokens, hidden), jnp.bfloat16),
            jax.ShapeDtypeStruct((tokens, hidden), jnp.bfloat16),
            jax.ShapeDtypeStruct((tokens, D), jnp.float32),
        ],
        compiler_params=pltpu.CompilerParams(vmem_limit_bytes=VMEM_LIMIT),
        cost_estimate=pl.CostEstimate(
            flops=8 * tokens * hidden * D,
            bytes_accessed=10 * 1024 * 1024,
            transcendentals=2 * tokens * hidden,
        ),
        name="feed",
    )(rows, w_in, w_down, before)


def select_kernel(by_row, count, place_ref, *refs):
    blocks, out_ref = refs[:-1], refs[-1]
    total = jnp.zeros(out_ref.shape, jnp.float32)
    offset = 0
    for block in blocks:
        rows = block.shape[0]
        shape = (count, rows)
        if by_row:
            hit = lax.broadcasted_iota(jnp.int32, shape, 1) + offset == place_ref[...]
        else:
            hit = lax.broadcasted_iota(jnp.int32, shape, 0) == place_ref[...]
        hit = jnp.where(hit, 1.0, 0.0).astype(jnp.bfloat16)
        total = total + jnp.dot(hit, block[...], preferred_element_type=jnp.float32)
        offset += rows
    out_ref[...] = total.astype(out_ref.dtype)


def select_rows(blocks, count, source=None, target=None, dtype=jnp.bfloat16):
    if len(blocks) > 16:
        blocks = [jnp.concatenate(blocks, axis=0)]
    place = source[:, None] if target is None else target[None, :]
    total = sum(block.shape[0] for block in blocks)
    return pl.pallas_call(
        functools.partial(select_kernel, target is None, count),
        out_shape=jax.ShapeDtypeStruct((count, D), dtype),
        compiler_params=pltpu.CompilerParams(vmem_limit_bytes=VMEM_LIMIT),
        cost_estimate=pl.CostEstimate(
            flops=2 * count * total * D, bytes_accessed=2 * (count + total) * D, transcendentals=0
        ),
        name="select_rows",
    )(place, *blocks)


def adamw(weights, grads, first, second, step):
    first_new = beta_first * first + (1.0 - beta_first) * grads
    second_new = beta_second * second + (1.0 - beta_second) * grads * grads
    first_hat = first_new / (1.0 - beta_first**step)
    second_hat = second_new / (1.0 - beta_second**step)
    weights_new = weights - rate_per_step * step * (
        first_hat / (jnp.sqrt(second_hat) + adam_epsilon) + weight_decay * weights
    )
    return (weights_new, first_new, second_new)


def per_device(
    tokens,
    cotangent,
    segment_ids,
    buckets,
    owners,
    master,
    first_moment,
    second_moment,
    small_params,
    small_first,
    small_second,
    adapter_ema,
    step_count,
):
    dp_count = lax.axis_size("dp")
    tensor_count = lax.axis_size("tensor")
    capacity = master.shape[1]
    group_heads = H // tensor_count
    head_rows = group_heads * HS
    hidden_rows = FF // tensor_count
    dp_pos = lax.axis_index("dp")
    tensor_pos = lax.axis_index("tensor")

    ends = (0, 3 * head_rows, 4 * head_rows, 4 * head_rows + hidden_rows, owners.shape[0])
    sizes = [high - low for low, high in zip(ends[:-1], ends[1:])]
    roles = len(sizes)

    pair_rows = -(-((capacity + roles * (dp_count - 1)) // dp_count) // 16) * 16
    owner_hot = (owners[:, None] == jnp.arange(dp_count, dtype=jnp.int32)[None, :]).astype(jnp.int32)
    counts = jnp.stack(
        [jnp.sum(owner_hot[low:high], axis=0) for low, high in zip(ends[:-1], ends[1:])]
    )
    dps = jnp.arange(dp_count, dtype=jnp.int32)
    starts = jnp.sum(
        jnp.where(dps[None, :] < dps[:, None], counts[:, None, :], 0), axis=2, dtype=jnp.int32
    )
    role_ids = jnp.arange(roles, dtype=jnp.int32)
    earlier = role_ids[None, :] < role_ids[:, None]
    role_starts = jnp.sum(jnp.where(earlier[:, :, None], counts[None], 0), axis=1, dtype=jnp.int32)

    def hits(first, number, target):
        return (first + number - 1 - target) // dp_count - (first - 1 - target) // dp_count

    def own(values):
        return lax.dynamic_index_in_dim(values, dp_pos, values.ndim - 1, keepdims=False)

    slot = jnp.arange(capacity, dtype=jnp.int32)
    slot_place = jnp.full((capacity,), -1, jnp.int32)
    own_counts, own_starts, own_role_starts = own(counts), own(starts), own(role_starts)
    for role in range(roles):
        inside = (slot >= own_role_starts[role]) & (
            slot < own_role_starts[role] + own_counts[role]
        )
        rank = slot - own_role_starts[role]
        target = (own_starts[role] + rank) % dp_count
        place = rank // dp_count
        for other in range(role):
            place = place + hits(own_starts[other], own_counts[other], target)
        slot_place = jnp.where(
            inside, ((target - dp_pos) % dp_count) * pair_rows + place, slot_place
        )
    local_sizes = [-(-size // dp_count // 16) * 16 for size in sizes]
    local_starts = [sum(local_sizes[:role]) for role in range(roles)]
    source_dp = (dp_pos - dps) % dp_count
    sent_counts, sent_starts = counts[:, source_dp], starts[:, source_dp]
    pair_place = jnp.arange(pair_rows, dtype=jnp.int32)[None, :]
    spread_place = jnp.full((dp_count, pair_rows), -1, jnp.int32)
    passed = jnp.zeros((dp_count, 1), jnp.int32)
    for role in range(roles):
        number = hits(sent_starts[role], sent_counts[role], dp_pos)[:, None]
        first = sent_starts[role] + (dp_pos - sent_starts[role]) % dp_count
        rank = pair_place - passed
        local = local_starts[role] + first[:, None] // dp_count + rank
        spread_place = jnp.where((rank >= 0) & (rank < number), local, spread_place)
        passed = passed + number
    spread_place = spread_place.reshape(-1)
    below = jnp.cumsum(owner_hot, axis=0) - 1
    row_target = []
    row_rank = []
    for role, (low, high) in enumerate(zip(ends[:-1], ends[1:])):
        number = jnp.sum(
            owner_hot[low:high] * (below[low:high] - role_starts[role] + starts[role]), axis=1
        )
        row_target.append(number % dp_count)
        row_rank.append(number // dp_count)

    def swap(values, axis, bit):
        count = lax.axis_size(axis)
        return lax.ppermute(values, axis, [(i, i ^ bit) for i in range(count)])

    orders = [
        ((dp_pos - row_target[role]) % dp_count) * local_sizes[role] + row_rank[role]
        for role in range(roles)
    ]

    gain_one, gain_two, adapter, table = unpack(small_params)
    bucket_onehot = (buckets[:, None] == jnp.arange(NB, dtype=jnp.int32)[None, :]).astype(
        jnp.float32
    )
    per_offset = lax.dot_general(
        table, bucket_onehot, (((0,), (1,)), ((), ())), precision=highest
    )
    bias_rows = jnp.concatenate([jnp.zeros((H, 1), jnp.float32), per_offset[:, ::-1]], axis=1)
    group_order = jnp.arange(tensor_count, dtype=jnp.int32) ^ tensor_pos
    bias_rows = bias_rows.reshape(tensor_count, group_heads, 2 * SEQ)[group_order]
    bias_rows = bias_rows.reshape(H, 1, 2 * SEQ)
    segments = lax.dynamic_slice_in_dim(segment_ids, tensor_pos * SEQ, SEQ, 0)

    inputs_f = tokens.astype(jnp.float32)
    normed_one = rms_norm(inputs_f, gain_one).astype(jnp.bfloat16)
    groups = range(tensor_count)
    w_qkv, w_out, w_in, w_down, projected, attended, scale, exp_scores = front(
        master[0].astype(jnp.bfloat16),
        slot_place,
        spread_place,
        orders,
        local_sizes,
        pair_rows,
        normed_one,
        bias_rows,
        segments,
    )
    attended = attended.reshape(tensor_count, head_rows, SEQ)
    mid = inputs_f
    for k in groups:
        mid = mid + contract(attended[k], w_out[k], 0, 0)
    normed_two = rms_norm(mid, gain_two).astype(jnp.bfloat16)
    activ, slope = [], []
    ffn_out = jnp.zeros(mid.shape, jnp.float32)
    for k in groups:
        part, part_slope, ffn_out = feed(normed_two, w_in[k], w_down[k], ffn_out)
        activ.append(part)
        slope.append(part_slope)
    final, adapter_pull = jax.vjp(adapter_apply, ffn_out, adapter)
    layer_out = (mid + final).astype(jnp.bfloat16)

    out_grad = cotangent.astype(jnp.float32)
    ffn_grad, adapter_grad = adapter_pull(out_grad)
    ffn_grad = ffn_grad.astype(jnp.bfloat16)

    def low_add(left, right):
        return (left.astype(jnp.float32) + right.astype(jnp.float32)).astype(jnp.bfloat16)

    def to_own(parts):
        total = low_add(parts[0], swap(parts[1], "tensor", 1))
        for bit in range(2, tensor_count, 2):
            pair = low_add(parts[bit], swap(parts[bit + 1], "tensor", 1))
            total = low_add(total, swap(pair, "tensor", bit))
        return total

    def to_spread(role, parts):
        total = to_own(parts)
        place = row_target[role] * local_sizes[role] + row_rank[role]
        total = select_rows([total], dp_count * local_sizes[role], target=place)
        total = lax.all_to_all(
            total.reshape(dp_count, local_sizes[role], D),
            "dp",
            split_axis=0,
            concat_axis=0,
            tiled=True,
        )
        return jnp.sum(total.astype(jnp.float32), axis=0).astype(jnp.bfloat16)

    back = list(groups)[::-1]
    normed_two_grad = jnp.zeros(mid.shape, jnp.float32)
    down_grad, in_grad = [None] * tensor_count, [None] * tensor_count
    for k in back:
        pre_grad = (contract(ffn_grad, w_down[k], 1, 1) * slope[k].astype(jnp.float32)).astype(
            jnp.bfloat16
        )
        down_grad[k] = contract(activ[k], ffn_grad, 0, 0).astype(jnp.bfloat16)
        in_grad[k] = contract(pre_grad, normed_two, 0, 0).astype(jnp.bfloat16)
        normed_two_grad = normed_two_grad + jnp.dot(
            pre_grad, w_in[k], preferred_element_type=jnp.float32
        )
    down_grad = to_spread(3, down_grad)
    in_grad = to_spread(2, in_grad)
    _, norm_two_pull = jax.vjp(rms_norm, mid, gain_two)
    mid_extra, gain_two_grad = norm_two_pull(normed_two_grad)
    mid_grad = out_grad + mid_extra
    mid_grad_low = mid_grad.astype(jnp.bfloat16)
    out_weight_grad = to_spread(
        1,
        [
            jnp.dot(attended[k], mid_grad_low, preferred_element_type=jnp.float32).astype(
                jnp.bfloat16
            )
            for k in groups
        ],
    )
    normed_one_grad = jnp.zeros(mid.shape, jnp.float32)
    qkv_grad, offset_grad = [None] * tensor_count, [None] * tensor_count
    for k in back:
        attended_grad = contract(w_out[k], mid_grad_low, 1, 1).astype(jnp.bfloat16)
        proj_grad, offset_grad[k] = attend_back(
            k, projected, exp_scores, attended, scale, attended_grad
        )
        proj_grad = proj_grad.reshape(3 * head_rows, SEQ)
        qkv_grad[k] = jnp.dot(proj_grad, normed_one, preferred_element_type=jnp.float32).astype(
            jnp.bfloat16
        )
        normed_one_grad = normed_one_grad + contract(proj_grad, w_qkv[k], 0, 0)
    qkv_grad = to_spread(0, qkv_grad)
    _, norm_one_pull = jax.vjp(rms_norm, inputs_f, gain_one)
    input_extra, gain_one_grad = norm_one_pull(normed_one_grad)
    input_grad = (mid_grad + input_extra).astype(jnp.bfloat16)
    offset_all = jnp.stack(offset_grad)
    offset_all = offset_all[group_order].reshape(H, 2 * SEQ)
    table_grad = jnp.dot(bucket_onehot.T, offset_all[:, 1:][:, ::-1].T, precision=highest)
    small_total = jnp.concatenate(
        [gain_one_grad, gain_two_grad]
        + [piece.reshape(-1) for piece in adapter_grad]
        + [table_grad.reshape(-1)]
    )
    for axis, count in (("tensor", tensor_count), ("dp", dp_count)):
        bit = 1
        while bit < count:
            small_total = small_total + swap(small_total, axis, bit)
            bit *= 2

    bank_grad = jnp.concatenate([qkv_grad, out_weight_grad, in_grad, down_grad], axis=0)
    sent = select_rows(
        [bank_grad],
        dp_count * pair_rows,
        source=spread_place.reshape(dp_count, pair_rows)[source_dp].reshape(-1),
    )
    received = lax.all_to_all(
        sent.reshape(dp_count, pair_rows, D), "dp", split_axis=0, concat_axis=0, tiled=True
    )
    back_place = jnp.where(
        slot_place >= 0,
        (slot_place // pair_rows + dp_pos) % dp_count * pair_rows + slot_place % pair_rows,
        -1,
    )
    owned_grad = select_rows(
        [received.reshape(-1, D)], capacity, source=back_place, dtype=jnp.float32
    )
    own_filled = (slot_place >= 0).astype(jnp.float32)[:, None]
    step = step_count[0].astype(jnp.float32)
    new_master, new_first, new_second = adamw(
        master[0], owned_grad, first_moment[0], second_moment[0], step
    )
    new_master = new_master * own_filled
    new_first = new_first * own_filled
    new_second = new_second * own_filled
    small_new, small_first_new, small_second_new = adamw(
        small_params, small_total, small_first, small_second, step
    )
    ema_new = average_keep * adapter_ema + (1.0 - average_keep) * small_new[2 * D : 2 * D + NADAPT]
    return (
        layer_out,
        input_grad,
        owned_grad[None],
        new_first[None],
        new_second[None],
        new_master[None],
        new_master.astype(jnp.bfloat16)[None],
        small_total,
        small_first_new,
        small_second_new,
        small_new,
        ema_new,
    )


def solution(mesh):
    token_spec = P(("dp", "tensor"), None)
    owner_spec = P("tensor", "dp", None)
    return jax.shard_map(
        per_device,
        mesh=mesh,
        in_specs=(token_spec, token_spec, P("dp"), P(), P())
        + (owner_spec,) * 3
        + (P(),) * 5,
        out_specs=(token_spec,) * 2 + (owner_spec,) * 5 + (P(),) * 5,
        check_vma=False,
    )
```

time: 674 us -> 574 us (0.85)
  waiting for transfers between devices: 335 us -> 32.9 us
  Pallas kernels: 90.7 us -> 254 us
  starting transfers between devices: 0.88 us -> 57.9 us
  blocking collectives: 42.1 us -> 0 us
  other arithmetic: 31.7 us -> 59 us
  local copies, waits for them, and re-layouts: 51.9 us -> 35.7 us
  matrix products: 98.7 us -> 114 us
    pallas_call x3 -> x15, Pallas kernels: 90.7 us -> 254 us  [the longest x1 153 us: front(): pl.pallas_call(functools.partial(front_kernel, sizes), in_specs=[whole] *...]
    all_gather x5 -> x0, waiting for transfers between devices: 159 us -> none  [the longest x1 110 us: per_device(): lax.all_gather(master[0].astype(jnp.bfloat16), 'dp', axis=0, tiled=True)]
    reduce_scatter x4 -> x0, waiting for transfers between devices: 104 us -> none  [reduce_rows(): lax.psum_scatter(part.astype(jnp.bfloat16), 'tensor', scatter_dimension=0...]
    psum x1 -> x0, waiting for transfers between devices: 71.8 us -> none  [reduce_rows(): return lax.psum(part, 'dp')]
    all_to_all x0 -> x5, starting transfers between devices: none -> 43.6 us  [the longest x4 39.4 us: to_spread(): lax.all_to_all(total.reshape(dp_count, local_sizes[role], D), 'dp', split...]
    psum x1 -> x0, blocking collectives: 42.1 us -> none  [per_device(): small_total = lax.psum(small_local, ('dp', 'tensor'))]
    gather x5 -> x7, local copies, waits for them, and re-layouts: 30.8 us -> 3.33 us  [the longest x2 1.11 us: per_device(): sent_counts, sent_starts = (counts[:, source_dp], starts[:, source_dp])]
    ppermute x0 -> x17, waiting for transfers between devices: none -> 23.8 us  [swap(): return lax.ppermute(values, axis, [(i, i ^ bit) for i in range(count)])]
  transfers between devices with their start and end apart: 10 -> 22, of which waited for: 7 -> 5; matrix products, arithmetic and copies ran while one was open for 19% -> 21% of each run, Pallas kernels for 11% -> 10%
where the time goes in v2:
time: 574 us; the launch traced here: 568 us
  Pallas kernels  254 us (44%)
  matrix products  114 us (20%)
  other arithmetic  59 us (10%)
  starting transfers between devices  57.9 us (10%)
  local copies, waits for them, and re-layouts  35.7 us (6%)
  waiting for transfers between devices  32.9 us (6%)
  between operations  14 us (2%)
    pallas_call x1, Pallas kernels, front(): pl.pallas_call(functools.partial(front_kernel, sizes), in_specs=[whole] *...  153 us
    dot_general x24, matrix products, contract(): lax.dot_general(left, right, (((left_dim,), (right_dim,)), ((), ())), pre...  61.4 us
    pallas_call x4, Pallas kernels, attend_back(): pl.pallas_call(attend_back_kernel, grid=(heads,), in_specs=[pl.BlockSpec(...  45.2 us
    pallas_call x4, Pallas kernels, feed(): pl.pallas_call(feed_kernel, grid=(hidden // width,), in_specs=[pl.BlockSp...  45.1 us
    all_to_all x4, starting transfers between devices, to_spread(): lax.all_to_all(total.reshape(dp_count, local_sizes[role], D), 'dp', split...  39.4 us
    ppermute x17, waiting for transfers between devices, swap(): return lax.ppermute(values, axis, [(i, i ^ bit) for i in range(count)])  23.8 us
    ppermute x17, starting transfers between devices, swap(): return lax.ppermute(values, axis, [(i, i ^ bit) for i in range(count)])  14.3 us
  transfers between devices with their start and end apart: 22, of which 5 were waited for; matrix products, arithmetic and copies ran while one was open for 21% of the time, Pallas kernels for 10%

profile of v2, /device:TPU:0, one launch (start us, length us, event | category | flops | bytes accessed | tf_op | source)
XLA Modules:
  0.0 567.7 jit_solution(10936188305329773431)
XLA Ops:
  6.0 1.8 fusion.7
  21.9 2.3 reduce-window.6
  30.9 2.6 bitcast_convert_fusion.mine_ref
  35.7 2.0 fusion.49
  39.2 5.9 %and_select_fusion.33.slot_place_ref = s32[1,576]{1,0:T(1,128)} fusion(s32[]{:T(128)} %bitcast.8, s32[]{:T(128)S(6)} %add.1847, s32[]{:T(128)} %bitcast.16, s32[]{:T(128)} %bitcast.10, s32[]{:T(128)S(6)} %add.1840, s32[]{:T(128)} %bitcast.15, s32[]{:T(128)} %bitcast.12, s32[]{:T(128)S(6)} %add.1832, s32[]{:T(128)} %bitcast.14, s32[]{:T(128)S(6)} %sub.1325, ...), kind=kLoop, calls=%fused_computation.552 | loop fusion | flops 223488 | bytes 2380 | tf_op jit(solution)/shard_map/jit(_where)/select_n | solution.py:699
  46.1 152.8 %front.1 = (bf16[4,576,768]{2,1,0:T(8,128)(2,1)}, bf16[4,192,768]{2,1,0:T(8,128)(2,1)}, bf16[4,768,768]{2,1,0:T(8,128)(2,1)}, bf16[4,768,768]{2,1,0:T(8,128)(2,1...) custom-call(bf16[576,768]{1,0:T(8,128)(2,1)} %bitcast_convert_fusion, ...), custom_call_target="tpu_custom_call" | custom-call | flops 32212254720 | bytes 67108864 | tf_op jit(solution)/shard_map/front/pallas_call | solution.py:385
  198.9 3.5 fusion.63
  202.4 2.4 fusion.68
  204.8 2.4 fusion.71
  210.2 4.8 multiply_reduce_fusion.2
  215.0 3.8 slice_bitcast_fusion.1
  218.8 2.6 slice_bitcast_fusion
  222.9 2.0 broadcast_in_dim.68.before_ref
  224.9 9.0 %feed.4 = (bf16[1024,768]{1,0:T(8,128)(2,1)S(1)}, bf16[1024,768]{1,0:T(8,128)(2,1)S(1)}, f32[1024,768]{1,0:T(8,128)}) custom-call(bf16[1024,768]{1,0:T(8,128)(2,1)} %multiply_convert_fusion.4.rows_ref, bf16[768,768]{1,0:T(8,128)(2,1)S(1)} %get-tuple-element.99.w_in_ref, bf16[768,768]{1,0:T(8,128)(2,1)S(1)} %get-tuple-element.95.w_down_ref, ...), custom_call_target="tpu_custom_call" | custom-call | flops 4831838208 | bytes 10485760 | tf_op jit(solution)/shard_map/feed/pallas_call | solution.py:567
  235.0 9.0 %feed.5 = (bf16[1024,768]{1,0:T(8,128)(2,1)S(1)}, bf16[1024,768]{1,0:T(8,128)(2,1)S(1)}, f32[1024,768]{1,0:T(8,128)}) custom-call(bf16[1024,768]{1,0:T(8,128)(2,1)} %multiply_convert_fusion.4.rows_ref, bf16[768,768]{1,0:T(8,128)(2,1)S(1)} %get-tuple-element.100.w_in_ref, bf16[768,768]{1,0:T(8,128)(2,1)S(1)} %get-tuple-element.96.w_down_ref, ...), custom_call_target="tpu_custom_call" | custom-call | flops 4831838208 | bytes 10485760 | tf_op jit(solution)/shard_map/feed/pallas_call | solution.py:567
  245.2 9.5 %feed.6 = (bf16[1024,768]{1,0:T(8,128)(2,1)S(1)}, bf16[1024,768]{1,0:T(8,128)(2,1)S(1)}, f32[1024,768]{1,0:T(8,128)}) custom-call(bf16[1024,768]{1,0:T(8,128)(2,1)} %multiply_convert_fusion.4.rows_ref, bf16[768,768]{1,0:T(8,128)(2,1)S(1)} %get-tuple-element.101.w_in_ref, bf16[768,768]{1,0:T(8,128)(2,1)S(1)} %get-tuple-element.97.w_down_ref, ...), custom_call_target="tpu_custom_call" | custom-call | flops 4831838208 | bytes 10485760 | tf_op jit(solution)/shard_map/feed/pallas_call | solution.py:567
  255.9 17.5 %feed.7 = (bf16[1024,768]{1,0:T(8,128)(2,1)S(1)}, bf16[1024,768]{1,0:T(8,128)(2,1)S(1)}, f32[1024,768]{1,0:T(8,128)}) custom-call(bf16[1024,768]{1,0:T(8,128)(2,1)} %multiply_convert_fusion.4.rows_ref, bf16[768,768]{1,0:T(8,128)(2,1)S(1)} %get-tuple-element.102.w_in_ref, bf16[768,768]{1,0:T(8,128)(2,1)S(1)} %get-tuple-element.98.w_down_ref, ...), custom_call_target="tpu_custom_call" | custom-call | flops 4831838208 | bytes 10485760 | tf_op jit(solution)/shard_map/feed/pallas_call | solution.py:567
  273.5 5.6 fusion.397
  280.8 2.7 fusion.4
  285.5 2.5 convolution_convert_fusion.6
  289.8 2.5 convolution_convert_fusion.4
  300.9 2.7 multiply_reduce_fusion
  310.0 11.5 %attend_back.4 = (bf16[3,3,64,1024]{3,2,1,0:T(8,128)(2,1)S(1)}, f32[3,1,2048]{2,1,0:T(1,128)S(1)}) custom-call(bf16[4,576,1024]{2,1,0:T(8,128)(2,1)} %get-tuple-element.52.query_ref.key_ref.value_ref, bf16[4,576,1024]{2,1,0:T(8,128)(2,1)} %get-tuple-element.52.query_ref.key_ref.value_ref, ...), custom_call_target="tpu_custom_call" | custom-call | flops 9663676416 | bytes 9437184 | tf_op jit(solution)/shard_map/attend_back/pallas_call | solution.py:511
  321.6 2.0 convolution_convert_fusion.8
  324.2 2.8 fusion.205
  327.0 2.1 fusion.398
  336.0 4.5 convolution_convert_fusion
  340.6 2.5 convolution_convert_fusion.2
  343.1 11.0 %attend_back.5 = (bf16[3,3,64,1024]{3,2,1,0:T(8,128)(2,1)S(1)}, f32[3,1,2048]{2,1,0:T(1,128)S(1)}) custom-call(bf16[4,576,1024]{2,1,0:T(8,128)(2,1)} %get-tuple-element.52.query_ref.key_ref.value_ref, bf16[4,576,1024]{2,1,0:T(8,128)(2,1)} %get-tuple-element.52.query_ref.key_ref.value_ref, ...), custom_call_target="tpu_custom_call" | custom-call | flops 9663676416 | bytes 9437184 | tf_op jit(solution)/shard_map/attend_back/pallas_call | solution.py:511
  354.1 11.3 %attend_back.6 = (bf16[3,3,64,1024]{3,2,1,0:T(8,128)(2,1)S(1)}, f32[3,1,2048]{2,1,0:T(1,128)S(1)}) custom-call(bf16[4,576,1024]{2,1,0:T(8,128)(2,1)} %get-tuple-element.52.query_ref.key_ref.value_ref, bf16[4,576,1024]{2,1,0:T(8,128)(2,1)} %get-tuple-element.52.query_ref.key_ref.value_ref, ...), custom_call_target="tpu_custom_call" | custom-call | flops 9663676416 | bytes 9437184 | tf_op jit(solution)/shard_map/attend_back/pallas_call | solution.py:511
  365.5 11.3 %attend_back.7 = (bf16[3,3,64,1024]{3,2,1,0:T(8,128)(2,1)S(1)}, f32[3,1,2048]{2,1,0:T(1,128)S(1)}) custom-call(bf16[4,576,1024]{2,1,0:T(8,128)(2,1)} %get-tuple-element.52.query_ref.key_ref.value_ref, bf16[4,576,1024]{2,1,0:T(8,128)(2,1)} %get-tuple-element.52.query_ref.key_ref.value_ref, ...), custom_call_target="tpu_custom_call" | custom-call | flops 9663676416 | bytes 9437184 | tf_op jit(solution)/shard_map/attend_back/pallas_call | solution.py:511
  376.8 2.0 convolution_convert_fusion.10
  383.2 3.2 add_convert_fusion.8
  386.4 5.3 collective-permute-done.5
  393.3 15.3 %all-to-all-start.1 = ((bf16[8,32,768]{2,1,0:T(8,128)(2,1)}), bf16[8,32,768]{2,1,0:T(8,128)(2,1)S(1)}, u32[]{:S(2)}, u32[]{:S(2)}) async-start(bf16[8,32,768]{2,1,0:T(8,128)(2,1)} %bitcast.62), calls=%async_computation.1 | async-start | bytes 786432 | tf_op jit(solution)/shard_map/all_to_all | solution.py:795
  408.7 2.4 add_convert_fusion.9
  411.1 3.7 add_convert_fusion.5
  417.8 1.9 select_rows.6
  420.4 13.4 %all-to-all-start = ((bf16[8,80,768]{2,1,0:T(8,128)(2,1)}), bf16[8,80,768]{2,1,0:T(8,128)(2,1)}, u32[]{:S(2)}, u32[]{:S(2)}) async-start(bf16[8,80,768]{2,1,0:T(8,128)(2,1)} %bitcast.60), calls=%async_computation | async-start | bytes 1966080 | tf_op jit(solution)/shard_map/all_to_all | solution.py:795
  441.3 3.2 add_convert_fusion.6
  446.1 2.1 select_rows.8
  448.2 7.1 %all-to-all-done = bf16[8,80,768]{2,1,0:T(8,128)(2,1)} async-done(((bf16[8,80,768]{2,1,0:T(8,128)(2,1)}), bf16[8,80,768]{2,1,0:T(8,128)(2,1)}, u32[]{:S(2)}, u32[]{:S(2)}) %all-to-all-start) | async-done | bytes 983072 | tf_op jit(solution)/shard_map/all_to_all | solution.py:795
  455.3 4.7 all-to-all-start.2
  460.0 3.3 add_convert_fusion.2
  464.0 3.1 fusion.22
  467.1 3.1 fusion.24
  470.3 2.7 add_convert_fusion.3
  473.0 15.9 %collective-permute-done.11 = bf16[768,768]{1,0:T(8,128)(2,1)S(1)} collective-permute-done((bf16[768,768]{1,0:T(8,128)(2,1)S(1)}, bf16[768,768]{1,0:T(8,128)(2,1)S(1)}, u32[]{:S(2)}, u32[]{:S(2)}) %collective-permute-start.11) | collective-permute-done | bytes 1179680 | tf_op jit(solution)/shard_map/ppermute | solution.py:729
  489.2 2.1 select_rows.9
  491.3 6.1 %all-to-all-start.3 = ((bf16[8,96,768]{2,1,0:T(8,128)(2,1)}), bf16[8,96,768]{2,1,0:T(8,128)(2,1)}, u32[]{:S(2)}, u32[]{:S(2)}) async-start(bf16[8,96,768]{2,1,0:T(8,128)(2,1)} %bitcast.64), calls=%async_computation.3 | async-start | bytes 2359296 | tf_op jit(solution)/shard_map/all_to_all | solution.py:795
  498.4 2.8 fusion.20
  502.0 5.0 fusion.3
  507.1 9.4 %fusion.136.place_ref = s32[576,1]{1,0:T(8,128)S(1)} fusion(s32[]{:T(128)} %bitcast.8, s32[]{:T(128)S(6)} %add.1847, s32[]{:T(128)} %bitcast.16, s32[]{:T(128)} %bitcast.10, s32[]{:T(128)S(6)} %add.1840, s32[]{:T(128)} %bitcast.15, s32[]{:T(128)} %bitcast.12, s32[]{:T(128)S(6)} %add.1832, s32[]{:T(128)} %bitcast.14, s32[]{:T(128)S(6)} %sub.1325, ...), kind=kLoop, calls=%fused_computation.337 | loop fusion | flops 239616 | bytes 2380 | tf_op jit(solution)/shard_map/jit(_where)/select_n | solution.py:870
  520.8 2.0 all-to-all-done.3
  526.0 4.2 all-to-all-start.4
  530.3 2.1 collective-permute-start.14
  532.5 6.1 %fusion.6 = bf16[1024,768]{1,0:T(8,128)(2,1)} fusion(bf16[1024,768]{1,0:T(8,128)(2,1)S(1)} %copy-done.25, f32[1024,768]{1,0:T(8,128)} %get-tuple-element.139, f32[1024]{0:T(1024)S(1)} %multiply_multiply_fusion.10, f32[768]{0:T(1024)S(1)} %copy-done.64, f32[1024]{0:T(1024)S(1)} %copy-done.62, f32[1024,768]{1,0:T(8,128)} %copy-done.20, ...), kind=kLoop, calls=%fused_computation.20 | loop fusion | flops 11796480 | bytes 14178304 | tf_op jit(solution)/shard_map/convert_element_type | solution.py:846
  538.6 2.3 collective-permute-start.15
  540.9 4.2 add_convert_fusion
  545.1 2.5 collective-permute-done.15
  547.6 4.0 collective-permute-start.16
  551.6 5.1 fusion.331
  558.6 2.1 select_rows.11
  560.7 6.7 %convert_bitcast_fusion = (bf16[1,576,768]{2,1,0:T(8,128)(2,1)}, f32[576,768]{1,0:T(8,128)}, f32[1,576,768]{2,1,0:T(8,128)}, f32[1,576,768]{2,1,0:T(8,128)}) fusion(f32[576]{0:T(1024)S(1)} %fusion.331, f32[576,768]{1,0:T(8,128)} %select_rows.11, f32[1,576,768]{2,1,0:T(8,128)} %param.20, f32[]{:T(128)} %bitcast.73, f32[1,576,768]{2,1,0:T(8,128)} %param.19, ...), kind=kLoop, calls=%fused_computation.112 | loop fusion | flops 7962624 | bytes 13273352 | tf_op jit(solution)/shard_map/broadcast_in_dim | solution.py:897
  (385 shorter events, 85.6 us)
Async XLA Ops:
  0.6 21.2 %copy-start.65 = (s32[2304]{0:T(1024)S(1)}, s32[2304]{0:T(1024)}, u32[]{:S(2)}) copy-start(s32[2304]{0:T(1024)} %param.17) | copy-start | bytes 27652
  2.2 204.9 %copy-start.93 = (f32[48]{0:T(128)}, f32[48]{0:T(128)S(1)}, u32[]{:S(2)}) copy-start(f32[48]{0:T(128)S(1)} %get-tuple-element.109) | copy-start | bytes 580
  3.8 33.8 %copy-start.63 = (f32[768]{0:T(1024)}, f32[768]{0:T(1024)S(1)}, u32[]{:S(2)}) copy-start(f32[768]{0:T(1024)S(1)} %get-tuple-element.107) | copy-start | bytes 9220
  3.8 299.8 %copy-start.58 = (f32[768]{0:T(1024)}, f32[768]{0:T(1024)S(1)}, u32[]{:S(2)}) copy-start(f32[768]{0:T(1024)S(1)} %get-tuple-element.106) | copy-start | bytes 9220
  4.5 21.2 %copy-start.97 = (s32[2047]{0:T(1024)S(1)}, s32[2047]{0:T(1024)}, u32[]{:S(2)}) copy-start(s32[2047]{0:T(1024)} %param.16) | copy-start | bytes 24568
  6.0 20.8 %copy-start.91 = (s32[1024]{0:T(1024)}, s32[1024]{0:T(1024)S(1)}, u32[]{:S(2)}) copy-start(s32[1024]{0:T(1024)S(1)} %pad_clamp_fusion.1) | copy-start | bytes 12292
  6.0 22.1 %copy-start.92 = (s32[1024]{0:T(1024)}, s32[1024]{0:T(1024)S(1)}, u32[]{:S(2)}) copy-start(s32[1024]{0:T(1024)S(1)} %pad_clamp_fusion) | copy-start | bytes 12292
  7.8 29.9 %copy-start.61 = (f32[1024]{0:T(1024)}, f32[1024]{0:T(1024)S(1)}, u32[]{:S(2)}) copy-start(f32[1024]{0:T(1024)S(1)} %fusion.332) | copy-start | bytes 12292
  24.9 8.7 %copy-start.86 = (s32[192]{0:T(256)}, s32[192]{0:T(256)S(1)}, u32[]{:S(2)}) copy-start(s32[192]{0:T(256)S(1)} %fusion.240) | copy-start | bytes 2308
  34.2 10.9 %copy-start.82 = (s32[1024]{0:T(1024)}, s32[1024]{0:T(1024)S(1)}, u32[]{:S(2)}) copy-start(s32[1024]{0:T(1024)S(1)} %dynamic_slice.16) | copy-start | bytes 12292
  215.0 88.6 %copy-start.56 = (f32[1024]{0:T(1024)}, f32[1024]{0:T(1024)S(1)}, u32[]{:S(2)}) copy-start(f32[1024]{0:T(1024)S(1)} %fusion.333) | copy-start | bytes 12292
  245.2 9.5 %copy-start.8 = (bf16[1024,768]{1,0:T(8,128)(2,1)}, bf16[1024,768]{1,0:T(8,128)(2,1)S(1)}, u32[]{:S(2)}) copy-start(bf16[1024,768]{1,0:T(8,128)(2,1)S(1)} %get-tuple-element.50) | copy-start | bytes 4718596
  255.9 23.2 %copy-start.51 = (f32[48,768]{1,0:T(8,128)S(1)}, f32[48,768]{1,0:T(8,128)}, u32[]{:S(2)}) copy-start(f32[48,768]{1,0:T(8,128)} %reshape.4218) | copy-start | bytes 442372
  273.5 10.0 %slice-start.2 = ((s8[4718592]{0:T(1024)(128)(4,1)}), s8[4194304]{0:T(1024)(128)(4,1)S(1)}, s32[]{:S(2)}) async-start(s8[4718592]{0:T(1024)(128)(4,1)} %bitcast.309), calls=%async_computation.7 | async-start | bytes 8388608
  279.1 45.0 %copy-start.49 = (f32[1024,48]{0,1:T(8,128)}, f32[1024,48]{0,1:T(8,128)S(1)}, u32[]{:S(2)}) copy-start(f32[1024,48]{0,1:T(8,128)S(1)} %fusion.397) | copy-start | bytes 589828
  283.5 13.5 %copy-start.37 = (bf16[1024,768]{1,0:T(8,128)(2,1)}, bf16[1024,768]{1,0:T(8,128)(2,1)S(1)}, u32[]{:S(2)}) copy-start(bf16[1024,768]{1,0:T(8,128)(2,1)S(1)} %fusion.4) | copy-start | bytes 4718596
  288.0 153.3 %collective-permute-start.6 = (bf16[768,768]{1,0:T(8,128)(2,1)}, bf16[768,768]{1,0:T(8,128)(2,1)}, u32[]{:S(2)}, u32[]{:S(2)}) collective-permute-start(bf16[768,768]{1,0:T(8,128)(2,1)} %convolution_convert_fusion.6), channel_id=1, source_target_pairs={{0,1},{1,0},{2,3},{3,2},{4,5},{5,4},{6,7},{7,6},{8,9},{9,8},{10,11... | collective-permute-start | bytes 3538952 | tf_op jit(solution)/shard_map/ppermute | solution.py:729
  292.4 118.7 %collective-permute-start.7 = (bf16[768,768]{1,0:T(8,128)(2,1)}, bf16[768,768]{1,0:T(8,128)(2,1)}, u32[]{:S(2)}, u32[]{:S(2)}) collective-permute-start(bf16[768,768]{1,0:T(8,128)(2,1)} %convolution_convert_fusion.4), channel_id=1, source_target_pairs={{0,1},{1,0},{2,3},{3,2},{4,5},{5,4},{6,7},{7,6},{8,9},{9,8},{10,11... | collective-permute-start | bytes 3538952 | tf_op jit(solution)/shard_map/ppermute | solution.py:729
  306.6 72.4 %collective-permute-start.3 = (bf16[192,768]{1,0:T(8,128)(2,1)}, bf16[192,768]{1,0:T(8,128)(2,1)}, u32[]{:S(2)}, u32[]{:S(2)}) collective-permute-start(bf16[192,768]{1,0:T(8,128)(2,1)} %convolution_convert_fusion.18), channel_id=1, source_target_pairs={{0,1},{1,0},{2,3},{3,2},{4,5},{5,4},{6,7},{7,6},{8,9},{9,8},{10,11... | collective-permute-start | bytes 884744 | tf_op jit(solution)/shard_map/ppermute | solution.py:729
  308.2 72.4 %collective-permute-start.4 = (bf16[192,768]{1,0:T(8,128)(2,1)}, bf16[192,768]{1,0:T(8,128)(2,1)}, u32[]{:S(2)}, u32[]{:S(2)}) collective-permute-start(bf16[192,768]{1,0:T(8,128)(2,1)} %convolution_convert_fusion.16), channel_id=1, source_target_pairs={{0,1},{1,0},{2,3},{3,2},{4,5},{5,4},{6,7},{7,6},{8,9},{9,8},{10,11... | collective-permute-start | bytes 884744 | tf_op jit(solution)/shard_map/ppermute | solution.py:729
  310.0 11.6 %copy-start.40 = (bf16[1024,768]{1,0:T(8,128)(2,1)S(1)}, bf16[1024,768]{1,0:T(8,128)(2,1)}, u32[]{:S(2)}) copy-start(bf16[1024,768]{1,0:T(8,128)(2,1)} %fusion.2.normed_ref) | copy-start | bytes 4718596
  323.6 59.0 %collective-permute-start.1 = (bf16[576,768]{1,0:T(8,128)(2,1)}, bf16[576,768]{1,0:T(8,128)(2,1)}, u32[]{:S(2)}, u32[]{:S(2)}) collective-permute-start(bf16[576,768]{1,0:T(8,128)(2,1)} %convolution_convert_fusion.8), channel_id=1, source_target_pairs={{0,1},{1,0},{2,3},{3,2},{4,5},{5,4},{6,7},{7,6},{8,9},{9,8},{10,11... | collective-permute-start | bytes 2654216 | tf_op jit(solution)/shard_map/ppermute | solution.py:729
  324.1 8.2 %copy-start.89 = (f32[4,4,4,1]{2,1,0,3:T(4,128)}, f32[4,4,4,1]{2,1,0,3:T(4,128)S(1)}, u32[]{:S(2)}) copy-start(f32[4,4,4,1]{2,1,0,3:T(4,128)S(1)} %reshape.4291) | copy-start | bytes 772
  331.3 9.2 %copy-start.35 = (f32[4,12,4,192]{3,2,1,0:T(4,128)}, f32[4,12,4,192]{3,2,1,0:T(4,128)S(1)}, u32[]{:S(2)}) copy-start(f32[4,12,4,192]{3,2,1,0:T(4,128)S(1)} %reshape.4230) | copy-start | bytes 442372
  354.1 29.0 %copy-start.6 = (bf16[3,3,64,1024]{3,2,1,0:T(8,128)(2,1)}, bf16[3,3,64,1024]{3,2,1,0:T(8,128)(2,1)S(1)}, u32[]{:S(2)}) copy-start(bf16[3,3,64,1024]{3,2,1,0:T(8,128)(2,1)S(1)} %get-tuple-element.57) | copy-start | bytes 3538948
  365.4 11.3 %copy-start.2 = (bf16[3,3,64,1024]{3,2,1,0:T(8,128)(2,1)}, bf16[3,3,64,1024]{3,2,1,0:T(8,128)(2,1)S(1)}, u32[]{:S(2)}) copy-start(bf16[3,3,64,1024]{3,2,1,0:T(8,128)(2,1)S(1)} %get-tuple-element.58) | copy-start | bytes 3538948
  365.4 11.3 %copy-start.41 = (bf16[1024,768]{1,0:T(8,128)(2,1)S(1)}, bf16[1024,768]{1,0:T(8,128)(2,1)}, u32[]{:S(2)}) copy-start(bf16[1024,768]{1,0:T(8,128)(2,1)} %fusion.2.normed_ref) | copy-start | bytes 4718596
  379.0 91.3 %collective-permute-start.9 = (bf16[768,768]{1,0:T(8,128)(2,1)}, bf16[768,768]{1,0:T(8,128)(2,1)}, u32[]{:S(2)}, u32[]{:S(2)}) collective-permute-start(bf16[768,768]{1,0:T(8,128)(2,1)} %convolution_convert_fusion.2), channel_id=1, source_target_pairs={{0,1},{1,0},{2,3},{3,2},{4,5},{5,4},{6,7},{7,6},{8,9},{9,8},{10,11... | collective-permute-start | bytes 3538952 | tf_op jit(solution)/shard_map/ppermute | solution.py:729
  380.7 27.9 %collective-permute-start = (bf16[576,768]{1,0:T(8,128)(2,1)}, bf16[576,768]{1,0:T(8,128)(2,1)}, u32[]{:S(2)}, u32[]{:S(2)}) collective-permute-start(bf16[576,768]{1,0:T(8,128)(2,1)} %convolution_convert_fusion.10), channel_id=1, source_target_pairs={{0,1},{1,0},{2,3},{3,2},{4,5},{5,4},{6,7},{7,6},{8,9},{9,8},{10,11... | collective-permute-start | bytes 2654216 | tf_op jit(solution)/shard_map/ppermute | solution.py:729
  382.6 9.1 %collective-permute-start.5 = (bf16[192,768]{1,0:T(8,128)(2,1)S(1)}, bf16[192,768]{1,0:T(8,128)(2,1)S(1)}, u32[]{:S(2)}, u32[]{:S(2)}) collective-permute-start(bf16[192,768]{1,0:T(8,128)(2,1)S(1)} %add_convert_fusion.11), channel_id=1, source_target_pairs={{0,2},{1,3},{2,0},{3,1},{4,6},{5,7},{6,4},{7,5},{8,10},{9,11},{10,... | collective-permute-start | bytes 884744 | tf_op jit(solution)/shard_map/ppermute | solution.py:729
  386.4 22.3 %copy-start.42 = (bf16[1024,768]{1,0:T(8,128)(2,1)S(1)}, bf16[1024,768]{1,0:T(8,128)(2,1)}, u32[]{:S(2)}) copy-start(bf16[1024,768]{1,0:T(8,128)(2,1)} %fusion.2.normed_ref) | copy-start | bytes 4718596
  391.7 24.7 %collective-permute-start.2 = (bf16[576,768]{1,0:T(8,128)(2,1)}, bf16[576,768]{1,0:T(8,128)(2,1)}, u32[]{:S(2)}, u32[]{:S(2)}) collective-permute-start(bf16[576,768]{1,0:T(8,128)(2,1)} %add_convert_fusion.8), channel_id=1, source_target_pairs={{0,2},{1,3},{2,0},{3,1},{4,6},{5,7},{6,4},{7,5},{8,10},{9,11},{10,... | collective-permute-start | bytes 2654216 | tf_op jit(solution)/shard_map/ppermute | solution.py:729
  393.3 26.4 %all-to-all-start.1 = ((bf16[8,32,768]{2,1,0:T(8,128)(2,1)}), bf16[8,32,768]{2,1,0:T(8,128)(2,1)S(1)}, u32[]{:S(2)}, u32[]{:S(2)}) async-start(bf16[8,32,768]{2,1,0:T(8,128)(2,1)} %bitcast.62), calls=%async_computation.1 | async-start | bytes 786432 | tf_op jit(solution)/shard_map/all_to_all | solution.py:795
  408.6 51.4 %collective-permute-start.10 = (bf16[768,768]{1,0:T(8,128)(2,1)}, bf16[768,768]{1,0:T(8,128)(2,1)}, u32[]{:S(2)}, u32[]{:S(2)}) collective-permute-start(bf16[768,768]{1,0:T(8,128)(2,1)} %convolution_convert_fusion), channel_id=1, source_target_pairs={{0,1},{1,0},{2,3},{3,2},{4,5},{5,4},{6,7},{7,6},{8,9},{9,8},{10,11... | collective-permute-start | bytes 3538952 | tf_op jit(solution)/shard_map/ppermute | solution.py:729
  414.9 29.6 %collective-permute-start.8 = (bf16[768,768]{1,0:T(8,128)(2,1)}, bf16[768,768]{1,0:T(8,128)(2,1)}, u32[]{:S(2)}, u32[]{:S(2)}) collective-permute-start(bf16[768,768]{1,0:T(8,128)(2,1)} %add_convert_fusion.5), channel_id=1, source_target_pairs={{0,2},{1,3},{2,0},{3,1},{4,6},{5,7},{6,4},{7,5},{8,10},{9,11},{10,... | collective-permute-start | bytes 3538952 | tf_op jit(solution)/shard_map/ppermute | solution.py:729
  417.8 16.0 %copy-start.90 = (f32[4,4,4,1]{2,1,0,3:T(4,128)S(1)}, f32[4,4,4,1]{2,1,0,3:T(4,128)}, u32[]{:S(2)}) copy-start(f32[4,4,4,1]{2,1,0,3:T(4,128)} %copy-done.89) | copy-start | bytes 772
  417.8 16.8 %copy-start.94 = (f32[48]{0:T(128)S(1)}, f32[48]{0:T(128)}, u32[]{:S(2)}) copy-start(f32[48]{0:T(128)} %copy-done.93) | copy-start | bytes 580
  420.4 17.0 %copy-start.36 = (f32[4,12,4,192]{3,2,1,0:T(4,128)S(1)}, f32[4,12,4,192]{3,2,1,0:T(4,128)}, u32[]{:S(2)}) copy-start(f32[4,12,4,192]{3,2,1,0:T(4,128)} %copy-done.35) | copy-start | bytes 442372
  420.4 17.0 %copy-start.81 = (f32[4,12]{1,0:T(4,128)S(1)}, f32[4,12]{1,0:T(4,128)}, u32[]{:S(2)}) copy-start(f32[4,12]{1,0:T(4,128)} %copy-done.80) | copy-start | bytes 580
  420.4 19.0 %copy-start.73 = (s32[768]{0:T(1024)S(1)}, s32[768]{0:T(1024)}, u32[]{:S(2)}) copy-start(s32[768]{0:T(1024)} %copy-done.72) | copy-start | bytes 9220
  420.4 20.8 %copy-start.47 = (bf16[1024,768]{1,0:T(8,128)(2,1)S(1)}, bf16[1024,768]{1,0:T(8,128)(2,1)}, u32[]{:S(2)}) copy-start(bf16[1024,768]{1,0:T(8,128)(2,1)} %multiply_convert_fusion.4.rows_ref) | copy-start | bytes 4718596
  420.4 34.9 %all-to-all-start = ((bf16[8,80,768]{2,1,0:T(8,128)(2,1)}), bf16[8,80,768]{2,1,0:T(8,128)(2,1)}, u32[]{:S(2)}, u32[]{:S(2)}) async-start(bf16[8,80,768]{2,1,0:T(8,128)(2,1)} %bitcast.60), calls=%async_computation | async-start | bytes 1966080 | tf_op jit(solution)/shard_map/all_to_all | solution.py:795
  448.2 11.8 %copy-start.13 = (bf16[1024,768]{1,0:T(8,128)(2,1)S(1)}, bf16[1024,768]{1,0:T(8,128)(2,1)}, u32[]{:S(2)}) copy-start(bf16[1024,768]{1,0:T(8,128)(2,1)} %copy-done.12) | copy-start | bytes 4718596
  455.3 36.0 %all-to-all-start.2 = ((bf16[8,96,768]{2,1,0:T(8,128)(2,1)}), bf16[8,96,768]{2,1,0:T(8,128)(2,1)}, u32[]{:S(2)}, u32[]{:S(2)}) async-start(bf16[8,96,768]{2,1,0:T(8,128)(2,1)} %bitcast.63), calls=%async_computation.2 | async-start | bytes 2359296 | tf_op jit(solution)/shard_map/all_to_all | solution.py:795
  463.4 25.5 %collective-permute-start.11 = (bf16[768,768]{1,0:T(8,128)(2,1)S(1)}, bf16[768,768]{1,0:T(8,128)(2,1)S(1)}, u32[]{:S(2)}, u32[]{:S(2)}) collective-permute-start(bf16[768,768]{1,0:T(8,128)(2,1)S(1)} %add_convert_fusion.2), channel_id=1, source_target_pairs={{0,2},{1,3},{2,0},{3,1},{4,6},{5,7},{6,4},{7,5},{8,10},{9,11},{10,... | collective-permute-start | bytes 3538952 | tf_op jit(solution)/shard_map/ppermute | solution.py:729
  491.3 31.5 %all-to-all-start.3 = ((bf16[8,96,768]{2,1,0:T(8,128)(2,1)}), bf16[8,96,768]{2,1,0:T(8,128)(2,1)}, u32[]{:S(2)}, u32[]{:S(2)}) async-start(bf16[8,96,768]{2,1,0:T(8,128)(2,1)} %bitcast.64), calls=%async_computation.3 | async-start | bytes 2359296 | tf_op jit(solution)/shard_map/all_to_all | solution.py:795
  502.0 14.6 %copy-start.54 = (s32[8,80]{1,0:T(8,128)S(1)}, s32[8,80]{1,0:T(8,128)}, u32[]{:S(2)}) copy-start(s32[8,80]{1,0:T(8,128)} %copy-done.53) | copy-start | bytes 7684
  502.0 16.0 %copy-start.44 = (bf16[8,32,768]{2,1,0:T(8,128)(2,1)S(1)}, bf16[8,32,768]{2,1,0:T(8,128)(2,1)}, u32[]{:S(2)}) copy-start(bf16[8,32,768]{2,1,0:T(8,128)(2,1)} %copy-done.43) | copy-start | bytes 1179652
  507.1 10.3 %collective-permute-start.12 = (f32[3616]{0:T(1024)S(1)}, f32[3616]{0:T(1024)S(1)}, u32[]{:S(2)}, u32[]{:S(2)}) collective-permute-start(f32[3616]{0:T(1024)S(1)} %concatenate.8), channel_id=1, source_target_pairs={{0,1},{1,0},{2,3},{3,2},{4,5},{5,4},{6,7},{7,6},{8,9},{9,8},{10,11... | collective-permute-start | bytes 43400 | tf_op jit(solution)/shard_map/ppermute | solution.py:729
  517.4 12.9 %collective-permute-start.13 = (f32[3616]{0:T(1024)S(1)}, f32[3616]{0:T(1024)S(1)}, u32[]{:S(2)}, u32[]{:S(2)}) collective-permute-start(f32[3616]{0:T(1024)S(1)} %add.2005), channel_id=1, source_target_pairs={{0,2},{1,3},{2,0},{3,1},{4,6},{5,7},{6,4},{7,5},{8,10},{9,11},{10,... | collective-permute-start | bytes 43400 | tf_op jit(solution)/shard_map/ppermute | solution.py:729
  524.3 8.1 %copy-start.25 = (bf16[1024,768]{1,0:T(8,128)(2,1)S(1)}, bf16[1024,768]{1,0:T(8,128)(2,1)}, u32[]{:S(2)}) copy-start(bf16[1024,768]{1,0:T(8,128)(2,1)} %param.13) | copy-start | bytes 4718596
  526.0 32.6 %all-to-all-start.4 = ((bf16[8,80,768]{2,1,0:T(8,128)(2,1)}), bf16[8,80,768]{2,1,0:T(8,128)(2,1)S(1)}, u32[]{:S(2)}, u32[]{:S(2)}) async-start(bf16[8,80,768]{2,1,0:T(8,128)(2,1)} %bitcast.65), calls=%async_computation.4 | async-start | bytes 1966080 | tf_op jit(solution)/shard_map/all_to_all | solution.py:867
  530.3 8.2 %collective-permute-start.14 = (f32[3616]{0:T(1024)S(1)}, f32[3616]{0:T(1024)S(1)}, u32[]{:S(2)}, u32[]{:S(2)}) collective-permute-start(f32[3616]{0:T(1024)S(1)} %add.2006), channel_id=1, source_target_pairs={{0,4},{4,0},{8,12},{12,8},{16,20},{20,16},{24,28},{28,24},{1,5},{5... | collective-permute-start | bytes 43400 | tf_op jit(solution)/shard_map/ppermute | solution.py:729
  532.4 8.5 %copy-start.22 = (f32[1024,768]{1,0:T(8,128)S(1)}, f32[1024,768]{1,0:T(8,128)}, u32[]{:S(2)}) copy-start(f32[1024,768]{1,0:T(8,128)} %copy-done.20) | copy-start | bytes 9437188
  532.4 8.5 %copy-start.27 = (f32[1024,768]{1,0:T(8,128)S(1)}, f32[1024,768]{1,0:T(8,128)}, u32[]{:S(2)}) copy-start(f32[1024,768]{1,0:T(8,128)} %get-tuple-element.47) | copy-start | bytes 9437188
  532.4 8.4 %copy-start.50 = (f32[1024,48]{0,1:T(8,128)S(1)}, f32[1024,48]{0,1:T(8,128)}, u32[]{:S(2)}) copy-start(f32[1024,48]{0,1:T(8,128)} %copy-done.49) | copy-start | bytes 589828
  532.5 8.4 %copy-start.52 = (f32[48,768]{1,0:T(8,128)S(1)}, f32[48,768]{1,0:T(8,128)}, u32[]{:S(2)}) copy-start(f32[48,768]{1,0:T(8,128)} %reshape.4218) | copy-start | bytes 442372
  538.5 18.8 %copy-start.60 = (f32[3616]{0:T(1024)S(1)}, f32[3616]{0:T(1024)}, u32[]{:S(2)}) copy-start(f32[3616]{0:T(1024)} %param.21) | copy-start | bytes 43396
  538.5 18.8 %copy-start.83 = (f32[3616]{0:T(1024)S(1)}, f32[3616]{0:T(1024)}, u32[]{:S(2)}) copy-start(f32[3616]{0:T(1024)} %param.23) | copy-start | bytes 43396
  538.6 18.8 %copy-start.84 = (f32[3616]{0:T(1024)S(1)}, f32[3616]{0:T(1024)}, u32[]{:S(2)}) copy-start(f32[3616]{0:T(1024)} %param.22) | copy-start | bytes 43396
  538.6 19.4 %copy-start.88 = (f32[1696]{0:T(1024)S(1)}, f32[1696]{0:T(1024)}, u32[]{:S(2)}) copy-start(f32[1696]{0:T(1024)} %param.24) | copy-start | bytes 20356
  538.6 9.0 %collective-permute-start.15 = (f32[3616]{0:T(1024)S(1)}, f32[3616]{0:T(1024)S(1)}, u32[]{:S(2)}, u32[]{:S(2)}) collective-permute-start(f32[3616]{0:T(1024)S(1)} %add.2007), channel_id=1, source_target_pairs={{0,8},{4,12},{8,0},{12,4},{16,24},{20,28},{24,16},{28,20},{1,9},{5... | collective-permute-start | bytes 43400 | tf_op jit(solution)/shard_map/ppermute | solution.py:729
  547.6 9.7 %collective-permute-start.16 = (f32[3616]{0:T(1024)S(1)}, f32[3616]{0:T(1024)S(1)}, u32[]{:S(2)}, u32[]{:S(2)}) collective-permute-start(f32[3616]{0:T(1024)S(1)} %add.2008), channel_id=1, source_target_pairs={{0,16},{4,20},{8,24},{12,28},{16,0},{20,4},{24,8},{28,12},{1,17},{... | collective-permute-start | bytes 43400 | tf_op jit(solution)/shard_map/ppermute | solution.py:729
  558.0 9.5 %copy-start.74 = (f32[3616]{0:T(1024)}, f32[3616]{0:T(1024)S(1)}, u32[]{:S(2)}) copy-start(f32[3616]{0:T(1024)S(1)} %get-tuple-element.84) | copy-start | bytes 43396
  (62 other events, 231.7 us)

commit v3 on v2

--- a/solution.py
+++ b/solution.py
@@ -434,21 +434,20 @@
     )
 
 
-def attend_back_kernel(
-    query_ref,
-    key_ref,
-    value_ref,
+def attend_head_back(
+    query_rows,
+    key_rows,
+    value_rows,
     exp_ref,
-    out_ref,
-    scale_ref,
-    out_grad_ref,
-    proj_grad_ref,
-    offset_grad_ref,
+    attended,
+    scale,
+    attended_grad,
     window,
     score_grads,
+    store,
 ):
-    scaled = out_grad_ref[...].astype(jnp.float32) * scale_ref[0]
-    delta = jnp.sum(scaled * out_ref[0].astype(jnp.float32), axis=0, keepdims=True)
+    scaled = attended_grad.astype(jnp.float32) * scale
+    delta = jnp.sum(scaled * attended.astype(jnp.float32), axis=0, keepdims=True)
     scaled_low = scaled.astype(jnp.bfloat16)
     delta_high = delta.astype(jnp.bfloat16).astype(jnp.float32)
     delta_rest = delta - delta_high
@@ -459,9 +458,8 @@
         jnp.where(place == 1, jnp.broadcast_to(-delta_rest, (16, SEQ)), 0.0),
     ).astype(jnp.bfloat16)
     grads = jnp.concatenate([scaled_low, extra], axis=0)
-    values = jnp.concatenate([value_ref[0], jnp.ones((16, SEQ), jnp.bfloat16)], axis=0).T
+    values = jnp.concatenate([value_rows, jnp.ones((16, SEQ), jnp.bfloat16)], axis=0).T
     window[...] = jnp.zeros_like(window)
-    keys = key_ref[0]
     for q0 in range(0, SEQ, QUERY_TILE):
         total = jnp.zeros((HS, QUERY_TILE), jnp.float32)
         for k0 in range(0, SEQ, KEY_TILE):
@@ -471,7 +469,7 @@
                 preferred_element_type=jnp.float32,
             )
             score_grad = centered * exp_ref[
-                0, k0 : k0 + KEY_TILE, q0 : q0 + QUERY_TILE
+                k0 : k0 + KEY_TILE, q0 : q0 + QUERY_TILE
             ].astype(jnp.float32)
             for l0 in range(0, QUERY_TILE, TILE):
                 start = SEQ - TILE - (q0 + l0) + k0
@@ -479,21 +477,21 @@
             score_low = score_grad.astype(jnp.bfloat16)
             score_grads[k0 : k0 + KEY_TILE, q0 : q0 + QUERY_TILE] = score_low
             total = total + jnp.dot(
-                keys[:, k0 : k0 + KEY_TILE], score_low, preferred_element_type=jnp.float32
+                key_rows[:, k0 : k0 + KEY_TILE], score_low, preferred_element_type=jnp.float32
             )
-        proj_grad_ref[0, 0, :, q0 : q0 + QUERY_TILE] = total.astype(jnp.bfloat16)
-    queries = query_ref[0].T
+        store(0, q0, total.astype(jnp.bfloat16))
+    queries = query_rows.T
     scaled_rows = scaled_low.T
     for k0 in range(0, SEQ, KEY_TILE):
         key_grad = jnp.dot(
             score_grads[k0 : k0 + KEY_TILE, :], queries, preferred_element_type=jnp.float32
         )
         value_grad = jnp.dot(
-            exp_ref[0, k0 : k0 + KEY_TILE, :], scaled_rows, preferred_element_type=jnp.float32
-        )
-        proj_grad_ref[1, 0, :, k0 : k0 + KEY_TILE] = key_grad.T.astype(jnp.bfloat16)
-        proj_grad_ref[2, 0, :, k0 : k0 + KEY_TILE] = value_grad.T.astype(jnp.bfloat16)
-    offset_grad_ref[...] = jnp.zeros_like(offset_grad_ref)
+            exp_ref[k0 : k0 + KEY_TILE, :], scaled_rows, preferred_element_type=jnp.float32
+        )
+        store(1, k0, key_grad.T.astype(jnp.bfloat16))
+        store(2, k0, value_grad.T.astype(jnp.bfloat16))
+    pieces = [jnp.zeros((1, TILE), jnp.float32)] * (2 * SEQ // TILE)
     for tile in range(WINDOW // TILE):
         base = WINDOW - TILE * tile
         block = window[TILE * tile : TILE * (tile + 1), :]
@@ -502,43 +500,543 @@
         while rows >= 1:
             folded = folded[:rows] + pltpu.roll(folded[rows:], 2 * TILE - rows, 1)
             rows //= 2
-        offset_grad_ref[0, :, base - TILE : base + TILE] += folded
-
-
-def attend_back(group, projected, exp_scores, attended, scale, attended_grad):
-    heads = H // projected.shape[0]
-    first = group * heads
+        pieces[base // TILE - 1] += folded[:, :TILE]
+        pieces[base // TILE] += folded[:, TILE:]
+    return jnp.concatenate(pieces, axis=1)
+
+
+SMALL_ROWS = 48
+TABLE_ROW = 32
+
+
+def back_kernel(
+    sizes,
+    grad_out_ref,
+    grad_in_ref,
+    grad_down_ref,
+    projected_ref,
+    exp_ref,
+    attended_ref,
+    scale_ref,
+    attended_grad_ref,
+    normed_ref,
+    w_qkv_ref,
+    tokens_ref,
+    mid_grad_ref,
+    gain_ref,
+    small_ref,
+    bucket_ref,
+    place_qkv_ref,
+    place_out_ref,
+    place_in_ref,
+    place_down_ref,
+    spread_place_ref,
+    slot_place_ref,
+    owned_ref,
+    input_grad_ref,
+    small_total_ref,
+    proj,
+    proj_grad,
+    normed_grad,
+    window,
+    score_grads,
+    exp_stage,
+    qkv_odd,
+    zero_qkv,
+    zero_out,
+    zero_in,
+    zero_down,
+    two_qkv,
+    two_out,
+    two_in,
+    two_down,
+    core_one_qkv,
+    core_one_out,
+    core_one_in,
+    core_one_down,
+    core_three_qkv,
+    core_three_out,
+    core_three_in,
+    core_three_down,
+    far_qkv,
+    far_out,
+    far_in,
+    far_down,
+    got_qkv,
+    got_out,
+    got_in,
+    got_down,
+    spread,
+    sent,
+    received,
+    small_own,
+    small_tensor,
+    small_dp,
+    core_send,
+    core_recv,
+    far_send,
+    far_recv,
+    deal_send,
+    deal_recv,
+    back_send,
+    back_recv,
+    small_send,
+    small_recv,
+    load_sem,
+    exp_sem,
+    proj_sem,
+):
+    dp_count, pair_rows = sent.shape[0], sent.shape[1]
+    tensor_count = w_qkv_ref.shape[0]
+    heads = scale_ref.shape[0]
+    group_heads = heads // tensor_count
+    head_rows = group_heads * HS
+    dp_pos, tensor_pos = lax.axis_index("dp"), lax.axis_index("tensor")
+    core_pos = tensor_pos + 1 - 2 * lax.rem(tensor_pos, 2)
+    far_pos = lax.rem(tensor_pos + 2, tensor_count)
+    core_peer, far_peer = (dp_pos, core_pos), (dp_pos, far_pos)
+    grad_refs = (None, grad_out_ref, grad_in_ref, grad_down_ref)
+    zeros = (zero_qkv, zero_out, zero_in, zero_down)
+    twos = (two_qkv, two_out, two_in, two_down)
+    core_ones = (core_one_qkv, core_one_out, core_one_in, core_one_down)
+    core_threes = (core_three_qkv, core_three_out, core_three_in, core_three_down)
+    fars = (far_qkv, far_out, far_in, far_down)
+    gots = (got_qkv, got_out, got_in, got_down)
+    places = (place_qkv_ref, place_out_ref, place_in_ref, place_down_ref)
+    offsets = [sum(got.shape[1] for got in gots[:role]) for role in range(len(gots))]
+    low = jnp.bfloat16
+
+    def up(m):
+        return lax.rem(dp_pos + m, dp_count)
+
+    def down(m):
+        return lax.rem(dp_pos + dp_count - m, dp_count)
+
+    def each_peer(run):
+        def step(m, carry):
+            run(m)
+            return carry
+
+        lax.fori_loop(1, dp_count, step, 0)
+
+    def tensor_peer(m):
+        return (dp_pos, lax.rem(tensor_pos + m, tensor_count))
+
+    barrier = pltpu.get_barrier_semaphore()
+
+    def greet(m):
+        pl.semaphore_signal(barrier, inc=1, device_id=(up(m), tensor_pos), device_id_type=MESH)
+
+    each_peer(greet)
+    for m in range(1, tensor_count):
+        pl.semaphore_signal(barrier, inc=1, device_id=tensor_peer(m), device_id_type=MESH)
+
+    def load_exp(head, slot):
+        return pltpu.make_async_copy(exp_ref.at[head], exp_stage.at[slot], exp_sem.at[slot])
+
+    def load_proj(group):
+        return pltpu.make_async_copy(projected_ref.at[group], proj, proj_sem)
+
+    def load(role, which):
+        target = zeros[role] if which == 0 else twos[role]
+        return pltpu.make_async_copy(
+            grad_refs[role].at[which], target, load_sem.at[role, which // 2]
+        )
+
+    def core_copy(role, which):
+        if role == 0:
+            src = qkv_odd.at[which // 2]
+        else:
+            src = grad_refs[role].at[which]
+        target = core_ones[role] if which == 1 else core_threes[role].at[pl.ds(0, sizes[role])]
+        return pltpu.make_async_remote_copy(
+            src,
+            target,
+            core_send.at[role, which // 2],
+            core_recv.at[role, which // 2],
+            device_id=core_peer,
+            device_id_type=MESH,
+        )
+
+    def far_copy(role):
+        return pltpu.make_async_remote_copy(
+            twos[role],
+            fars[role],
+            far_send.at[role],
+            far_recv.at[role],
+            device_id=far_peer,
+            device_id_type=MESH,
+        )
+
+    def deal_copy(role, m):
+        count = gots[role].shape[1]
+        start = pl.multiple_of(m * count, 16)
+        return pltpu.make_async_remote_copy(
+            core_threes[role].at[pl.ds(start, count)],
+            gots[role].at[m],
+            deal_send.at[role, m],
+            deal_recv.at[role, m],
+            device_id=(up(m), tensor_pos),
+            device_id_type=MESH,
+        )
+
+    def send_far(role):
+        core_copy(role, 3).wait_recv()
+        if role > 0:
+            load(role, 2).wait()
+        count = twos[role].shape[0]
+        twos[role][...] = (
+            twos[role][...].astype(jnp.float32)
+            + core_threes[role][0:count, :].astype(jnp.float32)
+        ).astype(low)
+        far_copy(role).start()
+
+    def send_deal(role):
+        core_copy(role, 1).wait_recv()
+        if role > 0:
+            load(role, 0).wait()
+        far_copy(role).wait_recv()
+        total = (
+            zeros[role][...].astype(jnp.float32)
+            + core_ones[role][...].astype(jnp.float32)
+            + fars[role][...].astype(jnp.float32)
+        ).astype(low)
+        count = gots[role].shape[1]
+        for m in range(dp_count):
+            hot = one_hot(places[role][...] - m * count, (count, sizes[role]), 0)
+            core_threes[role][m * count : (m + 1) * count, :] = jnp.dot(
+                hot, total, preferred_element_type=jnp.float32
+            ).astype(low)
+        each_peer(lambda m: deal_copy(role, m).start())
+
+    def finish_deal(role):
+        each_peer(lambda m: deal_copy(role, m).wait())
+        count = gots[role].shape[1]
+        total = core_threes[role][0:count, :].astype(jnp.float32)
+        for m in range(1, dp_count):
+            total = total + gots[role][m].astype(jnp.float32)
+        spread[offsets[role] : offsets[role] + count, :] = total.astype(low)
+
+    load_exp(heads - group_heads, 0).start()
+    load_proj(tensor_count - 1).start()
+    for role in (3, 2, 1):
+        load(role, 2).start()
+        load(role, 0).start()
+    normed_grad[...] = jnp.zeros_like(normed_grad)
+    small_own[0:TABLE_ROW, :] = small_ref[...]
+    small_own[TABLE_ROW:SMALL_ROWS, :] = jnp.zeros((SMALL_ROWS - TABLE_ROW, TILE), jnp.float32)
+    pl.semaphore_wait(barrier, dp_count + tensor_count - 2)
+    for role in (3, 2, 1):
+        core_copy(role, 3).start()
+        core_copy(role, 1).start()
+
+    def head_step(i, carry):
+        group = tensor_count - 1 - lax.div(i, group_heads)
+        part_head = lax.rem(i, group_heads)
+        head = group * group_heads + part_head
+        slot = lax.rem(i, 2)
+
+        @pl.when(i == 1)
+        def _():
+            send_far(3)
+
+        @pl.when(i == 7)
+        def _():
+            send_far(2)
+
+        @pl.when(i == 9)
+        def _():
+            send_deal(3)
+
+        @pl.when(part_head == 0)
+        def _():
+            load_proj(group).wait()
+
+        @pl.when(i + 1 < heads)
+        def _():
+            later = i + 1
+            later_group = tensor_count - 1 - lax.div(later, group_heads)
+            later_head = later_group * group_heads + lax.rem(later, group_heads)
+            load_exp(later_head, lax.rem(later, 2)).start()
+
+        load_exp(head, slot).wait()
+
+        def rows(part):
+            return pl.ds(pl.multiple_of(part * head_rows + part_head * HS, HS), HS)
+
+        def store(part, column, value):
+            proj_grad[rows(part), column : column + value.shape[1]] = value
+
+        here = pl.ds(pl.multiple_of(head * HS, HS), HS)
+        offset_grad = attend_head_back(
+            proj[rows(0), :],
+            proj[rows(1), :],
+            proj[rows(2), :],
+            exp_stage.at[slot],
+            attended_ref[here, :],
+            scale_ref[head],
+            attended_grad_ref[here, :],
+            window,
+            score_grads,
+            store,
+        )
+        flips = (tensor_pos, core_pos, far_pos, tensor_count - 1 - tensor_pos)
+        true_group = flips[0]
+        for g in range(1, tensor_count):
+            true_group = true_group + (flips[g] - flips[0]) * (
+                lax.div(group + tensor_count - g, tensor_count)
+                - lax.div(group + tensor_count - g - 1, tensor_count)
+            )
+        high = offset_grad.astype(low)
+        rest = (offset_grad - high.astype(jnp.float32)).astype(low)
+        both = jnp.concatenate([high, rest] + [jnp.zeros_like(high)] * 6, axis=0)
+        sums = jnp.dot(both, bucket_ref[...], preferred_element_type=jnp.float32)
+        line = lax.broadcasted_iota(jnp.int32, (SMALL_ROWS - TABLE_ROW, TILE), 0)
+        small_own[TABLE_ROW:SMALL_ROWS, :] += jnp.where(
+            line == true_group * group_heads + part_head,
+            jnp.broadcast_to(sums[0:1] + sums[1:2], (SMALL_ROWS - TABLE_ROW, TILE)),
+            0.0,
+        )
+
+        @pl.when(part_head == group_heads - 1)
+        def _():
+            @pl.when(group > 0)
+            def _():
+                load_proj(group - 1).start()
+
+            def weight_grad(target):
+                for r0 in range(0, 3 * head_rows, head_rows):
+                    target[r0 : r0 + head_rows, :] = jnp.dot(
+                        proj_grad[r0 : r0 + head_rows, :],
+                        normed_ref[...],
+                        preferred_element_type=jnp.float32,
+                    ).astype(low)
+
+            @pl.when(group == 3)
+            def _():
+                weight_grad(qkv_odd.at[1])
+                core_copy(0, 3).start()
+
+            @pl.when(group == 2)
+            def _():
+                weight_grad(two_qkv)
+
+            @pl.when(group == 1)
+            def _():
+                weight_grad(qkv_odd.at[0])
+                core_copy(0, 1).start()
+
+            @pl.when(group == 0)
+            def _():
+                weight_grad(zero_qkv)
+
+            for r0 in range(0, SEQ, 256):
+                normed_grad[r0 : r0 + 256, :] += jnp.dot(
+                    proj_grad[:, r0 : r0 + 256].T,
+                    w_qkv_ref[group],
+                    preferred_element_type=jnp.float32,
+                )
+
+        return carry
+
+    lax.fori_loop(0, heads, head_step, 0)
+    send_far(1)
+    send_far(0)
+
+    gain_grad = jnp.zeros((1, D), jnp.float32)
+    for r0 in range(0, SEQ, 128):
+        values = tokens_ref[r0 : r0 + 128, :].astype(jnp.float32)
+        grads = normed_grad[r0 : r0 + 128, :]
+        inverse = lax.rsqrt(jnp.mean(values * values, axis=1, keepdims=True) + norm_epsilon)
+        scaled = values * inverse
+        gain_grad = gain_grad + jnp.sum(grads * scaled, axis=0, keepdims=True)
+        grads = grads * gain_ref[...]
+        inner = jnp.mean(grads * scaled, axis=1, keepdims=True)
+        input_grad_ref[r0 : r0 + 128, :] = (
+            mid_grad_ref[r0 : r0 + 128, :].astype(jnp.float32) + inverse * (grads - scaled * inner)
+        ).astype(low)
+    for part in range(D // TILE):
+        small_own[part : part + 1, :] = gain_grad[:, TILE * part : TILE * (part + 1)]
+
+    def small_copy(stage, m):
+        if stage == 0:
+            src, target, peer = small_own, small_tensor.at[tensor_pos], tensor_peer(m)
+        else:
+            src, target, peer = small_total_ref, small_dp.at[dp_pos], (up(m), tensor_pos)
+        return pltpu.make_async_remote_copy(
+            src,
+            target,
+            small_send.at[stage, m],
+            small_recv.at[stage, m],
+            device_id=peer,
+            device_id_type=MESH,
+        )
+
+    for m in range(1, tensor_count):
+        small_copy(0, m).start()
+    send_deal(2)
+    small_tensor[tensor_pos] = small_own[...]
+    for m in range(1, tensor_count):
+        small_copy(0, m).wait()
+    total = small_tensor[0]
+    for m in range(1, tensor_count):
+        total = total + small_tensor[m]
+    small_total_ref[...] = total
+    each_peer(lambda m: small_copy(1, m).start())
+    send_deal(1)
+    finish_deal(3)
+    send_deal(0)
+    small_dp[dp_pos] = small_total_ref[...]
+    each_peer(lambda m: small_copy(1, m).wait())
+    total = small_dp[0]
+    for m in range(1, dp_count):
+        total = total + small_dp[m]
+    small_total_ref[...] = total
+    for role in (2, 1, 0):
+        finish_deal(role)
+
+    values = spread[...]
+    for m in range(dp_count):
+        hot = one_hot(
+            spread_place_ref[m * pair_rows : (m + 1) * pair_rows, :],
+            (pair_rows, values.shape[0]),
+            1,
+        )
+        sent[m] = jnp.dot(hot, values, preferred_element_type=jnp.float32).astype(low)
+
+    def back_copy(m):
+        return pltpu.make_async_remote_copy(
+            sent.at[m],
+            received.at[m],
+            back_send.at[m],
+            back_recv.at[m],
+            device_id=(down(m), tensor_pos),
+            device_id_type=MESH,
+        )
+
+    each_peer(lambda m: back_copy(m).start())
+    received[0] = sent[0]
+    each_peer(lambda m: back_copy(m).wait())
+    capacity = owned_ref.shape[0]
+    hot = one_hot(slot_place_ref[...], (capacity, dp_count * pair_rows), 1)
+    owned_ref[...] = jnp.dot(
+        hot, received[...].reshape(dp_count * pair_rows, D), preferred_element_type=jnp.float32
+    )
+    for role in range(len(gots)):
+        core_copy(role, 1).wait_send()
+        core_copy(role, 3).wait_send()
+        far_copy(role).wait_send()
+
+
+def back(
+    weight_grads,
+    projected,
+    exp_scores,
+    attended,
+    scale,
+    attended_grad,
+    normed,
+    w_qkv,
+    tokens,
+    mid_grad,
+    gain,
+    small,
+    buckets,
+    places,
+    local_sizes,
+    pair_rows,
+    spread_place,
+    slot_place,
+):
+    dp_count, tensor_count = lax.axis_size("dp"), lax.axis_size("tensor")
+    sizes = [place.shape[0] for place in places]
+    capacity = slot_place.shape[0]
+    low = jnp.bfloat16
+    dma = pltpu.SemaphoreType.DMA
+    roles = len(sizes)
+    whole = pl.BlockSpec(memory_space=pltpu.VMEM)
+    away = pl.BlockSpec(memory_space=pl.ANY)
+    parts = [pltpu.VMEM((size, D), low) for size in sizes]
+    padded = [pltpu.VMEM((dp_count * size, D), low) for size in local_sizes]
+    padded = [
+        pltpu.VMEM((max(dp_count * size, full), D), low) for size, full in zip(local_sizes, sizes)
+    ]
+    bucket_place = jnp.concatenate([jnp.full((1,), -1, jnp.int32), buckets[::-1]])
+    bucket_hot = (
+        bucket_place[:, None] == jnp.arange(TILE, dtype=jnp.int32)[None, :]
+    ).astype(low)
     return pl.pallas_call(
-        attend_back_kernel,
-        grid=(heads,),
-        in_specs=[
-            pl.BlockSpec((1, HS, SEQ), lambda h, part=part: (group, part * heads + h, 0))
-            for part in range(3)
-        ]
-        + [
-            pl.BlockSpec((1, SEQ, SEQ), lambda h: (first + h, 0, 0)),
-            pl.BlockSpec((1, HS, SEQ), lambda h: (group, h, 0)),
-            pl.BlockSpec((1, 1, SEQ), lambda h: (first + h, 0, 0)),
-            pl.BlockSpec((HS, SEQ), lambda h: (h, 0)),
-        ],
-        out_specs=[
-            pl.BlockSpec((3, 1, HS, SEQ), lambda h: (0, h, 0, 0)),
-            pl.BlockSpec((1, 1, 2 * SEQ), lambda h: (h, 0, 0)),
-        ],
+        functools.partial(back_kernel, sizes),
+        in_specs=[away] * 5 + [whole] * 16,
+        out_specs=[whole] * 3,
         out_shape=[
-            jax.ShapeDtypeStruct((3, heads, HS, SEQ), jnp.bfloat16),
-            jax.ShapeDtypeStruct((heads, 1, 2 * SEQ), jnp.float32),
+            jax.ShapeDtypeStruct((capacity, D), jnp.float32),
+            jax.ShapeDtypeStruct((SEQ, D), low),
+            jax.ShapeDtypeStruct((SMALL_ROWS, TILE), jnp.float32),
         ],
         scratch_shapes=[
+            pltpu.VMEM((sizes[0], SEQ), low),
+            pltpu.VMEM((sizes[0], SEQ), low),
+            pltpu.VMEM((SEQ, D), jnp.float32),
             pltpu.VMEM((WINDOW, TILE), jnp.float32),
-            pltpu.VMEM((SEQ, SEQ), jnp.bfloat16),
+            pltpu.VMEM((SEQ, SEQ), low),
+            pltpu.VMEM((2, SEQ, SEQ), low),
+            pltpu.VMEM((2, sizes[0], D), low),
+        ]
+        + parts
+        + parts
+        + parts
+        + padded
+        + parts
+        + [pltpu.VMEM((dp_count, size, D), low) for size in local_sizes]
+        + [
+            pltpu.VMEM((sum(local_sizes), D), low),
+            pltpu.VMEM((dp_count, pair_rows, D), low),
+            pltpu.VMEM((dp_count, pair_rows, D), low),
+            pltpu.VMEM((SMALL_ROWS, TILE), jnp.float32),
+            pltpu.VMEM((tensor_count, SMALL_ROWS, TILE), jnp.float32),
+            pltpu.VMEM((dp_count, SMALL_ROWS, TILE), jnp.float32),
+            dma((roles, 2)),
+            dma((roles, 2)),
+            dma((roles,)),
+            dma((roles,)),
+            dma((roles, dp_count)),
+            dma((roles, dp_count)),
+            dma((dp_count,)),
+            dma((dp_count,)),
+            dma((2, max(dp_count, tensor_count))),
+            dma((2, max(dp_count, tensor_count))),
+            dma((roles, 2)),
+            dma((2,)),
+            dma,
         ],
-        compiler_params=pltpu.CompilerParams(vmem_limit_bytes=VMEM_LIMIT),
+        compiler_params=pltpu.CompilerParams(
+            collective_id=2, has_side_effects=True, vmem_limit_bytes=62 * 1024 * 1024
+        ),
         cost_estimate=pl.CostEstimate(
-            flops=12 * heads * SEQ * SEQ * 256, bytes_accessed=3 * heads * SEQ * SEQ, transcendentals=0
+            flops=16 * H * SEQ * SEQ * 256,
+            bytes_accessed=64 * 1024 * 1024,
+            transcendentals=0,
         ),
-        name="attend_back",
-    )(projected, projected, projected, exp_scores, attended, scale, attended_grad)
+        name="back",
+    )(
+        *weight_grads,
+        projected,
+        exp_scores,
+        attended,
+        scale,
+        attended_grad,
+        normed,
+        w_qkv,
+        tokens,
+        mid_grad,
+        gain[None, :],
+        small,
+        bucket_hot,
+        *[place[None, :] for place in places],
+        spread_place[:, None],
+        slot_place[:, None],
+    )
 
 
 def feed_kernel(rows_ref, w_in_ref, w_down_ref, before_ref, activ_ref, slope_ref, out_ref):
@@ -593,39 +1091,6 @@
     )(rows, w_in, w_down, before)
 
 
-def select_kernel(by_row, count, place_ref, *refs):
-    blocks, out_ref = refs[:-1], refs[-1]
-    total = jnp.zeros(out_ref.shape, jnp.float32)
-    offset = 0
-    for block in blocks:
-        rows = block.shape[0]
-        shape = (count, rows)
-        if by_row:
-            hit = lax.broadcasted_iota(jnp.int32, shape, 1) + offset == place_ref[...]
-        else:
-            hit = lax.broadcasted_iota(jnp.int32, shape, 0) == place_ref[...]
-        hit = jnp.where(hit, 1.0, 0.0).astype(jnp.bfloat16)
-        total = total + jnp.dot(hit, block[...], preferred_element_type=jnp.float32)
-        offset += rows
-    out_ref[...] = total.astype(out_ref.dtype)
-
-
-def select_rows(blocks, count, source=None, target=None, dtype=jnp.bfloat16):
-    if len(blocks) > 16:
-        blocks = [jnp.concatenate(blocks, axis=0)]
-    place = source[:, None] if target is None else target[None, :]
-    total = sum(block.shape[0] for block in blocks)
-    return pl.pallas_call(
-        functools.partial(select_kernel, target is None, count),
-        out_shape=jax.ShapeDtypeStruct((count, D), dtype),
-        compiler_params=pltpu.CompilerParams(vmem_limit_bytes=VMEM_LIMIT),
-        cost_estimate=pl.CostEstimate(
-            flops=2 * count * total * D, bytes_accessed=2 * (count + total) * D, transcendentals=0
-        ),
-        name="select_rows",
-    )(place, *blocks)
-
-
 def adamw(weights, grads, first, second, step):
     first_new = beta_first * first + (1.0 - beta_first) * grads
     second_new = beta_second * second + (1.0 - beta_second) * grads * grads
@@ -724,10 +1189,6 @@
         row_target.append(number % dp_count)
         row_rank.append(number // dp_count)
 
-    def swap(values, axis, bit):
-        count = lax.axis_size(axis)
-        return lax.ppermute(values, axis, [(i, i ^ bit) for i in range(count)])
-
     orders = [
         ((dp_pos - row_target[role]) % dp_count) * local_sizes[role] + row_rank[role]
         for role in range(roles)
@@ -778,33 +1239,9 @@
     ffn_grad, adapter_grad = adapter_pull(out_grad)
     ffn_grad = ffn_grad.astype(jnp.bfloat16)
 
-    def low_add(left, right):
-        return (left.astype(jnp.float32) + right.astype(jnp.float32)).astype(jnp.bfloat16)
-
-    def to_own(parts):
-        total = low_add(parts[0], swap(parts[1], "tensor", 1))
-        for bit in range(2, tensor_count, 2):
-            pair = low_add(parts[bit], swap(parts[bit + 1], "tensor", 1))
-            total = low_add(total, swap(pair, "tensor", bit))
-        return total
-
-    def to_spread(role, parts):
-        total = to_own(parts)
-        place = row_target[role] * local_sizes[role] + row_rank[role]
-        total = select_rows([total], dp_count * local_sizes[role], target=place)
-        total = lax.all_to_all(
-            total.reshape(dp_count, local_sizes[role], D),
-            "dp",
-            split_axis=0,
-            concat_axis=0,
-            tiled=True,
-        )
-        return jnp.sum(total.astype(jnp.float32), axis=0).astype(jnp.bfloat16)
-
-    back = list(groups)[::-1]
     normed_two_grad = jnp.zeros(mid.shape, jnp.float32)
     down_grad, in_grad = [None] * tensor_count, [None] * tensor_count
-    for k in back:
+    for k in reversed(groups):
         pre_grad = (contract(ffn_grad, w_down[k], 1, 1) * slope[k].astype(jnp.float32)).astype(
             jnp.bfloat16
         )
@@ -813,67 +1250,52 @@
         normed_two_grad = normed_two_grad + jnp.dot(
             pre_grad, w_in[k], preferred_element_type=jnp.float32
         )
-    down_grad = to_spread(3, down_grad)
-    in_grad = to_spread(2, in_grad)
     _, norm_two_pull = jax.vjp(rms_norm, mid, gain_two)
     mid_extra, gain_two_grad = norm_two_pull(normed_two_grad)
     mid_grad = out_grad + mid_extra
     mid_grad_low = mid_grad.astype(jnp.bfloat16)
-    out_weight_grad = to_spread(
-        1,
+    attended_all = attended.reshape(D, SEQ)
+    out_weight_grad = jnp.dot(
+        attended_all, mid_grad_low, preferred_element_type=jnp.float32
+    ).astype(jnp.bfloat16)
+    attended_grad = contract(w_out.reshape(D, D), mid_grad_low, 1, 1).astype(jnp.bfloat16)
+    small_local = jnp.concatenate(
+        [jnp.zeros((D,), jnp.float32), gain_two_grad]
+        + [piece.reshape(-1) for piece in adapter_grad]
+        + [jnp.zeros((TABLE_ROW * TILE - 2 * D - NADAPT,), jnp.float32)]
+    ).reshape(TABLE_ROW, TILE)
+    owned_grad, input_grad, small_total = back(
+        (
+            out_weight_grad.reshape(tensor_count, head_rows, D),
+            jnp.stack(in_grad),
+            jnp.stack(down_grad),
+        ),
+        projected,
+        exp_scores,
+        attended_all,
+        scale,
+        attended_grad,
+        normed_one,
+        w_qkv,
+        tokens,
+        mid_grad_low,
+        gain_one,
+        small_local,
+        buckets,
         [
-            jnp.dot(attended[k], mid_grad_low, preferred_element_type=jnp.float32).astype(
-                jnp.bfloat16
-            )
-            for k in groups
+            ((row_target[role] - dp_pos) % dp_count) * local_sizes[role] + row_rank[role]
+            for role in range(roles)
         ],
-    )
-    normed_one_grad = jnp.zeros(mid.shape, jnp.float32)
-    qkv_grad, offset_grad = [None] * tensor_count, [None] * tensor_count
-    for k in back:
-        attended_grad = contract(w_out[k], mid_grad_low, 1, 1).astype(jnp.bfloat16)
-        proj_grad, offset_grad[k] = attend_back(
-            k, projected, exp_scores, attended, scale, attended_grad
-        )
-        proj_grad = proj_grad.reshape(3 * head_rows, SEQ)
-        qkv_grad[k] = jnp.dot(proj_grad, normed_one, preferred_element_type=jnp.float32).astype(
-            jnp.bfloat16
-        )
-        normed_one_grad = normed_one_grad + contract(proj_grad, w_qkv[k], 0, 0)
-    qkv_grad = to_spread(0, qkv_grad)
-    _, norm_one_pull = jax.vjp(rms_norm, inputs_f, gain_one)
-    input_extra, gain_one_grad = norm_one_pull(normed_one_grad)
-    input_grad = (mid_grad + input_extra).astype(jnp.bfloat16)
-    offset_all = jnp.stack(offset_grad)
-    offset_all = offset_all[group_order].reshape(H, 2 * SEQ)
-    table_grad = jnp.dot(bucket_onehot.T, offset_all[:, 1:][:, ::-1].T, precision=highest)
+        local_sizes,
+        pair_rows,
+        spread_place,
+        slot_place,
+    )
     small_total = jnp.concatenate(
-        [gain_one_grad, gain_two_grad]
-        + [piece.reshape(-1) for piece in adapter_grad]
-        + [table_grad.reshape(-1)]
-    )
-    for axis, count in (("tensor", tensor_count), ("dp", dp_count)):
-        bit = 1
-        while bit < count:
-            small_total = small_total + swap(small_total, axis, bit)
-            bit *= 2
-
-    bank_grad = jnp.concatenate([qkv_grad, out_weight_grad, in_grad, down_grad], axis=0)
-    sent = select_rows(
-        [bank_grad],
-        dp_count * pair_rows,
-        source=spread_place.reshape(dp_count, pair_rows)[source_dp].reshape(-1),
-    )
-    received = lax.all_to_all(
-        sent.reshape(dp_count, pair_rows, D), "dp", split_axis=0, concat_axis=0, tiled=True
-    )
-    back_place = jnp.where(
-        slot_place >= 0,
-        (slot_place // pair_rows + dp_pos) % dp_count * pair_rows + slot_place % pair_rows,
-        -1,
-    )
-    owned_grad = select_rows(
-        [received.reshape(-1, D)], capacity, source=back_place, dtype=jnp.float32
+        [
+            small_total[:TABLE_ROW].reshape(-1)[: 2 * D + NADAPT],
+            small_total[TABLE_ROW : TABLE_ROW + H, :NB].T.reshape(-1),
+        ]
     )
     own_filled = (slot_place >= 0).astype(jnp.float32)[:, None]
     step = step_count[0].astype(jnp.float32)

time: 574 us -> 550 us (0.958)
  Pallas kernels: 254 us -> 367 us
  starting transfers between devices: 57.9 us -> 0 us
  matrix products: 114 us -> 68 us
  waiting for transfers between devices: 32.9 us -> 0 us
    pallas_call x10 -> x1, Pallas kernels: 56.1 us -> 178 us  [back(): pl.pallas_call(functools.partial(back_kernel, sizes), in_specs=[away] * 5...]
    all_to_all x5 -> x0, starting transfers between devices: 43.6 us -> none  [the longest x4 39.4 us: to_spread(): lax.all_to_all(total.reshape(dp_count, local_sizes[role], D), 'dp', split...]
    dot_general x24 -> x17, matrix products: 61.4 us -> 24.8 us  [contract(): lax.dot_general(left, right, (((left_dim,), (right_dim,)), ((), ())), pre...]
    ppermute x17 -> x0, waiting for transfers between devices: 23.8 us -> none  [swap(): return lax.ppermute(values, axis, [(i, i ^ bit) for i in range(count)])]
    ppermute x17 -> x0, starting transfers between devices: 14.3 us -> none  [swap(): return lax.ppermute(values, axis, [(i, i ^ bit) for i in range(count)])]
    dot_general x9 -> x1, matrix products: 16.7 us -> 2.41 us  [per_device(): jnp.dot(attended_all, mid_grad_low, preferred_element_type=jnp.float32)]
    select_n x1 -> x2, other arithmetic: 5.85 us -> 15.9 us  [per_device(): jnp.where(inside, (target - dp_pos) % dp_count * pair_rows + place, slot_...]
    select_n x1 -> x0, other arithmetic: 9.44 us -> none  [per_device(): jnp.where(slot_place >= 0, (slot_place // pair_rows + dp_pos) % dp_count...]
  transfers between devices with their start and end apart: 22 -> 0, of which waited for: 5 -> 0; matrix products, arithmetic and copies ran while one was open for 21% -> 0% of each run, Pallas kernels for 10% -> 0%
where the time goes in v3:
time: 550 us; the launch traced here: 541 us
  Pallas kernels  367 us (67%)
  matrix products  68 us (12%)
  other arithmetic  54.9 us (10%)
  local copies, waits for them, and re-layouts  37.1 us (7%)
  between operations  13.5 us (2%)
    pallas_call x1, Pallas kernels, back(): pl.pallas_call(functools.partial(back_kernel, sizes), in_specs=[away] * 5...  178 us
    pallas_call x1, Pallas kernels, front(): pl.pallas_call(functools.partial(front_kernel, sizes), in_specs=[whole] *...  153 us
    pallas_call x4, Pallas kernels, feed(): pl.pallas_call(feed_kernel, grid=(hidden // width,), in_specs=[pl.BlockSp...  36.8 us
    dot_general x17, matrix products, contract(): lax.dot_general(left, right, (((left_dim,), (right_dim,)), ((), ())), pre...  24.8 us
    select_n x2, other arithmetic, per_device(): jnp.where(inside, (target - dp_pos) % dp_count * pair_rows + place, slot_...  15.9 us
    dot_general x3, matrix products, adapter_apply(): hidden = jnp.dot(features, down_matrix, precision=highest)  13.2 us
    unnamed x115, local copies, waits for them, and re-layouts  12.6 us

profile of v3, /device:TPU:0, one launch (start us, length us, event | category | flops | bytes accessed | tf_op | source)
XLA Modules:
  0.0 540.9 jit_solution(16528252430962664060)
XLA Ops:
  5.9 1.8 fusion.2
  26.1 6.0 %and_select_fusion.36.slot_place_ref = s32[1,576]{1,0:T(1,128)} fusion(s32[]{:T(128)} %bitcast.8, s32[]{:T(128)S(6)} %add.1808, s32[]{:T(128)} %bitcast.16, s32[]{:T(128)} %bitcast.10, s32[]{:T(128)S(6)} %add.1801, s32[]{:T(128)} %bitcast.15, s32[]{:T(128)} %bitcast.12, s32[]{:T(128)S(6)} %add.1793, s32[]{:T(128)} %bitcast.14, s32[]{:T(128)S(6)} %sub.1393, ...), kind=kLoop, calls=%fused_computation.500 | loop fusion | flops 223488 | bytes 2380 | tf_op jit(solution)/shard_map/jit(_where)/select_n | solution.py:1164
  32.0 5.8 %fusion.297 = f32[576]{0:T(1024)} fusion(s32[]{:T(128)} %bitcast.8, s32[]{:T(128)S(6)} %add.1808, s32[]{:T(128)} %bitcast.16, s32[]{:T(128)} %bitcast.10, s32[]{:T(128)S(6)} %add.1801, s32[]{:T(128)} %bitcast.15, s32[]{:T(128)} %bitcast.12, s32[]{:T(128)S(6)} %add.1793, s32[]{:T(128)} %bitcast.14, s32[]{:T(128)S(6)} %sub.1393, s32[]{:T(128)S(6)} %sub.1389, ...), kind=kLoop, calls=%fused_computation.796 | loop fusion | flops 224640 | bytes 2380 | tf_op jit(solution)/shard_map/convert_element_type | solution.py:1300
  37.8 2.3 reduce-window.6
  44.8 1.2 reverse
  50.1 9.9 %fusion.67.slot_place_ref = s32[576,1]{1,0:T(8,128)} fusion(s32[]{:T(128)} %bitcast.8, s32[]{:T(128)S(6)} %add.1808, s32[]{:T(128)} %bitcast.16, s32[]{:T(128)} %bitcast.10, s32[]{:T(128)S(6)} %add.1801, s32[]{:T(128)} %bitcast.15, s32[]{:T(128)} %bitcast.12, s32[]{:T(128)S(6)} %add.1793, s32[]{:T(128)} %bitcast.14, s32[]{:T(128)S(6)} %sub.1393, ...), kind=kLoop, calls=%fused_computation.242 | loop fusion | flops 223488 | bytes 2380 | tf_op jit(solution)/shard_map/jit(_where)/select_n | solution.py:1164
  60.0 1.2 fusion.62.order_qkv_ref
  62.0 1.2 fusion.20.bucket_ref
  63.2 1.0 broadcast_in_dim.69.segment_keys_ref
  64.2 2.0 fusion.37
  66.2 1.0 bitcast_convert_fusion.mine_ref
  67.2 1.6 fusion.4.normed_ref
  68.7 152.9 %front.1 = (bf16[4,576,768]{2,1,0:T(8,128)(2,1)}, bf16[4,192,768]{2,1,0:T(8,128)(2,1)}, bf16[4,768,768]{2,1,0:T(8,128)(2,1)}, bf16[4,768,768]{2,1,0:T(8,128)(2,1...) custom-call(bf16[576,768]{1,0:T(8,128)(2,1)} %bitcast_convert_fusion, ...), custom_call_target="tpu_custom_call" | custom-call | flops 32212254720 | bytes 67108864 | tf_op jit(solution)/shard_map/front/pallas_call | solution.py:385
  221.7 1.9 fusion.45
  224.9 1.2 multiply_reduce_fusion.2
  226.1 1.7 copy-done.12
  227.7 1.5 multiply_convert_fusion.4.rows_ref
  231.1 1.9 broadcast_in_dim.71.before_ref
  233.0 8.9 %feed.4 = (bf16[1024,768]{1,0:T(8,128)(2,1)S(1)}, bf16[1024,768]{1,0:T(8,128)(2,1)S(1)}, f32[1024,768]{1,0:T(8,128)}) custom-call(bf16[1024,768]{1,0:T(8,128)(2,1)} %multiply_convert_fusion.4.rows_ref, bf16[768,768]{1,0:T(8,128)(2,1)S(1)} %get-tuple-element.87.w_in_ref, bf16[768,768]{1,0:T(8,128)(2,1)S(1)} %get-tuple-element.83.w_down_ref, ...), custom_call_target="tpu_custom_call" | custom-call | flops 4831838208 | bytes 10485760 | tf_op jit(solution)/shard_map/feed/pallas_call | solution.py:1065
  241.9 1.2 copy-done.4
  243.2 9.3 %feed.5 = (bf16[1024,768]{1,0:T(8,128)(2,1)S(1)}, bf16[1024,768]{1,0:T(8,128)(2,1)S(1)}, f32[1024,768]{1,0:T(8,128)}) custom-call(bf16[1024,768]{1,0:T(8,128)(2,1)} %multiply_convert_fusion.4.rows_ref, bf16[768,768]{1,0:T(8,128)(2,1)S(1)} %get-tuple-element.88.w_in_ref, bf16[768,768]{1,0:T(8,128)(2,1)S(1)} %get-tuple-element.84.w_down_ref, ...), custom_call_target="tpu_custom_call" | custom-call | flops 4831838208 | bytes 10485760 | tf_op jit(solution)/shard_map/feed/pallas_call | solution.py:1065
  252.5 9.5 %feed.6 = (bf16[1024,768]{1,0:T(8,128)(2,1)S(1)}, bf16[1024,768]{1,0:T(8,128)(2,1)S(1)}, f32[1024,768]{1,0:T(8,128)}) custom-call(bf16[1024,768]{1,0:T(8,128)(2,1)} %multiply_convert_fusion.4.rows_ref, bf16[768,768]{1,0:T(8,128)(2,1)S(1)} %get-tuple-element.89.w_in_ref, bf16[768,768]{1,0:T(8,128)(2,1)S(1)} %get-tuple-element.85.w_down_ref, ...), custom_call_target="tpu_custom_call" | custom-call | flops 4831838208 | bytes 10485760 | tf_op jit(solution)/shard_map/feed/pallas_call | solution.py:1065
  262.0 1.1 copy-done
  263.1 1.2 copy-done.8
  264.3 9.1 %feed.7 = (bf16[1024,768]{1,0:T(8,128)(2,1)S(1)}, bf16[1024,768]{1,0:T(8,128)(2,1)S(1)}, f32[1024,768]{1,0:T(8,128)}) custom-call(bf16[1024,768]{1,0:T(8,128)(2,1)} %multiply_convert_fusion.4.rows_ref, bf16[768,768]{1,0:T(8,128)(2,1)S(1)} %get-tuple-element.90.w_in_ref, bf16[768,768]{1,0:T(8,128)(2,1)S(1)} %get-tuple-element.86.w_down_ref, ...), custom_call_target="tpu_custom_call" | custom-call | flops 4831838208 | bytes 10485760 | tf_op jit(solution)/shard_map/feed/pallas_call | solution.py:1065
  273.4 6.1 %fusion.368 = f32[1024,48]{0,1:T(8,128)S(1)} fusion(f32[1024,768]{1,0:T(8,128)} %get-tuple-element.42, f32[768,48]{0,1:T(8,128)S(1)} %reshape.4474), kind=kOutput, calls=%fused_computation.952 | convolution fusion | flops 452984832 | bytes 3489792 | tf_op jit(solution)/shard_map/jvp()/dot_general | solution.py:65
  280.2 1.9 fusion.171
  282.2 1.1 reshape.4480
  283.2 1.0 convolution_bitcast_fusion.6
  284.2 1.0 convolution_bitcast_fusion.5
  285.2 1.4 reshape.4486
  287.5 2.3 fusion.183
  289.9 3.3 multiply_add_fusion.1
  293.2 2.7 fusion.369
  296.0 4.5 add_convert_fusion
  300.5 1.1 reshape.4481
  301.9 1.1 convolution_bitcast_fusion.4
  303.3 1.0 fusion.179
  304.5 4.3 fusion
  308.9 1.5 fusion.19
  310.4 1.5 fusion.18
  311.9 1.5 fusion.17
  313.4 1.5 fusion.16
  314.9 1.4 multiply_convert_fusion
  316.4 1.4 multiply_convert_fusion.1
  317.9 1.8 multiply_convert_fusion.2
  319.7 1.4 multiply_convert_fusion.3
  321.2 2.5 pad_maximum_fusion.1.grad_down_ref
  323.6 1.5 fusion.15
  325.1 1.5 fusion.14
  326.6 1.5 fusion.13
  328.1 1.5 fusion.12
  329.5 2.6 pad_maximum_fusion.grad_in_ref
  332.2 1.4 fusion.354
  333.6 1.4 fusion.353
  335.0 1.4 fusion.352
  336.9 3.7 multiply_reduce_fusion
  341.3 3.3 fusion.1.mid_grad_ref
  344.6 2.6 convolution_convert_fusion.attended_grad_ref
  347.2 2.4 convolution_convert_fusion.9
  349.6 177.8 %back.1 = (f32[576,768]{1,0:T(8,128)}, bf16[1024,768]{1,0:T(8,128)(2,1)}, f32[48,128]{1,0:T(8,128)}) custom-call(bf16[4,192,768]{2,1,0:T(8,128)(2,1)} %bitcast.293, bf16[4,768,768]{2,1,0:T(8,128)(2,1)} %pad_maximum_fusion.grad_in_ref, bf16[4,768,768]{2,1,0:T(8,128)(2,1)} %pad_maximum_fusion.1.grad_down_ref, ...), custom_call_target="tpu_custom_call" | custom-call | flops 51539607552 | bytes 67108864 | tf_op jit(solution)/shard_map/back/pallas_call | solution.py:968
  530.4 6.8 %convert_bitcast_fusion = (bf16[1,576,768]{2,1,0:T(8,128)(2,1)}, f32[576,768]{1,0:T(8,128)}, f32[1,576,768]{2,1,0:T(8,128)}, f32[1,576,768]{2,1,0:T(8,128)}) fusion(f32[576]{0:T(1024)S(1)} %copy-done.37, f32[576,768]{1,0:T(8,128)} %get-tuple-element.56, f32[1,576,768]{2,1,0:T(8,128)} %param.20, f32[]{:T(128)} %bitcast.88, f32[1,576,768]{2,1,0:T(8,128)} %param.19, ...), kind=kLoop, calls=%fused_computation.85 | loop fusion | flops 7962624 | bytes 13273352 | tf_op jit(solution)/shard_map/broadcast_in_dim | solution.py:1319
  537.2 1.1 copy.154
  539.3 1.2 copy.155
  (210 shorter events, 32.6 us)
Async XLA Ops:
  0.6 8.3 %copy-start.32 = (f32[3616]{0:T(1024)S(1)}, f32[3616]{0:T(1024)}, u32[]{:S(2)}) copy-start(f32[3616]{0:T(1024)} %param.21) | copy-start | bytes 43396
  0.7 9.2 %copy-start.34 = (s32[2304]{0:T(1024)S(1)}, s32[2304]{0:T(1024)}, u32[]{:S(2)}) copy-start(s32[2304]{0:T(1024)} %param.17) | copy-start | bytes 27652
  0.7 8.0 %copy-start.43 = (s32[2047]{0:T(1024)S(1)}, s32[2047]{0:T(1024)}, u32[]{:S(2)}) copy-start(s32[2047]{0:T(1024)} %param.16) | copy-start | bytes 24568
  5.9 57.3 %copy-start.38 = (s32[1024]{0:T(1024)}, s32[1024]{0:T(1024)S(1)}, u32[]{:S(2)}) copy-start(s32[1024]{0:T(1024)S(1)} %dynamic_slice.16) | copy-start | bytes 12292
  49.9 16.2 %copy-start.18 = (f32[1,576,768]{2,1,0:T(8,128)S(1)}, f32[1,576,768]{2,1,0:T(8,128)}, u32[]{:S(2)}) copy-start(f32[1,576,768]{2,1,0:T(8,128)} %param.18) | copy-start | bytes 5308420
  64.2 3.0 copy-start.16
  221.6 1.9 copy-start.23
  221.6 1.9 copy-start.26
  224.2 5.0 slice-start
  224.8 4.4 slice-start.1
  226.1 1.7 copy-start.12
  227.7 2.8 slice-start.4
  229.2 1.6 slice-start.5
  241.9 1.2 copy-start.4
  252.5 9.5 %copy-start.6 = (bf16[1024,768]{1,0:T(8,128)(2,1)}, bf16[1024,768]{1,0:T(8,128)(2,1)S(1)}, u32[]{:S(2)}) copy-start(bf16[1024,768]{1,0:T(8,128)(2,1)S(1)} %get-tuple-element.48) | copy-start | bytes 4718596
  262.0 1.1 copy-start
  263.1 1.2 copy-start.8
  273.4 6.2 %copy-start.2 = (bf16[1024,768]{1,0:T(8,128)(2,1)}, bf16[1024,768]{1,0:T(8,128)(2,1)S(1)}, u32[]{:S(2)}) copy-start(bf16[1024,768]{1,0:T(8,128)(2,1)S(1)} %get-tuple-element.43) | copy-start | bytes 4718596
  273.4 6.2 %copy-start.10 = (bf16[1024,768]{1,0:T(8,128)(2,1)}, bf16[1024,768]{1,0:T(8,128)(2,1)S(1)}, u32[]{:S(2)}) copy-start(bf16[1024,768]{1,0:T(8,128)(2,1)S(1)} %get-tuple-element.50) | copy-start | bytes 4718596
  273.4 6.8 %copy-start.20 = (bf16[1024,768]{1,0:T(8,128)(2,1)S(1)}, bf16[1024,768]{1,0:T(8,128)(2,1)}, u32[]{:S(2)}) copy-start(bf16[1024,768]{1,0:T(8,128)(2,1)} %param.14) | copy-start | bytes 4718596
  279.5 0.7 copy-start.29
  289.9 3.3 copy-start.15
  293.2 2.8 copy-start.28
  293.2 2.8 copy-start.13
  293.2 2.8 copy-start.30
  293.2 2.8 copy-start.31
  295.9 7.0 %copy-start.44 = (f32[4,4,4,1]{2,1,0,3:T(4,128)S(1)}, f32[4,4,4,1]{2,1,0,3:T(4,128)}, u32[]{:S(2)}) copy-start(f32[4,4,4,1]{2,1,0,3:T(4,128)} %reshape.4525) | copy-start | bytes 772
  296.0 7.3 %copy-start.45 = (f32[4,12,1,1]{1,0,2,3:T(4,128)S(1)}, f32[4,12,1,1]{1,0,2,3:T(4,128)}, u32[]{:S(2)}) copy-start(f32[4,12,1,1]{1,0,2,3:T(4,128)} %reshape.4522) | copy-start | bytes 580
  296.0 8.3 %copy-start.36 = (f32[4,1,4,4]{3,1,2,0:T(1,128)S(1)}, f32[4,1,4,4]{3,1,2,0:T(1,128)}, u32[]{:S(2)}) copy-start(f32[4,1,4,4]{3,1,2,0:T(1,128)} %fusion.183) | copy-start | bytes 772
  304.5 4.3 copy-start.11
  308.9 1.5 copy-start.9
  310.4 1.5 copy-start.7
  311.9 1.5 copy-start.5
  311.9 3.0 slice-start.6
  313.4 1.5 slice-start.7
  316.4 1.5 copy-start.1
  317.9 1.8 copy-start.3
  321.2 2.5 copy-start.25
  328.0 4.1 slice-start.2
  329.5 2.7 slice-start.3
  335.0 1.9 copy-start.14
  336.9 3.7 copy-start.39
  341.3 3.3 copy-start.27
  344.6 2.6 copy-start.21
  344.6 2.6 copy-start.24
  349.6 179.4 %copy-start.33 = (f32[3616]{0:T(1024)S(1)}, f32[3616]{0:T(1024)}, u32[]{:S(2)}) copy-start(f32[3616]{0:T(1024)} %param.21) | copy-start | bytes 43396
  349.6 179.5 %copy-start.40 = (f32[3616]{0:T(1024)S(1)}, f32[3616]{0:T(1024)}, u32[]{:S(2)}) copy-start(f32[3616]{0:T(1024)} %param.23) | copy-start | bytes 43396
  349.6 179.5 %copy-start.41 = (f32[3616]{0:T(1024)S(1)}, f32[3616]{0:T(1024)}, u32[]{:S(2)}) copy-start(f32[3616]{0:T(1024)} %param.22) | copy-start | bytes 43396
  349.6 180.2 %copy-start.42 = (f32[1696]{0:T(1024)S(1)}, f32[1696]{0:T(1024)}, u32[]{:S(2)}) copy-start(f32[1696]{0:T(1024)} %param.24) | copy-start | bytes 20356
  349.6 180.8 %copy-start.19 = (f32[1,576,768]{2,1,0:T(8,128)S(1)}, f32[1,576,768]{2,1,0:T(8,128)}, u32[]{:S(2)}) copy-start(f32[1,576,768]{2,1,0:T(8,128)} %param.18) | copy-start | bytes 5308420
  349.6 180.8 %copy-start.37 = (f32[576]{0:T(1024)S(1)}, f32[576]{0:T(1024)}, u32[]{:S(2)}) copy-start(f32[576]{0:T(1024)} %fusion.297) | copy-start | bytes 6916
  529.8 7.4 %copy-start.35 = (f32[3616]{0:T(1024)}, f32[3616]{0:T(1024)S(1)}, u32[]{:S(2)}) copy-start(f32[3616]{0:T(1024)S(1)} %get-tuple-element.163) | copy-start | bytes 43396
  530.4 6.8 %copy-start.22 = (bf16[1024,768]{1,0:T(8,128)(2,1)S(1)}, bf16[1024,768]{1,0:T(8,128)(2,1)}, u32[]{:S(2)}) copy-start(bf16[1024,768]{1,0:T(8,128)(2,1)} %get-tuple-element.154) | copy-start | bytes 4718596
  537.2 2.0 copy-start.17

commit v4 on v3

--- a/solution.py
+++ b/solution.py
@@ -54,22 +54,25 @@
     return (gain_one, gain_two, adapter, table_flat.reshape(NB, H))
 
 
-def adapter_apply(features, adapter):
+def adapter_factors(adapter):
     mix, down_left, down_right, up_left, up_right = adapter
-    down_matrix = jnp.einsum(
-        "iab,ip,iq->apbq", mix, down_left, down_right, precision=highest
-    ).reshape(D, R)
-    up_matrix = jnp.einsum("iab,iq,ip->aqbp", mix, up_left, up_right, precision=highest).reshape(
-        R, D
-    )
-    hidden = jnp.dot(features, down_matrix, precision=highest)
-    return features + jnp.dot(jax.nn.gelu(hidden, approximate=False), up_matrix, precision=highest)
-
-
-def rms_norm(values, gain):
-    return (
-        values * lax.rsqrt(jnp.mean(values * values, axis=-1, keepdims=True) + norm_epsilon) * gain
-    )
+    eye = jnp.eye(PHM, dtype=jnp.float32)
+    left = mix.transpose(2, 0, 1)[:, None] * down_right.T[None, :, :, None]
+    right = (eye[None, :, :, None] * down_left[:, None, None, :]).reshape(PHM * PHM, D)
+    wide = mix.transpose(1, 0, 2)[:, None] * up_left.T[None, :, :, None]
+    tall = (eye[None, :, :, None] * up_right[:, None, None, :]).reshape(PHM * PHM, D)
+    return (left.reshape(R, PHM * PHM), right, wide.reshape(R, PHM * PHM), tall)
+
+
+def normal_parts(values):
+    size = jnp.abs(values)
+    shrink = 1.0 / (1.0 + (0.3275911 * math.sqrt(0.5)) * size)
+    bell = jnp.exp(-0.5 * values * values)
+    series = 0.5 * 1.061405429
+    for term in (-1.453152027, 1.421413741, -0.284496736, 0.254829592):
+        series = series * shrink + 0.5 * term
+    tail = series * shrink * bell
+    return jnp.where(values >= 0.0, 1.0 - tail, tail), bell * (1.0 / math.sqrt(2.0 * math.pi))
 
 
 def contract(left, right, left_dim, right_dim):
@@ -135,6 +138,116 @@
     return jnp.where(hit, 1.0, 0.0).astype(jnp.bfloat16)
 
 
+def plan_kernel(dp_count, pair_rows, local_sizes, *refs):
+    roles = len(local_sizes)
+    owner_refs, slot_ref, spread_ref = refs[:roles], refs[roles], refs[roles + 1]
+    order_refs, place_refs = refs[roles + 2 : 2 * roles + 2], refs[2 * roles + 2 :]
+    dp_pos = lax.axis_index("dp").astype(jnp.float32)
+
+    def quotient(values):
+        return jnp.floor((values + 0.5) * (1.0 / dp_count))
+
+    def remainder(values):
+        return values - dp_count * quotient(values)
+
+    owners = [ref[...].astype(jnp.float32) for ref in owner_refs]
+
+    def stats(who):
+        counts = [
+            jnp.sum(jnp.where(row == who, 1.0, 0.0), axis=1, keepdims=True) for row in owners
+        ]
+        starts = [jnp.sum(jnp.where(row < who, 1.0, 0.0), axis=1, keepdims=True) for row in owners]
+        return counts, starts
+
+    def hits(first, number, target):
+        return quotient(first + number - 1.0 - target) - quotient(first - 1.0 - target)
+
+    counts, starts = stats(jnp.full((1, 1), dp_pos))
+    slot = lax.broadcasted_iota(jnp.int32, slot_ref.shape, 1).astype(jnp.float32)
+    found = jnp.full(slot_ref.shape, -1.0)
+    low = jnp.zeros((1, 1), jnp.float32)
+    for role in range(roles):
+        rank = slot - low
+        target = remainder(starts[role] + rank)
+        place = quotient(rank)
+        for other in range(role):
+            place = place + hits(starts[other], counts[other], target)
+        found = jnp.where(
+            (rank >= 0.0) & (rank < counts[role]),
+            remainder(target - dp_pos) * pair_rows + place,
+            found,
+        )
+        low = low + counts[role]
+    slot_ref[...] = found.astype(jnp.int32)
+
+    column = lax.broadcasted_iota(jnp.int32, (dp_count, 1), 0).astype(jnp.float32)
+    counts, starts = stats(remainder(dp_pos - column))
+    pair = lax.broadcasted_iota(jnp.int32, spread_ref.shape, 1).astype(jnp.float32)
+    found = jnp.full(spread_ref.shape, -1.0)
+    passed = jnp.zeros((dp_count, 1), jnp.float32)
+    for role in range(roles):
+        number = hits(starts[role], counts[role], dp_pos)
+        first = starts[role] + remainder(dp_pos - starts[role])
+        rank = pair - passed
+        local = sum(local_sizes[:role]) + quotient(first) + rank
+        found = jnp.where((rank >= 0.0) & (rank < number), local, found)
+        passed = passed + number
+    spread_ref[...] = found.astype(jnp.int32)
+
+    counts, starts = stats(column)
+    for role in range(roles):
+        width = owners[role].shape[1]
+        before = starts[role]
+        for c0 in range(0, width, TILE):
+            c1 = min(c0 + TILE, width)
+            hot = jnp.where(owners[role][:, c0:c1] == column, 1.0, 0.0)
+            shape = (c1 - c0, c1 - c0)
+            above = lax.broadcasted_iota(jnp.int32, shape, 0) < lax.broadcasted_iota(
+                jnp.int32, shape, 1
+            )
+            rank = jnp.dot(
+                hot.astype(jnp.bfloat16),
+                jnp.where(above, 1.0, 0.0).astype(jnp.bfloat16),
+                preferred_element_type=jnp.float32,
+            )
+            number = jnp.sum(hot * (rank + before), axis=0, keepdims=True)
+            before = before + jnp.sum(hot, axis=1, keepdims=True)
+            target, row = remainder(number), quotient(number)
+            order = remainder(dp_pos - target) * local_sizes[role] + row
+            place = remainder(target - dp_pos) * local_sizes[role] + row
+            order_refs[role][:, c0:c1] = order.astype(jnp.int32)
+            place_refs[role][:, c0:c1] = place.astype(jnp.int32)
+
+
+def plan(owners, sizes, local_sizes, capacity, pair_rows):
+    dp_count = lax.axis_size("dp")
+    rows, start = [], 0
+    for size in sizes:
+        rows.append(owners[start : start + size][None, :])
+        start += size
+    outs = pl.pallas_call(
+        functools.partial(plan_kernel, dp_count, pair_rows, local_sizes),
+        out_shape=[
+            jax.ShapeDtypeStruct((1, capacity), jnp.int32),
+            jax.ShapeDtypeStruct((dp_count, pair_rows), jnp.int32),
+        ]
+        + [jax.ShapeDtypeStruct((1, size), jnp.int32) for size in sizes] * 2,
+        name="plan",
+    )(*rows)
+    return outs[0], outs[1], outs[2 : 2 + len(sizes)], outs[2 + len(sizes) :]
+
+
+def true_group(positions, group, tensor_count):
+    flips = positions + (tensor_count - 1 - positions[0],)
+    found = flips[0]
+    for g in range(1, tensor_count):
+        found = found + (flips[g] - flips[0]) * (
+            lax.div(group + tensor_count - g, tensor_count)
+            - lax.div(group + tensor_count - g - 1, tensor_count)
+        )
+    return found
+
+
 def front_kernel(
     sizes,
     mine_ref,
@@ -144,10 +257,11 @@
     order_out_ref,
     order_in_ref,
     order_down_ref,
-    normed_ref,
-    bias_ref,
-    segment_keys_ref,
-    segment_queries_ref,
+    tokens_ref,
+    gain_ref,
+    table_ref,
+    bucket_ref,
+    segment_ref,
     w_qkv_ref,
     w_out_ref,
     w_in_ref,
@@ -155,10 +269,13 @@
     projected_ref,
     attended_ref,
     scale_ref,
+    normed_ref,
     exp_ref,
     sent,
     received,
     spread,
+    bias,
+    segment_keys,
     buf_qkv,
     buf_out,
     buf_in,
@@ -180,12 +297,13 @@
 ):
     dp_count, pair_rows = sent.shape[0], sent.shape[1]
     tensor_count = w_qkv_ref.shape[0]
-    heads = bias_ref.shape[0]
+    heads = scale_ref.shape[0]
     group_heads = heads // tensor_count
     head_rows = group_heads * HS
     dp_pos, tensor_pos = lax.axis_index("dp"), lax.axis_index("tensor")
-    core_peer = (dp_pos, tensor_pos + 1 - 2 * lax.rem(tensor_pos, 2))
-    far_peer = (dp_pos, lax.rem(tensor_pos + 2, tensor_count))
+    core_pos = tensor_pos + 1 - 2 * lax.rem(tensor_pos, 2)
+    far_pos = lax.rem(tensor_pos + 2, tensor_count)
+    core_peer, far_peer = (dp_pos, core_pos), (dp_pos, far_pos)
 
     def dp_peer(m):
         return (lax.rem(dp_pos + m, dp_count), tensor_pos)
@@ -207,7 +325,7 @@
         pl.semaphore_signal(barrier, inc=1, device_id=peer, device_id_type=MESH)
 
     place = slot_place_ref[...]
-    mine = mine_ref[...]
+    mine = mine_ref[...].astype(jnp.bfloat16)
     for m in range(dp_count):
         hot = one_hot(place - m * pair_rows, (pair_rows, mine.shape[0]), 0)
         sent[m] = jnp.dot(hot, mine, preferred_element_type=jnp.float32).astype(jnp.bfloat16)
@@ -225,12 +343,29 @@
 
     each_peer(lambda m: deal(m).start())
     received[0] = sent[0]
+
+    for r0 in range(0, SEQ, 128):
+        values = tokens_ref[r0 : r0 + 128, :].astype(jnp.float32)
+        inverse = lax.rsqrt(jnp.mean(values * values, axis=1, keepdims=True) + norm_epsilon)
+        normed_ref[r0 : r0 + 128, :] = (values * inverse * gain_ref[...]).astype(jnp.bfloat16)
+    rest = table_ref[...]
+    hot = one_hot(bucket_ref[...], (NB, 2 * SEQ), 0)
+    biases = jnp.zeros((rest.shape[0], 2 * SEQ), jnp.float32)
+    for _ in range(3):
+        part = rest.astype(jnp.bfloat16)
+        rest = rest - part.astype(jnp.float32)
+        biases = biases + jnp.dot(part, hot, preferred_element_type=jnp.float32)
+    for head in range(heads):
+        bias[head] = biases[head : head + 1, :]
+    segment_keys[...] = jnp.broadcast_to(segment_ref[...], (TILE, SEQ)).T
+
     each_peer(lambda m: deal(m).wait())
     rows = spread.shape[0]
-    hot = one_hot(spread_place_ref[...], (rows, dp_count * pair_rows), 0)
-    spread[...] = jnp.dot(
-        hot, received[...].reshape(dp_count * pair_rows, D), preferred_element_type=jnp.float32
-    ).astype(jnp.bfloat16)
+    total = jnp.zeros((rows, D), jnp.float32)
+    for m in range(dp_count):
+        hot = one_hot(spread_place_ref[m : m + 1, :], (rows, pair_rows), 0)
+        total = total + jnp.dot(hot, received[m], preferred_element_type=jnp.float32)
+    spread[...] = total.astype(jnp.bfloat16)
 
     bufs = (buf_qkv, buf_out, buf_in, buf_down)
     orders = (order_qkv_ref, order_out_ref, order_in_ref, order_down_ref)
@@ -257,12 +392,11 @@
         each_peer(lambda m: gather(role, m).wait())
         count = bufs[role].shape[1]
         source = bufs[role][...].reshape(dp_count * count, D)
-        step = 192
+        step = 256
         for r0 in range(0, sizes[role], step):
-            hot = one_hot(orders[role][r0 : r0 + step, :], (step, dp_count * count), 1)
-            stages[role][r0 : r0 + step, :] = jnp.dot(
-                hot, source, preferred_element_type=jnp.float32
-            ).astype(jnp.bfloat16)
+            r1 = min(r0 + step, sizes[role])
+            hot = one_hot(orders[role][:, r0:r1], (dp_count * count, r1 - r0), 0)
+            stages[role][r0:r1, :] = contract(hot, source, 0, 0).astype(jnp.bfloat16)
 
     def share(role, part):
         src, slot, peer = (
@@ -298,6 +432,9 @@
     start_gather(1)
     start_gather(2)
 
+    def true_head(group, head):
+        return true_group((tensor_pos, core_pos, far_pos), group, tensor_count) * group_heads + head
+
     def head_step(i, carry):
         group, head = lax.div(i, group_heads), lax.rem(i, group_heads)
 
@@ -340,13 +477,13 @@
         def _():
             save(i - 2, slot).wait()
 
-        bias_window(bias_ref[i], window)
+        bias_window(bias[true_head(group, head)], window)
         attended, scale = attend_head(
             head_part(0),
             head_part(1),
             head_part(2),
-            segment_keys_ref,
-            segment_queries_ref,
+            segment_keys,
+            segment_ref,
             window,
             scores,
             exp_stage.at[slot],
@@ -373,10 +510,21 @@
             keep(role).wait()
 
 
-def front(mine, slot_place, spread_place, orders, local_sizes, pair_rows, normed, bias, segments):
+def front(
+    mine,
+    slot_place,
+    spread_place,
+    orders,
+    local_sizes,
+    tokens,
+    gain,
+    table,
+    bucket_place,
+    segments,
+):
     dp_count, tensor_count = lax.axis_size("dp"), lax.axis_size("tensor")
-    sizes = [order.shape[0] for order in orders]
-    heads = bias.shape[0]
+    sizes = [order.shape[1] for order in orders]
+    pair_rows = spread_place.shape[1]
     low = jnp.bfloat16
     dma = pltpu.SemaphoreType.DMA
     roles = len(sizes)
@@ -384,19 +532,22 @@
     away = pl.BlockSpec(memory_space=pl.ANY)
     return pl.pallas_call(
         functools.partial(front_kernel, sizes),
-        in_specs=[whole] * 11,
-        out_specs=[whole, away, away, away, whole, whole, whole, away],
+        in_specs=[whole] * 12,
+        out_specs=[whole, away, away, away, whole, whole, whole, whole, away],
         out_shape=[jax.ShapeDtypeStruct((tensor_count, size, D), low) for size in sizes]
         + [
             jax.ShapeDtypeStruct((tensor_count, sizes[0], SEQ), low),
-            jax.ShapeDtypeStruct((heads * HS, SEQ), low),
-            jax.ShapeDtypeStruct((heads, 1, SEQ), jnp.float32),
-            jax.ShapeDtypeStruct((heads, SEQ, SEQ), low),
+            jax.ShapeDtypeStruct((H * HS, SEQ), low),
+            jax.ShapeDtypeStruct((H, 1, SEQ), jnp.float32),
+            jax.ShapeDtypeStruct((SEQ, D), low),
+            jax.ShapeDtypeStruct((H, SEQ, SEQ), low),
         ],
         scratch_shapes=[
             pltpu.VMEM((dp_count, pair_rows, D), low),
             pltpu.VMEM((dp_count, pair_rows, D), low),
             pltpu.VMEM((sum(local_sizes), D), low),
+            pltpu.VMEM((H, 1, 2 * SEQ), jnp.float32),
+            pltpu.VMEM((SEQ, TILE), jnp.float32),
         ]
         + [pltpu.VMEM((dp_count, size, D), low) for size in local_sizes]
         + [pltpu.VMEM((size, D), low) for size in sizes[1:]]
@@ -417,20 +568,21 @@
             collective_id=1, has_side_effects=True, vmem_limit_bytes=56 * 1024 * 1024
         ),
         cost_estimate=pl.CostEstimate(
-            flops=10 * heads * SEQ * SEQ * 256,
+            flops=10 * H * SEQ * SEQ * 256,
             bytes_accessed=64 * 1024 * 1024,
-            transcendentals=heads * SEQ * SEQ,
+            transcendentals=H * SEQ * SEQ,
         ),
         name="front",
     )(
         mine,
-        slot_place[None, :],
-        spread_place[None, :],
-        *[order[:, None] for order in orders],
-        normed,
-        bias,
-        jnp.broadcast_to(segments[:, None], (SEQ, TILE)),
-        segments[None, :],
+        slot_place,
+        spread_place,
+        *orders,
+        tokens,
+        gain[None, :],
+        table,
+        bucket_place,
+        segments.astype(jnp.float32)[None, :],
     )
 
 
@@ -535,6 +687,7 @@
     owned_ref,
     input_grad_ref,
     small_total_ref,
+    bucket_hot,
     proj,
     proj_grad,
     normed_grad,
@@ -722,6 +875,7 @@
     for role in (3, 2, 1):
         load(role, 2).start()
         load(role, 0).start()
+    bucket_hot[...] = one_hot(bucket_ref[...], (TILE, 2 * SEQ), 0)
     normed_grad[...] = jnp.zeros_like(normed_grad)
     small_own[0:TABLE_ROW, :] = small_ref[...]
     small_own[TABLE_ROW:SMALL_ROWS, :] = jnp.zeros((SMALL_ROWS - TABLE_ROW, TILE), jnp.float32)
@@ -780,20 +934,16 @@
             score_grads,
             store,
         )
-        flips = (tensor_pos, core_pos, far_pos, tensor_count - 1 - tensor_pos)
-        true_group = flips[0]
-        for g in range(1, tensor_count):
-            true_group = true_group + (flips[g] - flips[0]) * (
-                lax.div(group + tensor_count - g, tensor_count)
-                - lax.div(group + tensor_count - g - 1, tensor_count)
-            )
+        place = (
+            true_group((tensor_pos, core_pos, far_pos), group, tensor_count) * group_heads + part_head
+        )
         high = offset_grad.astype(low)
         rest = (offset_grad - high.astype(jnp.float32)).astype(low)
         both = jnp.concatenate([high, rest] + [jnp.zeros_like(high)] * 6, axis=0)
-        sums = jnp.dot(both, bucket_ref[...], preferred_element_type=jnp.float32)
+        sums = contract(both, bucket_hot[...], 1, 1)
         line = lax.broadcasted_iota(jnp.int32, (SMALL_ROWS - TABLE_ROW, TILE), 0)
         small_own[TABLE_ROW:SMALL_ROWS, :] += jnp.where(
-            line == true_group * group_heads + part_head,
+            line == place,
             jnp.broadcast_to(sums[0:1] + sums[1:2], (SMALL_ROWS - TABLE_ROW, TILE)),
             0.0,
         )
@@ -897,12 +1047,8 @@
 
     values = spread[...]
     for m in range(dp_count):
-        hot = one_hot(
-            spread_place_ref[m * pair_rows : (m + 1) * pair_rows, :],
-            (pair_rows, values.shape[0]),
-            1,
-        )
-        sent[m] = jnp.dot(hot, values, preferred_element_type=jnp.float32).astype(low)
+        hot = one_hot(spread_place_ref[m : m + 1, :], (values.shape[0], pair_rows), 0)
+        sent[m] = contract(hot, values, 0, 0).astype(low)
 
     def back_copy(m):
         return pltpu.make_async_remote_copy(
@@ -917,11 +1063,8 @@
     each_peer(lambda m: back_copy(m).start())
     received[0] = sent[0]
     each_peer(lambda m: back_copy(m).wait())
-    capacity = owned_ref.shape[0]
-    hot = one_hot(slot_place_ref[...], (capacity, dp_count * pair_rows), 1)
-    owned_ref[...] = jnp.dot(
-        hot, received[...].reshape(dp_count * pair_rows, D), preferred_element_type=jnp.float32
-    )
+    hot = one_hot(slot_place_ref[...], (dp_count * pair_rows, owned_ref.shape[0]), 0)
+    owned_ref[...] = contract(hot, received[...].reshape(dp_count * pair_rows, D), 0, 0)
     for role in range(len(gots)):
         core_copy(role, 1).wait_send()
         core_copy(role, 3).wait_send()
@@ -941,30 +1084,24 @@
     mid_grad,
     gain,
     small,
-    buckets,
+    bucket_place,
     places,
     local_sizes,
-    pair_rows,
     spread_place,
     slot_place,
 ):
     dp_count, tensor_count = lax.axis_size("dp"), lax.axis_size("tensor")
-    sizes = [place.shape[0] for place in places]
-    capacity = slot_place.shape[0]
+    sizes = [place.shape[1] for place in places]
+    capacity, pair_rows = slot_place.shape[1], spread_place.shape[1]
     low = jnp.bfloat16
     dma = pltpu.SemaphoreType.DMA
     roles = len(sizes)
     whole = pl.BlockSpec(memory_space=pltpu.VMEM)
     away = pl.BlockSpec(memory_space=pl.ANY)
     parts = [pltpu.VMEM((size, D), low) for size in sizes]
-    padded = [pltpu.VMEM((dp_count * size, D), low) for size in local_sizes]
     padded = [
         pltpu.VMEM((max(dp_count * size, full), D), low) for size, full in zip(local_sizes, sizes)
     ]
-    bucket_place = jnp.concatenate([jnp.full((1,), -1, jnp.int32), buckets[::-1]])
-    bucket_hot = (
-        bucket_place[:, None] == jnp.arange(TILE, dtype=jnp.int32)[None, :]
-    ).astype(low)
     return pl.pallas_call(
         functools.partial(back_kernel, sizes),
         in_specs=[away] * 5 + [whole] * 16,
@@ -975,6 +1112,7 @@
             jax.ShapeDtypeStruct((SMALL_ROWS, TILE), jnp.float32),
         ],
         scratch_shapes=[
+            pltpu.VMEM((TILE, 2 * SEQ), low),
             pltpu.VMEM((sizes[0], SEQ), low),
             pltpu.VMEM((sizes[0], SEQ), low),
             pltpu.VMEM((SEQ, D), jnp.float32),
@@ -1032,63 +1170,280 @@
         mid_grad,
         gain[None, :],
         small,
-        bucket_hot,
-        *[place[None, :] for place in places],
-        spread_place[:, None],
-        slot_place[:, None],
+        bucket_place,
+        *places,
+        spread_place,
+        slot_place,
     )
 
 
-def feed_kernel(rows_ref, w_in_ref, w_down_ref, before_ref, activ_ref, slope_ref, out_ref):
+FEED_WIDTH = 384
+
+
+def feed_kernel(
+    attended_ref,
+    w_out_ref,
+    tokens_ref,
+    gain_ref,
+    cotangent_ref,
+    left_ref,
+    right_ref,
+    wide_ref,
+    tall_ref,
+    w_in_ref,
+    w_down_ref,
+    activ_ref,
+    slope_ref,
+    normed_ref,
+    mid_ref,
+    layer_out_ref,
+    ffn_grad_ref,
+    left_grad_ref,
+    right_grad_ref,
+    wide_grad_ref,
+    tall_grad_ref,
+    ffn_out,
+):
+    low = jnp.bfloat16
     row_tile = 256
+    tiles = range(0, SEQ, row_tile)
 
     @pl.when(pl.program_id(0) == 0)
     def _():
-        out_ref[...] = before_ref[...]
-
-    for r0 in range(0, SEQ, row_tile):
-        pre = contract(rows_ref[r0 : r0 + row_tile, :], w_in_ref[...], 1, 1)
-        cdf = 0.5 * (1.0 + lax.erf(pre * (1.0 / math.sqrt(2.0))))
-        pdf = jnp.exp(-0.5 * pre * pre) * (1.0 / math.sqrt(2.0 * math.pi))
-        activ = (pre * cdf).astype(jnp.bfloat16)
-        activ_ref[r0 : r0 + row_tile, :] = activ
-        slope_ref[r0 : r0 + row_tile, :] = (cdf + pre * pdf).astype(jnp.bfloat16)
-        out_ref[r0 : r0 + row_tile, :] += jnp.dot(
-            activ, w_down_ref[...], preferred_element_type=jnp.float32
-        )
-
-
-def feed(rows, w_in, w_down, before):
-    width = 384
-    tokens = rows.shape[0]
-    hidden = w_in.shape[0]
-    return pl.pallas_call(
+        for r0 in tiles:
+            rows = slice(r0, r0 + row_tile)
+            attn = jnp.dot(
+                attended_ref[:, rows].T, w_out_ref[...], preferred_element_type=jnp.float32
+            )
+            mid = tokens_ref[rows, :].astype(jnp.float32) + attn
+            mid_ref[rows, :] = mid
+            inverse = lax.rsqrt(jnp.mean(mid * mid, axis=1, keepdims=True) + norm_epsilon)
+            normed_ref[rows, :] = (mid * inverse * gain_ref[...]).astype(low)
+            ffn_out[rows, :] = jnp.zeros((row_tile, D), jnp.float32)
+
+    for r0 in tiles:
+        rows = slice(r0, r0 + row_tile)
+        pre = contract(normed_ref[rows, :], w_in_ref[...], 1, 1)
+        cdf, density = normal_parts(pre)
+        activ = (pre * cdf).astype(low)
+        activ_ref[rows, :] = activ
+        slope_ref[rows, :] = (cdf + pre * density).astype(low)
+        ffn_out[rows, :] += jnp.dot(activ, w_down_ref[...], preferred_element_type=jnp.float32)
+
+    @pl.when(pl.program_id(0) == pl.num_programs(0) - 1)
+    def _():
+        down = jnp.dot(
+            left_ref[...], right_ref[...], precision=highest, preferred_element_type=jnp.float32
+        ).astype(low)
+        up = jnp.dot(
+            wide_ref[...], tall_ref[...], precision=highest, preferred_element_type=jnp.float32
+        ).astype(low)
+        down_grad = jnp.zeros((R, D), jnp.float32)
+        up_grad = jnp.zeros((R, D), jnp.float32)
+        for r0 in tiles:
+            rows = slice(r0, r0 + row_tile)
+            ffn = ffn_out[rows, :]
+            ffn_low = ffn.astype(low)
+            grad_low = cotangent_ref[rows, :]
+            zed = contract(ffn_low, down, 1, 1)
+            cdf, density = normal_parts(zed)
+            hidden = (zed * cdf).astype(low)
+            added = jnp.dot(hidden, up, preferred_element_type=jnp.float32)
+            layer_out_ref[rows, :] = (mid_ref[rows, :] + ffn + added).astype(low)
+            zed_grad = contract(grad_low, up, 1, 1) * (cdf + zed * density)
+            zed_low = zed_grad.astype(low)
+            ffn_grad_ref[rows, :] = (
+                grad_low.astype(jnp.float32)
+                + jnp.dot(zed_low, down, preferred_element_type=jnp.float32)
+            ).astype(low)
+            up_grad = up_grad + contract(hidden, grad_low, 0, 0)
+            down_grad = down_grad + contract(zed_low, ffn_low, 0, 0)
+
+        def exact(left, right, left_dim, right_dim):
+            return lax.dot_general(
+                left,
+                right,
+                (((left_dim,), (right_dim,)), ((), ())),
+                precision=highest,
+                preferred_element_type=jnp.float32,
+            )
+
+        left_grad_ref[...] = exact(down_grad, right_ref[...], 1, 1)
+        right_grad_ref[...] = exact(left_ref[...], down_grad, 0, 0)
+        wide_grad_ref[...] = exact(up_grad, tall_ref[...], 1, 1)
+        tall_grad_ref[...] = exact(wide_ref[...], up_grad, 0, 0)
+
+
+def feed(attended, w_out, tokens, gain, cotangent, factors, w_in, w_down):
+    def fixed(*shape):
+        return pl.BlockSpec(shape, lambda j: (0,) * len(shape))
+
+    def stripe():
+        return pl.BlockSpec((FEED_WIDTH, D), lambda j: (j, 0))
+
+    low = jnp.bfloat16
+    factor_specs = [fixed(*factor.shape) for factor in factors]
+    outs = pl.pallas_call(
         feed_kernel,
-        grid=(hidden // width,),
+        grid=(FF // FEED_WIDTH,),
         in_specs=[
-            pl.BlockSpec((tokens, D), lambda j: (0, 0)),
-            pl.BlockSpec((width, D), lambda j: (j, 0)),
-            pl.BlockSpec((width, D), lambda j: (j, 0)),
-            pl.BlockSpec((tokens, D), lambda j: (0, 0)),
+            fixed(D, SEQ),
+            fixed(D, D),
+            fixed(SEQ, D),
+            fixed(1, D),
+            fixed(SEQ, D),
+            *factor_specs,
+            stripe(),
+            stripe(),
         ],
         out_specs=[
-            pl.BlockSpec((tokens, width), lambda j: (0, j)),
-            pl.BlockSpec((tokens, width), lambda j: (0, j)),
-            pl.BlockSpec((tokens, D), lambda j: (0, 0)),
+            pl.BlockSpec((SEQ, FEED_WIDTH), lambda j: (0, j)),
+            pl.BlockSpec((SEQ, FEED_WIDTH), lambda j: (0, j)),
+            fixed(SEQ, D),
+            fixed(SEQ, D),
+            fixed(SEQ, D),
+            fixed(SEQ, D),
+            *factor_specs,
         ],
         out_shape=[
-            jax.ShapeDtypeStruct((tokens, hidden), jnp.bfloat16),
-            jax.ShapeDtypeStruct((tokens, hidden), jnp.bfloat16),
-            jax.ShapeDtypeStruct((tokens, D), jnp.float32),
+            jax.ShapeDtypeStruct((SEQ, FF), low),
+            jax.ShapeDtypeStruct((SEQ, FF), low),
+            jax.ShapeDtypeStruct((SEQ, D), low),
+            jax.ShapeDtypeStruct((SEQ, D), jnp.float32),
+            jax.ShapeDtypeStruct((SEQ, D), low),
+            jax.ShapeDtypeStruct((SEQ, D), low),
+            *[jax.ShapeDtypeStruct(factor.shape, jnp.float32) for factor in factors],
         ],
+        scratch_shapes=[pltpu.VMEM((SEQ, D), jnp.float32)],
         compiler_params=pltpu.CompilerParams(vmem_limit_bytes=VMEM_LIMIT),
         cost_estimate=pl.CostEstimate(
-            flops=8 * tokens * hidden * D,
-            bytes_accessed=10 * 1024 * 1024,
-            transcendentals=2 * tokens * hidden,
+            flops=6 * SEQ * FF * D, bytes_accessed=32 * 1024 * 1024, transcendentals=2 * SEQ * FF
         ),
         name="feed",
-    )(rows, w_in, w_down, before)
+    )(attended, w_out, tokens, gain[None, :], cotangent, *factors, w_in, w_down)
+    return outs[:6], tuple(outs[6:])
+
+
+def feed_back_kernel(
+    ffn_grad_ref,
+    normed_ref,
+    mid_ref,
+    gain_ref,
+    cotangent_ref,
+    attended_ref,
+    w_out_ref,
+    activ_ref,
+    slope_ref,
+    w_in_ref,
+    w_down_ref,
+    in_grad_ref,
+    down_grad_ref,
+    mid_grad_ref,
+    gain_grad_ref,
+    out_grad_ref,
+    attended_grad_ref,
+    normed_grad,
+    pre_grad,
+):
+    low = jnp.bfloat16
+    row_tile = 256
+    tiles = range(0, SEQ, row_tile)
+
+    @pl.when(pl.program_id(0) == 0)
+    def _():
+        normed_grad[...] = jnp.zeros_like(normed_grad)
+
+    for r0 in tiles:
+        rows = slice(r0, r0 + row_tile)
+        grad = contract(ffn_grad_ref[rows, :], w_down_ref[...], 1, 1)
+        grad = (grad * slope_ref[rows, :].astype(jnp.float32)).astype(low)
+        pre_grad[rows, :] = grad
+        normed_grad[rows, :] += jnp.dot(grad, w_in_ref[...], preferred_element_type=jnp.float32)
+    for c0 in range(0, FEED_WIDTH, TILE):
+        columns = slice(c0, c0 + TILE)
+        down_grad_ref[columns, :] = jnp.dot(
+            activ_ref[:, columns].T, ffn_grad_ref[...], preferred_element_type=jnp.float32
+        ).astype(low)
+        in_grad_ref[columns, :] = jnp.dot(
+            pre_grad[:, columns].T, normed_ref[...], preferred_element_type=jnp.float32
+        ).astype(low)
+
+    @pl.when(pl.program_id(0) == pl.num_programs(0) - 1)
+    def _():
+        gain_grad = jnp.zeros((1, D), jnp.float32)
+        for r0 in tiles:
+            rows = slice(r0, r0 + row_tile)
+            mid = mid_ref[rows, :]
+            grads = normed_grad[rows, :]
+            inverse = lax.rsqrt(jnp.mean(mid * mid, axis=1, keepdims=True) + norm_epsilon)
+            scaled = mid * inverse
+            gain_grad = gain_grad + jnp.sum(grads * scaled, axis=0, keepdims=True)
+            grads = grads * gain_ref[...]
+            inner = jnp.mean(grads * scaled, axis=1, keepdims=True)
+            mid_grad_ref[rows, :] = (
+                cotangent_ref[rows, :].astype(jnp.float32) + inverse * (grads - scaled * inner)
+            ).astype(low)
+        gain_grad_ref[...] = gain_grad
+        for r0 in range(0, D, 256):
+            rows = slice(r0, r0 + 256)
+            out_grad_ref[rows, :] = jnp.dot(
+                attended_ref[rows, :], mid_grad_ref[...], preferred_element_type=jnp.float32
+            ).astype(low)
+            attended_grad_ref[rows, :] = contract(
+                w_out_ref[rows, :], mid_grad_ref[...], 1, 1
+            ).astype(low)
+
+
+def feed_back(ffn_grad, normed, mid, gain, cotangent, attended, w_out, activ, slope, w_in, w_down):
+    def fixed(*shape):
+        return pl.BlockSpec(shape, lambda j: (0,) * len(shape))
+
+    def stripe():
+        return pl.BlockSpec((FEED_WIDTH, D), lambda j: (j, 0))
+
+    def column():
+        return pl.BlockSpec((SEQ, FEED_WIDTH), lambda j: (0, j))
+
+    low = jnp.bfloat16
+    return pl.pallas_call(
+        feed_back_kernel,
+        grid=(FF // FEED_WIDTH,),
+        in_specs=[
+            fixed(SEQ, D),
+            fixed(SEQ, D),
+            fixed(SEQ, D),
+            fixed(1, D),
+            fixed(SEQ, D),
+            fixed(D, SEQ),
+            fixed(D, D),
+            column(),
+            column(),
+            stripe(),
+            stripe(),
+        ],
+        out_specs=[
+            stripe(),
+            stripe(),
+            fixed(SEQ, D),
+            fixed(1, D),
+            fixed(D, D),
+            fixed(D, SEQ),
+        ],
+        out_shape=[
+            jax.ShapeDtypeStruct((FF, D), low),
+            jax.ShapeDtypeStruct((FF, D), low),
+            jax.ShapeDtypeStruct((SEQ, D), low),
+            jax.ShapeDtypeStruct((1, D), jnp.float32),
+            jax.ShapeDtypeStruct((D, D), low),
+            jax.ShapeDtypeStruct((D, SEQ), low),
+        ],
+        scratch_shapes=[pltpu.VMEM((SEQ, D), jnp.float32), pltpu.VMEM((SEQ, FEED_WIDTH), low)],
+        compiler_params=pltpu.CompilerParams(vmem_limit_bytes=VMEM_LIMIT),
+        cost_estimate=pl.CostEstimate(
+            flops=10 * SEQ * FF * D, bytes_accessed=32 * 1024 * 1024, transcendentals=0
+        ),
+        name="feed_back",
+    )(ffn_grad, normed, mid, gain[None, :], cotangent, attended, w_out, activ, slope, w_in, w_down)
 
 
 def adamw(weights, grads, first, second, step):
@@ -1123,171 +1478,72 @@
     group_heads = H // tensor_count
     head_rows = group_heads * HS
     hidden_rows = FF // tensor_count
-    dp_pos = lax.axis_index("dp")
     tensor_pos = lax.axis_index("tensor")
-
-    ends = (0, 3 * head_rows, 4 * head_rows, 4 * head_rows + hidden_rows, owners.shape[0])
-    sizes = [high - low for low, high in zip(ends[:-1], ends[1:])]
-    roles = len(sizes)
-
-    pair_rows = -(-((capacity + roles * (dp_count - 1)) // dp_count) // 16) * 16
-    owner_hot = (owners[:, None] == jnp.arange(dp_count, dtype=jnp.int32)[None, :]).astype(jnp.int32)
-    counts = jnp.stack(
-        [jnp.sum(owner_hot[low:high], axis=0) for low, high in zip(ends[:-1], ends[1:])]
+    sizes = [3 * head_rows, head_rows, hidden_rows, hidden_rows]
+    local_sizes = [-(-size // dp_count // 16) * 16 for size in sizes]
+    pair_rows = -(-((capacity + len(sizes) * (dp_count - 1)) // dp_count) // 16) * 16
+    slot_place, spread_place, orders, places = plan(
+        owners, sizes, local_sizes, capacity, pair_rows
     )
-    dps = jnp.arange(dp_count, dtype=jnp.int32)
-    starts = jnp.sum(
-        jnp.where(dps[None, :] < dps[:, None], counts[:, None, :], 0), axis=2, dtype=jnp.int32
-    )
-    role_ids = jnp.arange(roles, dtype=jnp.int32)
-    earlier = role_ids[None, :] < role_ids[:, None]
-    role_starts = jnp.sum(jnp.where(earlier[:, :, None], counts[None], 0), axis=1, dtype=jnp.int32)
-
-    def hits(first, number, target):
-        return (first + number - 1 - target) // dp_count - (first - 1 - target) // dp_count
-
-    def own(values):
-        return lax.dynamic_index_in_dim(values, dp_pos, values.ndim - 1, keepdims=False)
-
-    slot = jnp.arange(capacity, dtype=jnp.int32)
-    slot_place = jnp.full((capacity,), -1, jnp.int32)
-    own_counts, own_starts, own_role_starts = own(counts), own(starts), own(role_starts)
-    for role in range(roles):
-        inside = (slot >= own_role_starts[role]) & (
-            slot < own_role_starts[role] + own_counts[role]
-        )
-        rank = slot - own_role_starts[role]
-        target = (own_starts[role] + rank) % dp_count
-        place = rank // dp_count
-        for other in range(role):
-            place = place + hits(own_starts[other], own_counts[other], target)
-        slot_place = jnp.where(
-            inside, ((target - dp_pos) % dp_count) * pair_rows + place, slot_place
-        )
-    local_sizes = [-(-size // dp_count // 16) * 16 for size in sizes]
-    local_starts = [sum(local_sizes[:role]) for role in range(roles)]
-    source_dp = (dp_pos - dps) % dp_count
-    sent_counts, sent_starts = counts[:, source_dp], starts[:, source_dp]
-    pair_place = jnp.arange(pair_rows, dtype=jnp.int32)[None, :]
-    spread_place = jnp.full((dp_count, pair_rows), -1, jnp.int32)
-    passed = jnp.zeros((dp_count, 1), jnp.int32)
-    for role in range(roles):
-        number = hits(sent_starts[role], sent_counts[role], dp_pos)[:, None]
-        first = sent_starts[role] + (dp_pos - sent_starts[role]) % dp_count
-        rank = pair_place - passed
-        local = local_starts[role] + first[:, None] // dp_count + rank
-        spread_place = jnp.where((rank >= 0) & (rank < number), local, spread_place)
-        passed = passed + number
-    spread_place = spread_place.reshape(-1)
-    below = jnp.cumsum(owner_hot, axis=0) - 1
-    row_target = []
-    row_rank = []
-    for role, (low, high) in enumerate(zip(ends[:-1], ends[1:])):
-        number = jnp.sum(
-            owner_hot[low:high] * (below[low:high] - role_starts[role] + starts[role]), axis=1
-        )
-        row_target.append(number % dp_count)
-        row_rank.append(number // dp_count)
-
-    orders = [
-        ((dp_pos - row_target[role]) % dp_count) * local_sizes[role] + row_rank[role]
-        for role in range(roles)
-    ]
 
     gain_one, gain_two, adapter, table = unpack(small_params)
-    bucket_onehot = (buckets[:, None] == jnp.arange(NB, dtype=jnp.int32)[None, :]).astype(
-        jnp.float32
-    )
-    per_offset = lax.dot_general(
-        table, bucket_onehot, (((0,), (1,)), ((), ())), precision=highest
-    )
-    bias_rows = jnp.concatenate([jnp.zeros((H, 1), jnp.float32), per_offset[:, ::-1]], axis=1)
-    group_order = jnp.arange(tensor_count, dtype=jnp.int32) ^ tensor_pos
-    bias_rows = bias_rows.reshape(tensor_count, group_heads, 2 * SEQ)[group_order]
-    bias_rows = bias_rows.reshape(H, 1, 2 * SEQ)
+    table_rows = jnp.pad(table.T, ((0, 16 - H), (0, 0)))
+    bucket_place = jnp.concatenate([jnp.full((1,), -1, jnp.int32), buckets[::-1]])[None, :]
     segments = lax.dynamic_slice_in_dim(segment_ids, tensor_pos * SEQ, SEQ, 0)
-
-    inputs_f = tokens.astype(jnp.float32)
-    normed_one = rms_norm(inputs_f, gain_one).astype(jnp.bfloat16)
-    groups = range(tensor_count)
-    w_qkv, w_out, w_in, w_down, projected, attended, scale, exp_scores = front(
-        master[0].astype(jnp.bfloat16),
+    w_qkv, w_out, w_in, w_down, projected, attended, scale, normed_one, exp_scores = front(
+        master[0],
         slot_place,
         spread_place,
         orders,
         local_sizes,
-        pair_rows,
-        normed_one,
-        bias_rows,
+        tokens,
+        gain_one,
+        table_rows,
+        bucket_place,
         segments,
     )
-    attended = attended.reshape(tensor_count, head_rows, SEQ)
-    mid = inputs_f
-    for k in groups:
-        mid = mid + contract(attended[k], w_out[k], 0, 0)
-    normed_two = rms_norm(mid, gain_two).astype(jnp.bfloat16)
-    activ, slope = [], []
-    ffn_out = jnp.zeros(mid.shape, jnp.float32)
-    for k in groups:
-        part, part_slope, ffn_out = feed(normed_two, w_in[k], w_down[k], ffn_out)
-        activ.append(part)
-        slope.append(part_slope)
-    final, adapter_pull = jax.vjp(adapter_apply, ffn_out, adapter)
-    layer_out = (mid + final).astype(jnp.bfloat16)
-
-    out_grad = cotangent.astype(jnp.float32)
-    ffn_grad, adapter_grad = adapter_pull(out_grad)
-    ffn_grad = ffn_grad.astype(jnp.bfloat16)
-
-    normed_two_grad = jnp.zeros(mid.shape, jnp.float32)
-    down_grad, in_grad = [None] * tensor_count, [None] * tensor_count
-    for k in reversed(groups):
-        pre_grad = (contract(ffn_grad, w_down[k], 1, 1) * slope[k].astype(jnp.float32)).astype(
-            jnp.bfloat16
-        )
-        down_grad[k] = contract(activ[k], ffn_grad, 0, 0).astype(jnp.bfloat16)
-        in_grad[k] = contract(pre_grad, normed_two, 0, 0).astype(jnp.bfloat16)
-        normed_two_grad = normed_two_grad + jnp.dot(
-            pre_grad, w_in[k], preferred_element_type=jnp.float32
-        )
-    _, norm_two_pull = jax.vjp(rms_norm, mid, gain_two)
-    mid_extra, gain_two_grad = norm_two_pull(normed_two_grad)
-    mid_grad = out_grad + mid_extra
-    mid_grad_low = mid_grad.astype(jnp.bfloat16)
-    attended_all = attended.reshape(D, SEQ)
-    out_weight_grad = jnp.dot(
-        attended_all, mid_grad_low, preferred_element_type=jnp.float32
-    ).astype(jnp.bfloat16)
-    attended_grad = contract(w_out.reshape(D, D), mid_grad_low, 1, 1).astype(jnp.bfloat16)
+    w_out, w_in, w_down = [part.reshape(-1, D) for part in (w_out, w_in, w_down)]
+    factors, factors_pull = jax.vjp(adapter_factors, adapter)
+    (activ, slope, normed_two, mid, layer_out, ffn_grad), factor_grads = feed(
+        attended, w_out, tokens, gain_two, cotangent, factors, w_in, w_down
+    )
+    in_grad, down_grad, mid_grad, gain_two_grad, out_weight_grad, attended_grad = feed_back(
+        ffn_grad,
+        normed_two,
+        mid,
+        gain_two,
+        cotangent,
+        attended,
+        w_out,
+        activ,
+        slope,
+        w_in,
+        w_down,
+    )
+    (adapter_grad,) = factors_pull(factor_grads)
     small_local = jnp.concatenate(
-        [jnp.zeros((D,), jnp.float32), gain_two_grad]
+        [jnp.zeros((D,), jnp.float32), gain_two_grad[0]]
         + [piece.reshape(-1) for piece in adapter_grad]
         + [jnp.zeros((TABLE_ROW * TILE - 2 * D - NADAPT,), jnp.float32)]
     ).reshape(TABLE_ROW, TILE)
     owned_grad, input_grad, small_total = back(
-        (
-            out_weight_grad.reshape(tensor_count, head_rows, D),
-            jnp.stack(in_grad),
-            jnp.stack(down_grad),
-        ),
+        [
+            grad.reshape(tensor_count, -1, D) for grad in (out_weight_grad, in_grad, down_grad)
+        ],
         projected,
         exp_scores,
-        attended_all,
+        attended,
         scale,
         attended_grad,
         normed_one,
         w_qkv,
         tokens,
-        mid_grad_low,
+        mid_grad,
         gain_one,
         small_local,
-        buckets,
-        [
-            ((row_target[role] - dp_pos) % dp_count) * local_sizes[role] + row_rank[role]
-            for role in range(roles)
-        ],
+        bucket_place,
+        places,
         local_sizes,
-        pair_rows,
         spread_place,
         slot_place,
     )
@@ -1297,7 +1553,7 @@
             small_total[TABLE_ROW : TABLE_ROW + H, :NB].T.reshape(-1),
         ]
     )
-    own_filled = (slot_place >= 0).astype(jnp.float32)[:, None]
+    own_filled = (slot_place[0] >= 0).astype(jnp.float32)[:, None]
     step = step_count[0].astype(jnp.float32)
     new_master, new_first, new_second = adamw(
         master[0], owned_grad, first_moment[0], second_moment[0], step

time: 550 us -> 447 us (0.81)
  matrix products: 68 us -> 0 us
  other arithmetic: 54.9 us -> 10.8 us
  Pallas kernels: 367 us -> 402 us
  local copies, waits for them, and re-layouts: 37.1 us -> 24.5 us
  between operations: 13.5 us -> 2.05 us
    dot_general x39 -> x0, matrix products: 68 us -> none  [the longest x17 24.8 us: contract(): lax.dot_general(left, right, (((left_dim,), (right_dim,)), ((), ())), pre...]
    pallas_call x4 -> x3, Pallas kernels: 36.8 us -> 73.2 us  [the longest x1 38.1 us: feed_back(): pl.pallas_call(feed_back_kernel, grid=(FF // FEED_WIDTH,), in_specs=[fixe...]
    select_n x5 -> x0, other arithmetic: 16 us -> none  [the longest x2 15.9 us: per_device(): jnp.where(inside, (target - dp_pos) % dp_count * pair_rows + place, slot_...]
    convert_element_type x8 -> x3, other arithmetic: 14.3 us -> 1.3 us  [the longest x1 1.28 us: front(): segments.astype(jnp.float32)[None, :]]
    another operation x5 -> x0, other arithmetic: 7.66 us -> none  [the longest x1 2.63 us: per_device(): jnp.stack(in_grad)]
    pallas_call x1, Pallas kernels: 178 us -> 171 us  [back(): pl.pallas_call(functools.partial(back_kernel, sizes), in_specs=[away] * 5...]
    add x6 -> x0, other arithmetic: 5.79 us -> none  [the longest x3 3.9 us: per_device(): (dp_pos - row_target[role]) % dp_count * local_sizes[role] + row_rank[role]]
    unnamed x115 -> x38, local copies, waits for them, and re-layouts: 12.6 us -> 12.4 us
where the time goes in v4:
time: 447 us; the launch traced here: 439 us
  Pallas kernels  402 us (90%)
  local copies, waits for them, and re-layouts  24.5 us (5%)
  other arithmetic  10.8 us (2%)
    pallas_call x1, Pallas kernels, back(): pl.pallas_call(functools.partial(back_kernel, sizes), in_specs=[away] * 5...  171 us
    pallas_call x1, Pallas kernels, front(): pl.pallas_call(functools.partial(front_kernel, sizes), in_specs=[whole] *...  158 us
    pallas_call x1, Pallas kernels, feed_back(): pl.pallas_call(feed_back_kernel, grid=(FF // FEED_WIDTH,), in_specs=[fixe...  38.1 us
    pallas_call x1, Pallas kernels, feed(): pl.pallas_call(feed_kernel, grid=(FF // FEED_WIDTH,), in_specs=[fixed(D,...  33.5 us
    unnamed x38, local copies, waits for them, and re-layouts  12.4 us

profile of v4, /device:TPU:0, one launch (start us, length us, event | category | flops | bytes accessed | tf_op | source)
XLA Modules:
  0.0 439.1 jit_solution(15272522684998297548)
XLA Ops:
  0.6 0.8 fusion.8
  1.4 0.6 broadcast_in_dim.56.refs_2_
  2.0 0.6 broadcast_in_dim.57.refs_3_
  2.6 0.7 slice.56
  3.3 0.6 broadcast_in_dim.54.refs_0_
  3.9 1.3 slice.57
  5.2 1.7 plan.1
  6.9 1.3 dynamic-slice_convert_fusion
  8.2 0.8 fusion.6
  9.0 0.6 broadcast_in_dim.58.gain_ref
  9.6 0.8 reverse
  10.5 0.7 pad_add_fusion
  11.1 0.8 slice.61
  11.9 0.1 reshape.169
  12.0 0.1 copy.44
  12.1 0.6 pad.4.table_ref
  12.7 157.5 %front.1 = (bf16[4,576,768]{2,1,0:T(8,128)(2,1)}, bf16[4,192,768]{2,1,0:T(8,128)(2,1)}, bf16[4,768,768]{2,1,0:T(8,128)(2,1)}, bf16[4,768,768]{2,1,0:T(8,128)(2,1...) custom-call(f32[576,768]{1,0:T(8,128)} %bitcast.66, ...), custom_call_target="tpu_custom_call" | custom-call | flops 32212254720 | bytes 67108864 | tf_op jit(solution)/shard_map/front/pallas_call | solution.py:533
  170.4 0.1 broadcast_multiply_fusion
  170.5 0.1 mul.219.right_ref
  170.6 0.1 mul.227.tall_ref
  170.7 0.1 reshape.171
  170.8 0.1 copy.45
  170.9 0.1 reshape.173
  171.0 0.1 broadcast_multiply_fusion.2
  171.1 0.1 mul.223
  171.2 0.1 copy.47.wide_ref
  171.3 0.1 reshape.172
  171.4 0.1 broadcast_multiply_fusion.3
  171.5 0.1 mul.214
  171.5 0.1 copy.46.left_ref
  171.6 1.3 copy-done
  172.9 1.4 copy-done.3
  174.3 33.5 %feed.1 = (bf16[1024,3072]{1,0:T(8,128)(2,1)}, bf16[1024,3072]{1,0:T(8,128)(2,1)}, bf16[1024,768]{1,0:T(8,128)(2,1)S(1)}, f32[1024,768]{1,0:T(8,128)}, bf16[1024...) custom-call(bf16[768,1024]{1,0:T(8,128)(2,1)S(1)} %copy-done.3, ...), custom_call_target="tpu_custom_call" | custom-call | flops 14495514624 | bytes 33554432 | tf_op jit(solution)/shard_map/feed/pallas_call | solution.py:1286
  207.8 1.1 copy-done.4
  208.9 1.1 copy-done.5
  210.1 0.1 reshape.182
  210.2 0.1 reshape.186
  210.3 0.1 multiply_reduce_fusion
  210.4 0.1 reshape.183
  210.6 0.1 reshape.180
  210.7 0.1 multiply_reduce_fusion.3
  210.9 0.1 copy.50
  211.0 0.1 reshape.179
  211.1 0.1 multiply_reduce_fusion.2
  211.3 0.1 copy.51
  211.4 0.1 reshape.181
  211.5 38.1 %feed_back.1 = (bf16[3072,768]{1,0:T(8,128)(2,1)}, bf16[3072,768]{1,0:T(8,128)(2,1)}, bf16[1024,768]{1,0:T(8,128)(2,1)S(1)}, f32[1,768]{1,0:T(1,128)S(1)}, bf16[...) custom-call(bf16[1024,768]{1,0:T(8,128)(2,1)} %copy-done.5, bf16[1024,768]{1,0:T(8,128)(2,1)} %copy-done.4, ...), custom_call_target="tpu_custom_call" | custom-call | flops 24159191040 | bytes 33554432 | tf_op jit(solution)/shard_map/feed_back/pallas_call | solution.py:1408
  249.6 1.0 copy-done.2
  250.6 1.1 copy-done.6
  251.7 1.1 copy-done.7
  252.9 0.1 reshape.185
  253.0 0.1 reshape.184
  253.1 0.7 concatenate.10
  253.8 171.1 %back.1 = (f32[576,768]{1,0:T(8,128)}, bf16[1024,768]{1,0:T(8,128)(2,1)}, f32[48,128]{1,0:T(8,128)}) custom-call(bf16[4,192,768]{2,1,0:T(8,128)(2,1)} %bitcast.64, bf16[4,768,768]{2,1,0:T(8,128)(2,1)} %bitcast.89, bf16[4,768,768]{2,1,0:T(8,128)(2,1)} %bitcast.90, bf16[4,576,1024]{2,1,0:T(8,128)(2,1)} %get-tuple-element.69.projected_ref, ...), custom_call_target="tpu_custom_call" | custom-call | flops 51539607552 | bytes 67108864 | tf_op jit(solution)/shard_map/back/pallas_call | solution.py:1105
  424.8 0.7 slice_bitcast_fusion.1
  425.5 0.1 copy.52
  425.6 0.1 reshape.190
  425.7 0.7 slice_bitcast_fusion
  427.2 0.7 multiply_subtract_fusion
  427.9 0.6 fusion.2
  428.5 6.8 %convert_bitcast_fusion = (bf16[1,576,768]{2,1,0:T(8,128)(2,1)}, f32[576,768]{1,0:T(8,128)}, f32[1,576,768]{2,1,0:T(8,128)}, f32[1,576,768]{2,1,0:T(8,128)}) fusion(f32[576]{0:T(1024)S(1)} %fusion.3, f32[576,768]{1,0:T(8,128)} %get-tuple-element.86, f32[1,576,768]{2,1,0:T(8,128)} %param.20, f32[]{:T(128)} %bitcast.26, f32[1,576,768]{2,1,0:T(8,128)} %param.19, ...), kind=kLoop, calls=%fused_computation.6 | loop fusion | flops 7962624 | bytes 13273352 | tf_op jit(solution)/shard_map/broadcast_in_dim | solution.py:1575
  435.4 1.1 copy.56
  436.5 0.9 copy-done.8
  437.4 1.2 copy.57
  (41 shorter events, 0.6 us)
Async XLA Ops:
  12.7 158.0 %copy-start.11 = (f32[3616]{0:T(1024)S(1)}, f32[3616]{0:T(1024)}, u32[]{:S(2)}) copy-start(f32[3616]{0:T(1024)} %param.21) | copy-start | bytes 43396
  171.6 1.3 copy-start
  172.9 1.4 copy-start.3
  174.3 37.2 %copy-start.1 = (bf16[4,192,768]{2,1,0:T(8,128)(2,1)S(1)}, bf16[4,192,768]{2,1,0:T(8,128)(2,1)}, u32[]{:S(2)}) copy-start(bf16[4,192,768]{2,1,0:T(8,128)(2,1)} %get-tuple-element.57) | copy-start | bytes 3538948
  207.8 1.1 copy-start.4
  208.9 1.1 copy-start.5
  249.6 1.0 copy-start.2
  250.6 1.1 copy-start.6
  251.7 1.1 copy-start.7
  253.7 173.4 %copy-start.13 = (f32[3616]{0:T(1024)S(1)}, f32[3616]{0:T(1024)}, u32[]{:S(2)}) copy-start(f32[3616]{0:T(1024)} %param.23) | copy-start | bytes 43396
  253.7 173.4 %copy-start.14 = (f32[3616]{0:T(1024)S(1)}, f32[3616]{0:T(1024)}, u32[]{:S(2)}) copy-start(f32[3616]{0:T(1024)} %param.22) | copy-start | bytes 43396
  253.7 174.1 %copy-start.15 = (f32[1696]{0:T(1024)S(1)}, f32[1696]{0:T(1024)}, u32[]{:S(2)}) copy-start(f32[1696]{0:T(1024)} %param.24) | copy-start | bytes 20356
  253.8 174.7 %copy-start.16 = (s32[1,576]{1,0:T(1,128)S(1)}, s32[1,576]{1,0:T(1,128)}, u32[]{:S(2)}) copy-start(s32[1,576]{1,0:T(1,128)} %get-tuple-element.50.slot_place_ref) | copy-start | bytes 6916
  253.8 174.7 %copy-start.9 = (f32[1,576,768]{2,1,0:T(8,128)S(1)}, f32[1,576,768]{2,1,0:T(8,128)}, u32[]{:S(2)}) copy-start(f32[1,576,768]{2,1,0:T(8,128)} %param.18) | copy-start | bytes 5308420
  427.9 7.5 %copy-start.12 = (f32[3616]{0:T(1024)}, f32[3616]{0:T(1024)S(1)}, u32[]{:S(2)}) copy-start(f32[3616]{0:T(1024)S(1)} %get-tuple-element.134) | copy-start | bytes 43396
  428.5 6.8 %copy-start.10 = (bf16[1024,768]{1,0:T(8,128)(2,1)S(1)}, bf16[1024,768]{1,0:T(8,128)(2,1)}, u32[]{:S(2)}) copy-start(bf16[1024,768]{1,0:T(8,128)(2,1)} %get-tuple-element.125) | copy-start | bytes 4718596
  435.3 2.0 copy-start.8

commit v5 on v4

--- a/solution.py
+++ b/solution.py
@@ -150,6 +150,14 @@
     def remainder(values):
         return values - dp_count * quotient(values)
 
+    line = dp_count // 2
+
+    def halve(values):
+        return jnp.floor((values + 0.5) * 0.5)
+
+    def around(values):
+        return values - line * jnp.floor((values + 0.5) * (1.0 / line))
+
     owners = [ref[...].astype(jnp.float32) for ref in owner_refs]
 
     def stats(who):
@@ -213,8 +221,10 @@
             number = jnp.sum(hot * (rank + before), axis=0, keepdims=True)
             before = before + jnp.sum(hot, axis=1, keepdims=True)
             target, row = remainder(number), quotient(number)
-            order = remainder(dp_pos - target) * local_sizes[role] + row
-            place = remainder(target - dp_pos) * local_sizes[role] + row
+            side = jnp.abs(target - 2.0 * halve(target) - dp_pos + 2.0 * halve(dp_pos)) * line
+            ahead = halve(target) - halve(dp_pos)
+            order = (around(0.0 - ahead) + side) * local_sizes[role] + row
+            place = (around(ahead) + side) * local_sizes[role] + row
             order_refs[role][:, c0:c1] = order.astype(jnp.int32)
             place_refs[role][:, c0:c1] = place.astype(jnp.int32)
 
@@ -280,16 +290,23 @@
     buf_out,
     buf_in,
     buf_down,
+    buf_far,
+    far_spread,
     stage_out,
     stage_in,
     stage_down,
+    stage_far,
     window,
     scores,
     exp_stage,
     deal_send,
     deal_recv,
-    gather_send,
-    gather_recv,
+    far_send,
+    far_recv,
+    line_send,
+    line_recv,
+    side_send,
+    side_recv,
     group_send,
     group_recv,
     local_sem,
@@ -367,29 +384,74 @@
         total = total + jnp.dot(hot, received[m], preferred_element_type=jnp.float32)
     spread[...] = total.astype(jnp.bfloat16)
 
-    bufs = (buf_qkv, buf_out, buf_in, buf_down)
-    orders = (order_qkv_ref, order_out_ref, order_in_ref, order_down_ref)
-    stages = (w_qkv_ref.at[0], stage_out, stage_in, stage_down)
-    finals = (w_qkv_ref, w_out_ref, w_in_ref, w_down_ref)
-    offsets = [sum(buf.shape[1] for buf in bufs[:role]) for role in range(len(bufs))]
-
-    def gather(role, m):
-        count = bufs[role].shape[1]
+    bufs = (buf_qkv, buf_out, buf_in, buf_down, buf_far)
+    orders = (order_qkv_ref, order_out_ref, order_in_ref, order_down_ref, order_down_ref)
+    stages = (w_qkv_ref.at[0], stage_out, stage_in, stage_down, stage_far)
+    finals = (w_qkv_ref, w_out_ref, w_in_ref, w_down_ref, w_down_ref)
+    sizes = tuple(sizes) + (sizes[3],)
+    offsets = [sum(buf.shape[1] for buf in bufs[:role]) for role in range(4)]
+    line = dp_count // 2
+    line_pos, side = lax.div(dp_pos, 2), lax.rem(dp_pos, 2)
+    side_peer = (dp_pos + 1 - 2 * side, tensor_pos)
+
+    def far_exchange():
         return pltpu.make_async_remote_copy(
-            spread.at[pl.ds(offsets[role], count)],
+            spread.at[pl.ds(offsets[3], far_spread.shape[0])],
+            far_spread,
+            far_send,
+            far_recv,
+            device_id=far_peer,
+            device_id_type=MESH,
+        )
+
+    def block(role):
+        if role == 4:
+            return far_spread
+        return spread.at[pl.ds(offsets[role], bufs[role].shape[1])]
+
+    def along_line(role, m):
+        return pltpu.make_async_remote_copy(
+            block(role),
             bufs[role].at[m],
-            gather_send.at[role, m],
-            gather_recv.at[role, m],
-            device_id=dp_peer(m),
+            line_send.at[role, m],
+            line_recv.at[role, m],
+            device_id=(lax.rem(line_pos + m, line) * 2 + side, tensor_pos),
             device_id_type=MESH,
         )
 
-    def start_gather(role):
-        each_peer(lambda m: gather(role, m).start())
-        bufs[role][0] = spread[offsets[role] : offsets[role] + bufs[role].shape[1], :]
+    def to_side(role, m):
+        return pltpu.make_async_remote_copy(
+            bufs[role].at[m],
+            bufs[role].at[line + m],
+            side_send.at[role, m],
+            side_recv.at[role, m],
+            device_id=side_peer,
+            device_id_type=MESH,
+        )
+
+    def each_line(first, run):
+        def step(m, carry):
+            run(m)
+            return carry
+
+        lax.fori_loop(first, line, step, 0)
+
+    def start_line(role):
+        if role == 4:
+            far_exchange().wait()
+        each_line(1, lambda m: along_line(role, m).start())
+        bufs[role][0] = block(role)[...]
+        to_side(role, 0).start()
+
+    def start_side(role):
+        def step(m):
+            along_line(role, m).wait()
+            to_side(role, m).start()
+
+        each_line(1, step)
 
     def order(role):
-        each_peer(lambda m: gather(role, m).wait())
+        each_line(0, lambda m: to_side(role, m).wait())
         count = bufs[role].shape[1]
         source = bufs[role][...].reshape(dp_count * count, D)
         step = 256
@@ -399,11 +461,14 @@
             stages[role][r0:r1, :] = contract(hot, source, 0, 0).astype(jnp.bfloat16)
 
     def share(role, part):
-        src, slot, peer = (
-            (stages[role], 1, core_peer),
-            (stages[role], 2, far_peer),
-            (finals[role].at[2], 3, core_peer),
-        )[part]
+        if role == 4:
+            src, slot, peer = stages[role], 3, core_peer
+        else:
+            src, slot, peer = (
+                (stages[role], 1, core_peer),
+                (stages[role], 2, far_peer),
+                (finals[role].at[2], 3, core_peer),
+            )[part]
         return pltpu.make_async_remote_copy(
             src,
             finals[role].at[slot],
@@ -414,12 +479,14 @@
         )
 
     def keep(role):
-        return pltpu.make_async_copy(stages[role], finals[role].at[0], local_sem.at[role])
+        slot = 2 if role == 4 else 0
+        return pltpu.make_async_copy(stages[role], finals[role].at[slot], local_sem.at[role])
 
     def start_share(role):
         order(role)
         share(role, 0).start()
-        share(role, 1).start()
+        if role < 3:
+            share(role, 1).start()
         if role > 0:
             keep(role).start()
 
@@ -427,10 +494,12 @@
         share(role, 1).wait_recv()
         share(role, 2).start()
 
-    start_gather(0)
+    far_exchange().start()
+    start_line(0)
+    start_side(0)
     start_share(0)
-    start_gather(1)
-    start_gather(2)
+    start_line(1)
+    start_line(2)
 
     def true_head(group, head):
         return true_group((tensor_pos, core_pos, far_pos), group, tensor_count) * group_heads + head
@@ -440,7 +509,21 @@
 
         @pl.when(i == 1)
         def _():
+            start_side(1)
+
+        @pl.when(i == 3)
+        def _():
             start_share(1)
+
+        @pl.when(i == 5)
+        def _():
+            start_side(2)
+            start_line(3)
+            start_line(4)
+
+        @pl.when(i == 10)
+        def _():
+            start_share(2)
 
         @pl.when(i == group_heads)
         def _():
@@ -454,7 +537,10 @@
         def _():
             share(0, 2).wait_recv()
             forward(1)
-            start_gather(3)
+
+        @pl.when(i == 11)
+        def _():
+            start_side(3)
 
         @pl.when(head == 0)
         def _():
@@ -496,18 +582,20 @@
     lax.fori_loop(0, heads, head_step, 0)
     for i in (heads - 2, heads - 1):
         pltpu.make_async_copy(exp_stage.at[i % 2], exp_ref.at[i], exp_sem.at[i % 2]).wait()
-    start_share(2)
+    start_side(4)
     start_share(3)
+    start_share(4)
     forward(2)
-    forward(3)
     for role in range(len(bufs)):
         share(role, 0).wait_send()
-        share(role, 1).wait_send()
-        share(role, 2).wait_send()
+        if role < 3:
+            share(role, 1).wait_send()
+            share(role, 2).wait_send()
         if role > 0:
             share(role, 0).wait_recv()
+            keep(role).wait()
+        if role in (1, 2):
             share(role, 2).wait_recv()
-            keep(role).wait()
 
 
 def front(
@@ -549,19 +637,24 @@
             pltpu.VMEM((H, 1, 2 * SEQ), jnp.float32),
             pltpu.VMEM((SEQ, TILE), jnp.float32),
         ]
-        + [pltpu.VMEM((dp_count, size, D), low) for size in local_sizes]
-        + [pltpu.VMEM((size, D), low) for size in sizes[1:]]
+        + [pltpu.VMEM((dp_count, size, D), low) for size in local_sizes + local_sizes[3:]]
+        + [pltpu.VMEM((local_sizes[3], D), low)]
+        + [pltpu.VMEM((size, D), low) for size in sizes[1:] + sizes[3:]]
         + [
             pltpu.VMEM((WINDOW, TILE), jnp.float32),
             pltpu.VMEM((SEQ, QUERY_TILE), jnp.float32),
             pltpu.VMEM((2, SEQ, SEQ), low),
             dma((dp_count,)),
             dma((dp_count,)),
-            dma((roles, dp_count)),
-            dma((roles, dp_count)),
-            dma((roles, 3)),
-            dma((roles, 3)),
-            dma((roles,)),
+            dma,
+            dma,
+            dma((roles + 1, dp_count // 2)),
+            dma((roles + 1, dp_count // 2)),
+            dma((roles + 1, dp_count // 2)),
+            dma((roles + 1, dp_count // 2)),
+            dma((roles + 1, 3)),
+            dma((roles + 1, 3)),
+            dma((roles + 1,)),
             dma((2,)),
         ],
         compiler_params=pltpu.CompilerParams(
@@ -688,6 +781,7 @@
     input_grad_ref,
     small_total_ref,
     bucket_hot,
+    weights,
     proj,
     proj_grad,
     normed_grad,
@@ -719,6 +813,11 @@
     got_out,
     got_in,
     got_down,
+    side_qkv,
+    side_out,
+    side_down,
+    end_mine,
+    end_far,
     spread,
     sent,
     received,
@@ -729,8 +828,12 @@
     core_recv,
     far_send,
     far_recv,
-    deal_send,
-    deal_recv,
+    side_send,
+    side_recv,
+    line_send,
+    line_recv,
+    end_send,
+    end_recv,
     back_send,
     back_recv,
     small_send,
@@ -755,6 +858,7 @@
     core_threes = (core_three_qkv, core_three_out, core_three_in, core_three_down)
     fars = (far_qkv, far_out, far_in, far_down)
     gots = (got_qkv, got_out, got_in, got_down)
+    side_got = (side_qkv, side_out, far_in, side_down)
     places = (place_qkv_ref, place_out_ref, place_in_ref, place_down_ref)
     offsets = [sum(got.shape[1] for got in gots[:role]) for role in range(len(gots))]
     low = jnp.bfloat16
@@ -788,7 +892,10 @@
         return pltpu.make_async_copy(exp_ref.at[head], exp_stage.at[slot], exp_sem.at[slot])
 
     def load_proj(group):
-        return pltpu.make_async_copy(projected_ref.at[group], proj, proj_sem)
+        return pltpu.make_async_copy(projected_ref.at[group], proj, proj_sem.at[0])
+
+    def load_weights(group):
+        return pltpu.make_async_copy(w_qkv_ref.at[group], weights, proj_sem.at[1])
 
     def load(role, which):
         target = zeros[role] if which == 0 else twos[role]
@@ -801,7 +908,7 @@
             src = qkv_odd.at[which // 2]
         else:
             src = grad_refs[role].at[which]
-        target = core_ones[role] if which == 1 else core_threes[role].at[pl.ds(0, sizes[role])]
+        target = (core_ones if which == 1 else core_threes)[role].at[pl.ds(0, sizes[role])]
         return pltpu.make_async_remote_copy(
             src,
             target,
@@ -821,16 +928,45 @@
             device_id_type=MESH,
         )
 
-    def deal_copy(role, m):
+    line = dp_count // 2
+    line_pos, side = lax.div(dp_pos, 2), lax.rem(dp_pos, 2)
+    side_peer = (dp_pos + 1 - 2 * side, tensor_pos)
+
+    def each_line(run):
+        def step(m, carry):
+            run(m)
+            return carry
+
+        lax.fori_loop(1, line, step, 0)
+
+    def leaving(role, far):
+        return core_ones[role] if far else core_threes[role]
+
+    def side_copy(role, far=0):
+        count = gots[role].shape[1] * line
+        return pltpu.make_async_remote_copy(
+            leaving(role, far).at[pl.ds(count, count)],
+            side_got[role].at[pl.ds(count * far, count)],
+            side_send.at[role, far],
+            side_recv.at[role, far],
+            device_id=side_peer,
+            device_id_type=MESH,
+        )
+
+    def line_copy(role, m, far=0):
         count = gots[role].shape[1]
-        start = pl.multiple_of(m * count, 16)
         return pltpu.make_async_remote_copy(
-            core_threes[role].at[pl.ds(start, count)],
-            gots[role].at[m],
-            deal_send.at[role, m],
-            deal_recv.at[role, m],
-            device_id=(up(m), tensor_pos),
+            leaving(role, far).at[pl.ds(pl.multiple_of(m * count, 16), count)],
+            gots[role].at[far * line + m],
+            line_send.at[role, far * line + m],
+            line_recv.at[role, far * line + m],
+            device_id=(lax.rem(line_pos + m, line) * 2 + side, tensor_pos),
             device_id_type=MESH,
+        )
+
+    def end_copy():
+        return pltpu.make_async_remote_copy(
+            end_mine, end_far, end_send, end_recv, device_id=far_peer, device_id_type=MESH
         )
 
     def send_far(role):
@@ -844,6 +980,15 @@
         ).astype(low)
         far_copy(role).start()
 
+    def scatter(role, far, total):
+        count = gots[role].shape[1]
+        for m in range(dp_count):
+            hot = one_hot(places[role][...] - m * count, (count, sizes[role]), 0)
+            leaving(role, far)[m * count : (m + 1) * count, :] = jnp.dot(
+                hot, total, preferred_element_type=jnp.float32
+            ).astype(low)
+        side_copy(role, far).start()
+
     def send_deal(role):
         core_copy(role, 1).wait_recv()
         if role > 0:
@@ -854,24 +999,60 @@
             + core_ones[role][...].astype(jnp.float32)
             + fars[role][...].astype(jnp.float32)
         ).astype(low)
+        scatter(role, 0, total)
+
+    def send_both(role):
+        core_copy(role, 1).wait_recv()
+        core_copy(role, 3).wait_recv()
+        load(role, 0).wait()
+        load(role, 2).wait()
+        count = sizes[role]
+        near = (
+            zeros[role][...].astype(jnp.float32)
+            + core_ones[role][0:count, :].astype(jnp.float32)
+        ).astype(low)
+        far = (
+            twos[role][...].astype(jnp.float32)
+            + core_threes[role][0:count, :].astype(jnp.float32)
+        ).astype(low)
+        scatter(role, 0, near)
+        scatter(role, 1, far)
+
+    def pass_line(role, far=0):
+        side_copy(role, far).wait()
+        count = gots[role].shape[1] * line
+        leaving(role, far)[0:count, :] = (
+            leaving(role, far)[0:count, :].astype(jnp.float32)
+            + side_got[role][count * far : count * (far + 1), :].astype(jnp.float32)
+        ).astype(low)
+        each_line(lambda m: line_copy(role, m, far).start())
+
+    def line_sum(role, far=0):
+        each_line(lambda m: line_copy(role, m, far).wait())
+        total = leaving(role, far)[0 : gots[role].shape[1], :].astype(jnp.float32)
+        for m in range(1, line):
+            total = total + gots[role][far * line + m].astype(jnp.float32)
+        return total
+
+    def finish_deal(role):
         count = gots[role].shape[1]
-        for m in range(dp_count):
-            hot = one_hot(places[role][...] - m * count, (count, sizes[role]), 0)
-            core_threes[role][m * count : (m + 1) * count, :] = jnp.dot(
-                hot, total, preferred_element_type=jnp.float32
-            ).astype(low)
-        each_peer(lambda m: deal_copy(role, m).start())
-
-    def finish_deal(role):
-        each_peer(lambda m: deal_copy(role, m).wait())
-        count = gots[role].shape[1]
-        total = core_threes[role][0:count, :].astype(jnp.float32)
-        for m in range(1, dp_count):
-            total = total + gots[role][m].astype(jnp.float32)
-        spread[offsets[role] : offsets[role] + count, :] = total.astype(low)
+        spread[offsets[role] : offsets[role] + count, :] = line_sum(role).astype(low)
+
+    def finish_far():
+        end_mine[...] = line_sum(2, 1).astype(low)
+        end_copy().start()
+
+    def finish_near():
+        total = line_sum(2)
+        end_copy().wait()
+        count = gots[2].shape[1]
+        spread[offsets[2] : offsets[2] + count, :] = (
+            total + end_far[...].astype(jnp.float32)
+        ).astype(low)
 
     load_exp(heads - group_heads, 0).start()
     load_proj(tensor_count - 1).start()
+    load_weights(tensor_count - 1).start()
     for role in (3, 2, 1):
         load(role, 2).start()
         load(role, 0).start()
@@ -894,13 +1075,30 @@
         def _():
             send_far(3)
 
+        @pl.when(i == 2)
+        def _():
+            send_both(2)
+
+        @pl.when(i == 6)
+        def _():
+            send_far(0)
+
         @pl.when(i == 7)
         def _():
-            send_far(2)
+            send_far(1)
+
+        @pl.when(i == 8)
+        def _():
+            send_deal(3)
 
         @pl.when(i == 9)
         def _():
-            send_deal(3)
+            pass_line(2, 1)
+            pass_line(2, 0)
+
+        @pl.when(i == 11)
+        def _():
+            pass_line(3)
 
         @pl.when(part_head == 0)
         def _():
@@ -980,22 +1178,38 @@
             def _():
                 weight_grad(zero_qkv)
 
+            load_weights(group).wait()
             for r0 in range(0, SEQ, 256):
                 normed_grad[r0 : r0 + 256, :] += jnp.dot(
                     proj_grad[:, r0 : r0 + 256].T,
-                    w_qkv_ref[group],
+                    weights[...],
                     preferred_element_type=jnp.float32,
                 )
 
+            @pl.when(group > 0)
+            def _():
+                load_weights(group - 1).start()
+
         return carry
 
     lax.fori_loop(0, heads, head_step, 0)
-    send_far(1)
-    send_far(0)
+
+    def load_rows(which):
+        source = (tokens_ref, mid_grad_ref)[which]
+        return pltpu.make_async_copy(
+            source, exp_stage.at[which, :, pl.ds(0, D)], exp_sem.at[which]
+        )
+
+    load_rows(0).start()
+    load_rows(1).start()
+    send_deal(1)
+    send_deal(0)
+    load_rows(0).wait()
+    load_rows(1).wait()
 
     gain_grad = jnp.zeros((1, D), jnp.float32)
     for r0 in range(0, SEQ, 128):
-        values = tokens_ref[r0 : r0 + 128, :].astype(jnp.float32)
+        values = exp_stage[0, r0 : r0 + 128, 0:D].astype(jnp.float32)
         grads = normed_grad[r0 : r0 + 128, :]
         inverse = lax.rsqrt(jnp.mean(values * values, axis=1, keepdims=True) + norm_epsilon)
         scaled = values * inverse
@@ -1003,7 +1217,7 @@
         grads = grads * gain_ref[...]
         inner = jnp.mean(grads * scaled, axis=1, keepdims=True)
         input_grad_ref[r0 : r0 + 128, :] = (
-            mid_grad_ref[r0 : r0 + 128, :].astype(jnp.float32) + inverse * (grads - scaled * inner)
+            exp_stage[1, r0 : r0 + 128, 0:D].astype(jnp.float32) + inverse * (grads - scaled * inner)
         ).astype(low)
     for part in range(D // TILE):
         small_own[part : part + 1, :] = gain_grad[:, TILE * part : TILE * (part + 1)]
@@ -1024,7 +1238,6 @@
 
     for m in range(1, tensor_count):
         small_copy(0, m).start()
-    send_deal(2)
     small_tensor[tensor_pos] = small_own[...]
     for m in range(1, tensor_count):
         small_copy(0, m).wait()
@@ -1033,17 +1246,19 @@
         total = total + small_tensor[m]
     small_total_ref[...] = total
     each_peer(lambda m: small_copy(1, m).start())
-    send_deal(1)
+    finish_far()
+    pass_line(1)
+    pass_line(0)
+    finish_near()
     finish_deal(3)
-    send_deal(0)
     small_dp[dp_pos] = small_total_ref[...]
     each_peer(lambda m: small_copy(1, m).wait())
     total = small_dp[0]
     for m in range(1, dp_count):
         total = total + small_dp[m]
     small_total_ref[...] = total
-    for role in (2, 1, 0):
-        finish_deal(role)
+    finish_deal(1)
+    finish_deal(0)
 
     values = spread[...]
     for m in range(dp_count):
@@ -1068,7 +1283,8 @@
     for role in range(len(gots)):
         core_copy(role, 1).wait_send()
         core_copy(role, 3).wait_send()
-        far_copy(role).wait_send()
+        if role != 2:
+            far_copy(role).wait_send()
 
 
 def back(
@@ -1104,7 +1320,7 @@
     ]
     return pl.pallas_call(
         functools.partial(back_kernel, sizes),
-        in_specs=[away] * 5 + [whole] * 16,
+        in_specs=[away] * 5 + [whole] * 4 + [away] * 3 + [whole] * 9,
         out_specs=[whole] * 3,
         out_shape=[
             jax.ShapeDtypeStruct((capacity, D), jnp.float32),
@@ -1113,6 +1329,7 @@
         ],
         scratch_shapes=[
             pltpu.VMEM((TILE, 2 * SEQ), low),
+            pltpu.VMEM((sizes[0], D), low),
             pltpu.VMEM((sizes[0], SEQ), low),
             pltpu.VMEM((sizes[0], SEQ), low),
             pltpu.VMEM((SEQ, D), jnp.float32),
@@ -1123,11 +1340,21 @@
         ]
         + parts
         + parts
-        + parts
+        + parts[:2]
+        + padded[2:3]
+        + parts[3:]
         + padded
-        + parts
-        + [pltpu.VMEM((dp_count, size, D), low) for size in local_sizes]
+        + parts[:2]
+        + [pltpu.VMEM((dp_count * local_sizes[2], D), low)]
+        + parts[3:]
         + [
+            pltpu.VMEM((dp_count if role == 2 else dp_count // 2, size, D), low)
+            for role, size in enumerate(local_sizes)
+        ]
+        + [pltpu.VMEM((dp_count // 2 * local_sizes[role], D), low) for role in (0, 1, 3)]
+        + [
+            pltpu.VMEM((local_sizes[2], D), low),
+            pltpu.VMEM((local_sizes[2], D), low),
             pltpu.VMEM((sum(local_sizes), D), low),
             pltpu.VMEM((dp_count, pair_rows, D), low),
             pltpu.VMEM((dp_count, pair_rows, D), low),
@@ -1138,15 +1365,19 @@
             dma((roles, 2)),
             dma((roles,)),
             dma((roles,)),
+            dma((roles, 2)),
+            dma((roles, 2)),
             dma((roles, dp_count)),
             dma((roles, dp_count)),
+            dma,
+            dma,
             dma((dp_count,)),
             dma((dp_count,)),
             dma((2, max(dp_count, tensor_count))),
             dma((2, max(dp_count, tensor_count))),
             dma((roles, 2)),
             dma((2,)),
-            dma,
+            dma((2,)),
         ],
         compiler_params=pltpu.CompilerParams(
             collective_id=2, has_side_effects=True, vmem_limit_bytes=62 * 1024 * 1024

time: 447 us -> 372 us (0.83)
  Pallas kernels: 402 us -> 330 us
    pallas_call x1, Pallas kernels: 158 us -> 117 us  [front(): pl.pallas_call(functools.partial(front_kernel, sizes), in_specs=[whole] *...]
    pallas_call x1, Pallas kernels: 171 us -> 140 us  [back(): pl.pallas_call(functools.partial(back_kernel, sizes), in_specs=[away] * 5...]
where the time goes in v5:
time: 372 us; the launch traced here: 367 us
  Pallas kernels  330 us (89%)
  local copies, waits for them, and re-layouts  24.5 us (7%)
  other arithmetic  10.8 us (3%)
    pallas_call x1, Pallas kernels, back(): pl.pallas_call(functools.partial(back_kernel, sizes), in_specs=[away] * 5...  140 us
    pallas_call x1, Pallas kernels, front(): pl.pallas_call(functools.partial(front_kernel, sizes), in_specs=[whole] *...  117 us
    pallas_call x1, Pallas kernels, feed_back(): pl.pallas_call(feed_back_kernel, grid=(FF // FEED_WIDTH,), in_specs=[fixe...  37.9 us
    pallas_call x1, Pallas kernels, feed(): pl.pallas_call(feed_kernel, grid=(FF // FEED_WIDTH,), in_specs=[fixed(D,...  33.5 us
    unnamed x38, local copies, waits for them, and re-layouts  12.4 us

profile of v5, /device:TPU:0, one launch (start us, length us, event | category | flops | bytes accessed | tf_op | source)
XLA Modules:
  0.0 366.7 jit_solution(15288461166877663837)
XLA Ops:
  0.6 0.8 fusion.8
  1.4 0.6 broadcast_in_dim.56.refs_2_
  2.0 0.6 broadcast_in_dim.57.refs_3_
  2.6 0.7 slice.56
  3.3 0.6 broadcast_in_dim.54.refs_0_
  3.9 1.3 slice.57
  5.2 1.7 plan.1
  6.9 1.3 dynamic-slice_convert_fusion
  8.2 0.8 fusion.6
  9.1 0.6 broadcast_in_dim.58.gain_ref
  9.7 0.8 reverse
  10.5 0.7 pad_add_fusion
  11.2 0.8 slice.61
  11.9 0.1 reshape.169
  12.0 0.1 copy.44
  12.1 0.6 pad.4.table_ref
  12.7 116.6 %front.1 = (bf16[4,576,768]{2,1,0:T(8,128)(2,1)}, bf16[4,192,768]{2,1,0:T(8,128)(2,1)}, bf16[4,768,768]{2,1,0:T(8,128)(2,1)}, bf16[4,768,768]{2,1,0:T(8,128)(2,1...) custom-call(f32[576,768]{1,0:T(8,128)} %bitcast.66, ...), custom_call_target="tpu_custom_call" | custom-call | flops 32212254720 | bytes 67108864 | tf_op jit(solution)/shard_map/front/pallas_call | solution.py:621
  129.5 0.1 broadcast_multiply_fusion
  129.6 0.1 mul.219.right_ref
  129.7 0.1 mul.227.tall_ref
  129.8 0.1 reshape.171
  129.9 0.1 copy.45
  130.1 0.1 reshape.173
  130.1 0.1 broadcast_multiply_fusion.2
  130.2 0.1 mul.223
  130.3 0.1 copy.47.wide_ref
  130.4 0.1 reshape.172
  130.5 0.1 broadcast_multiply_fusion.3
  130.6 0.1 mul.214
  130.7 0.1 copy.46.left_ref
  130.8 1.3 copy-done
  132.0 1.4 copy-done.3
  133.4 33.5 %feed.1 = (bf16[1024,3072]{1,0:T(8,128)(2,1)}, bf16[1024,3072]{1,0:T(8,128)(2,1)}, bf16[1024,768]{1,0:T(8,128)(2,1)S(1)}, f32[1024,768]{1,0:T(8,128)}, bf16[1024...) custom-call(bf16[768,1024]{1,0:T(8,128)(2,1)S(1)} %copy-done.3, ...), custom_call_target="tpu_custom_call" | custom-call | flops 14495514624 | bytes 33554432 | tf_op jit(solution)/shard_map/feed/pallas_call | solution.py:1517
  167.0 1.1 copy-done.4
  168.1 1.1 copy-done.5
  169.3 0.1 reshape.182
  169.4 0.1 reshape.186
  169.5 0.1 multiply_reduce_fusion
  169.6 0.1 reshape.183
  169.8 0.1 reshape.180
  169.9 0.1 multiply_reduce_fusion.3
  170.1 0.1 copy.50
  170.2 0.1 reshape.179
  170.3 0.1 multiply_reduce_fusion.2
  170.5 0.1 copy.51
  170.6 0.1 reshape.181
  170.7 37.9 %feed_back.1 = (bf16[3072,768]{1,0:T(8,128)(2,1)}, bf16[3072,768]{1,0:T(8,128)(2,1)}, bf16[1024,768]{1,0:T(8,128)(2,1)S(1)}, f32[1,768]{1,0:T(1,128)S(1)}, bf16[...) custom-call(bf16[1024,768]{1,0:T(8,128)(2,1)} %copy-done.5, bf16[1024,768]{1,0:T(8,128)(2,1)} %copy-done.4, ...), custom_call_target="tpu_custom_call" | custom-call | flops 24159191040 | bytes 33554432 | tf_op jit(solution)/shard_map/feed_back/pallas_call | solution.py:1639
  208.6 1.0 copy-done.2
  209.6 1.1 copy-done.6
  210.7 1.1 copy-done.7
  211.9 0.1 reshape.185
  212.0 0.1 reshape.184
  212.1 0.7 concatenate.10
  212.8 140.0 %back.1 = (f32[576,768]{1,0:T(8,128)}, bf16[1024,768]{1,0:T(8,128)(2,1)}, f32[48,128]{1,0:T(8,128)}) custom-call(bf16[4,192,768]{2,1,0:T(8,128)(2,1)} %bitcast.64, bf16[4,768,768]{2,1,0:T(8,128)(2,1)} %bitcast.89, bf16[4,768,768]{2,1,0:T(8,128)(2,1)} %bitcast.90, bf16[4,576,1024]{2,1,0:T(8,128)(2,1)} %get-tuple-element.69.projected_ref, ...), custom_call_target="tpu_custom_call" | custom-call | flops 51539607552 | bytes 67108864 | tf_op jit(solution)/shard_map/back/pallas_call | solution.py:1321
  352.8 0.7 slice_bitcast_fusion.1
  353.5 0.1 copy.52
  353.5 0.1 reshape.190
  353.7 0.7 slice_bitcast_fusion
  355.1 0.7 multiply_subtract_fusion
  355.8 0.6 fusion.2
  356.4 6.8 %convert_bitcast_fusion = (bf16[1,576,768]{2,1,0:T(8,128)(2,1)}, f32[576,768]{1,0:T(8,128)}, f32[1,576,768]{2,1,0:T(8,128)}, f32[1,576,768]{2,1,0:T(8,128)}) fusion(f32[576]{0:T(1024)S(1)} %fusion.3, f32[576,768]{1,0:T(8,128)} %get-tuple-element.86, f32[1,576,768]{2,1,0:T(8,128)} %param.20, f32[]{:T(128)} %bitcast.26, f32[1,576,768]{2,1,0:T(8,128)} %param.19, ...), kind=kLoop, calls=%fused_computation.6 | loop fusion | flops 7962624 | bytes 13273352 | tf_op jit(solution)/shard_map/broadcast_in_dim | solution.py:1806
  363.3 1.1 copy.56
  364.4 0.9 copy-done.8
  365.3 1.2 copy.57
  (41 shorter events, 0.6 us)
Async XLA Ops:
  12.7 117.0 %copy-start.11 = (f32[3616]{0:T(1024)S(1)}, f32[3616]{0:T(1024)}, u32[]{:S(2)}) copy-start(f32[3616]{0:T(1024)} %param.21) | copy-start | bytes 43396
  130.8 1.3 copy-start
  132.0 1.4 copy-start.3
  133.4 37.3 %copy-start.1 = (bf16[4,192,768]{2,1,0:T(8,128)(2,1)S(1)}, bf16[4,192,768]{2,1,0:T(8,128)(2,1)}, u32[]{:S(2)}) copy-start(bf16[4,192,768]{2,1,0:T(8,128)(2,1)} %get-tuple-element.57) | copy-start | bytes 3538948
  167.0 1.1 copy-start.4
  168.1 1.1 copy-start.5
  208.6 1.0 copy-start.2
  209.6 1.1 copy-start.6
  210.7 1.1 copy-start.7
  212.7 142.3 %copy-start.13 = (f32[3616]{0:T(1024)S(1)}, f32[3616]{0:T(1024)}, u32[]{:S(2)}) copy-start(f32[3616]{0:T(1024)} %param.23) | copy-start | bytes 43396
  212.7 142.3 %copy-start.14 = (f32[3616]{0:T(1024)S(1)}, f32[3616]{0:T(1024)}, u32[]{:S(2)}) copy-start(f32[3616]{0:T(1024)} %param.22) | copy-start | bytes 43396
  212.7 143.0 %copy-start.15 = (f32[1696]{0:T(1024)S(1)}, f32[1696]{0:T(1024)}, u32[]{:S(2)}) copy-start(f32[1696]{0:T(1024)} %param.24) | copy-start | bytes 20356
  212.7 143.7 %copy-start.16 = (s32[1,576]{1,0:T(1,128)S(1)}, s32[1,576]{1,0:T(1,128)}, u32[]{:S(2)}) copy-start(s32[1,576]{1,0:T(1,128)} %get-tuple-element.50.slot_place_ref) | copy-start | bytes 6916
  212.8 143.7 %copy-start.9 = (f32[1,576,768]{2,1,0:T(8,128)S(1)}, f32[1,576,768]{2,1,0:T(8,128)}, u32[]{:S(2)}) copy-start(f32[1,576,768]{2,1,0:T(8,128)} %param.18) | copy-start | bytes 5308420
  355.8 7.5 %copy-start.12 = (f32[3616]{0:T(1024)}, f32[3616]{0:T(1024)S(1)}, u32[]{:S(2)}) copy-start(f32[3616]{0:T(1024)S(1)} %get-tuple-element.134) | copy-start | bytes 43396
  356.4 6.8 %copy-start.10 = (bf16[1024,768]{1,0:T(8,128)(2,1)S(1)}, bf16[1024,768]{1,0:T(8,128)(2,1)}, u32[]{:S(2)}) copy-start(bf16[1024,768]{1,0:T(8,128)(2,1)} %get-tuple-element.125) | copy-start | bytes 4718596
  363.3 2.0 copy-start.8
